TPU v7x, 32 devices: a whole 2x2x4 slice. The times are simulated.
32 devices in a mesh: group: 2 (over x), hid: 8 (over z, y), wid: 2 (over core).
Axes of the slice: x: 2, y: 2, z: 4, core: 2. Of those that a mesh axis runs over, the one named last changes fastest.
Arguments:
- activations: bfloat16 [256, 8192], P(('group', 'hid'), 'wid'), parts along dimension 0, may hold values from -6 to 6
- gate_quant: bfloat16 [8192, 32768], P('wid', 'hid'), may hold values from -0.0625 to 0.0625
- gate_scales: float32 [64, 256], P('wid', 'hid'), may hold values from 0.5 to 2
- up_quant: bfloat16 [8192, 32768], P('wid', 'hid'), may hold values from -0.0625 to 0.0625
- up_scales: float32 [64, 256], P('wid', 'hid'), may hold values from 0.5 to 2
- down_quant: bfloat16 [32768, 8192], P('hid', 'wid'), may hold values from -0.046875 to 0.046875
- down_scales: float32 [256, 64], P('hid', 'wid'), may hold values from 0.5 to 2
Outputs:
- ffn_out: bfloat16 [256, 8192], P(('group', 'hid'), 'wid'), parts along dimension 0
There are 2 independent parts, one for each index of `group`. A program takes and returns all parts, laid end to end along the dimension named above; an argument that names none is the same for every part. Nothing has to cross between parts.
All inputs are finite; a program needn't handle non-finite values.
Results may differ from a plain program's by a relative error of at most 0.0071.
Values may be sent and summed in bfloat16 or wider, within the bound.
No kernel may reach another device: no remote copies, remote signals or barrier semaphores. Data moves between devices by JAX's collectives and lax.ppermute only.
A program may use at most 320 MiB of HBM per device.

v0:
```python
import jax
import jax.numpy as jnp
from jax import lax
from jax.sharding import PartitionSpec as P

BLOCK = 128


def dequantize(quant, scales):
    rows, cols = quant.shape
    blocks = quant.astype(jnp.float32).reshape(rows // BLOCK, BLOCK, cols // BLOCK, BLOCK)
    scaled = blocks * scales[:, None, :, None]
    return scaled.reshape(rows, cols).astype(jnp.bfloat16)


def per_device(activations, gate_quant, gate_scales, up_quant, up_scales, down_quant, down_scales):
    gate_weight = dequantize(gate_quant, gate_scales)
    up_weight = dequantize(up_quant, up_scales)
    down_weight = dequantize(down_quant, down_scales)
    hidden_cols = gate_weight.shape[1]
    piece = lax.all_gather(activations, "hid", axis=0, tiled=True)
    gate_part = jnp.dot(piece, gate_weight, preferred_element_type=jnp.float32)
    up_part = jnp.dot(piece, up_weight, preferred_element_type=jnp.float32)
    partial_value = jnp.concatenate([gate_part, up_part], axis=1)
    summed = lax.psum(partial_value, "wid")
    hidden = (jax.nn.silu(summed[:, :hidden_cols]) * summed[:, hidden_cols:]).astype(jnp.bfloat16)
    total = lax.psum_scatter(
        jnp.dot(hidden, down_weight, preferred_element_type=jnp.float32),
        "hid",
        scatter_dimension=0,
        tiled=True,
    )
    return total.astype(jnp.bfloat16)


def solution(mesh):
    return jax.shard_map(
        per_device,
        mesh=mesh,
        in_specs=(
            P(("group", "hid"), "wid"),
            P("wid", "hid"),
            P("wid", "hid"),
            P("wid", "hid"),
            P("wid", "hid"),
            P("hid", "wid"),
            P("hid", "wid"),
        ),
        out_specs=P(("group", "hid"), "wid"),
        check_vma=False,
    )
```

profile of v0, /device:TPU:0, one launch (start us, length us, event | category | flops | bytes accessed | tf_op | source)
XLA Modules:
  0.0 419.8 jit_solution(12662106574035419747)
XLA Ops:
  6.5 0.0 all-gather.2.cloned.1.call-start
  6.5 0.7 all-gather.2.cloned.1.call-update
  7.3 0.0 all-reduce.2.cloned.1.call-start
  7.3 45.1 %all-gather.2.cloned.1.call-done = bf16[128,4096]{1,0:T(8,128)(2,1)} async-done(((bf16[16,4096]{1,0:T(8,128)(2,1)}), bf16[128,4096]{1,0:T(8,128)(2,1)}) %all-gather.2.cloned.1.call-update) | async-done | bytes 1048592 | tf_op jit(solution)/shard_map/all_gather | solution.py:21
  52.4 0.0 copy-start
  52.4 22.0 %mul.40 = f32[32,128,32,128]{3,2,1,0:T(8,128)} broadcast(f32[32,32]{1,0:T(8,128)} %param.9), dimensions={0,2} | broadcast | bytes 67112960 | tf_op jit(solution)/shard_map/mul | solution.py:12
  74.4 0.0 copy-done
  74.4 0.0 copy-start.2
  74.4 37.5 %fusion.12 = f32[128,4096]{0,1:T(8,128)S(1)} fusion(bf16[128,4096]{1,0:T(8,128)(2,1)S(1)} %copy-done, f32[512,8,32,128]{3,2,1,0:T(8,128)} %bitcast.3, bf16[4096,4096]{1,0:T(8,128)(2,1)} %param.8), kind=kOutput, calls=%fused_computation.10 | convolution fusion | flops 4345298944 | bytes 103809024 | tf_op jit(solution)/shard_map/dot_general | solution.py:22
  112.0 0.0 copy-done.2
  112.0 21.4 %mul.43 = f32[32,128,32,128]{3,2,1,0:T(8,128)} broadcast(f32[32,32]{1,0:T(8,128)S(1)} %copy-done.2), dimensions={0,2} | broadcast | bytes 67112960 | tf_op jit(solution)/shard_map/mul | solution.py:12
  133.4 0.0 copy-start.3
  133.4 91.5 %fusion.9 = f32[128,4096]{0,1:T(8,128)} fusion(bf16[128,4096]{1,0:T(8,128)(2,1)S(1)} %copy-done, f32[512,8,32,128]{3,2,1,0:T(8,128)} %bitcast.6, bf16[4096,4096]{1,0:T(8,128)(2,1)} %param.10), kind=kOutput, calls=%fused_computation.9 | convolution fusion | flops 4345298944 | bytes 103809024 | tf_op jit(solution)/shard_map/dot_general | solution.py:23
  224.9 3.8 pad_maximum_fusion
  228.7 0.0 all-reduce.2.cloned.1.call-update
  228.7 0.0 reduce-scatter.2.cloned.1.call-start
  228.8 27.3 %all-reduce.2.cloned.1.call-done = f32[128,8192]{0,1:T(8,128)} async-done(((f32[128,8192]{0,1:T(8,128)}), f32[128,8192]{0,1:T(8,128)}) %all-reduce.2.cloned.1.call-update) | async-done | bytes 4194320 | tf_op jit(solution)/shard_map/psum | solution.py:25
  256.1 0.0 copy-done.3
  256.1 0.0 copy-start.1
  256.1 21.8 %mul.48 = f32[32,128,32,128]{3,2,1,0:T(8,128)} broadcast(f32[32,32]{1,0:T(8,128)S(1)} %copy-done.3), dimensions={0,2} | broadcast | bytes 67112960 | tf_op jit(solution)/shard_map/mul | solution.py:12
  277.9 0.0 copy-done.1
  277.9 64.5 %fusion.7 = f32[128,4096]{1,0:T(8,128)} fusion(f32[512,8,32,128]{3,2,1,0:T(8,128)} %bitcast.9, bf16[4096,4096]{1,0:T(8,128)(2,1)} %param.12, f32[128,8192]{0,1:T(8,128)S(1)} %copy-done.1), kind=kOutput, calls=%fused_computation.8 | convolution fusion | flops 4348444672 | bytes 106954752 | tf_op jit(solution)/shard_map/dot_general | solution.py:28
  342.4 0.0 reduce-scatter.2.cloned.1.call-update
  342.4 69.1 %reduce-scatter.2.cloned.1.call-done = f32[16,4096]{1,0:T(8,128)} async-done(((f32[128,4096]{1,0:T(8,128)}), f32[16,4096]{1,0:T(8,128)}) %reduce-scatter.2.cloned.1.call-update) | async-done | bytes 262160 | tf_op jit(solution)/shard_map/reduce_scatter | solution.py:27
  411.5 1.6 convert_element_type.31
Async XLA Ops:
  6.5 45.8 %all-gather.2.cloned.1.call-start = ((), (), s32[]{:S(2)}) async-start(), calls=%async_computation.1 | async-start | bytes 1179648 | tf_op jit(solution)/shard_map/all_gather | solution.py:21
  7.3 248.8 %all-reduce.2.cloned.1.call-start = ((), (), s32[]{:S(2)}) async-start(), calls=%async_computation.2 | async-start | bytes 8388608 | tf_op jit(solution)/shard_map/psum | solution.py:25
  52.4 22.1 %copy-start = (bf16[128,4096]{1,0:T(8,128)(2,1)S(1)}, bf16[128,4096]{1,0:T(8,128)(2,1)}, u32[]{:S(2)}) copy-start(bf16[128,4096]{1,0:T(8,128)(2,1)} %all-gather.2.cloned.1.call-done) | copy-start | bytes 3145732
  74.4 37.6 %copy-start.2 = (f32[32,32]{1,0:T(8,128)S(1)}, f32[32,32]{1,0:T(8,128)}, u32[]{:S(2)}) copy-start(f32[32,32]{1,0:T(8,128)} %param.11) | copy-start | bytes 12292
  133.4 122.7 %copy-start.3 = (f32[32,32]{1,0:T(8,128)S(1)}, f32[32,32]{1,0:T(8,128)}, u32[]{:S(2)}) copy-start(f32[32,32]{1,0:T(8,128)} %param.13) | copy-start | bytes 12292
  228.7 182.8 %reduce-scatter.2.cloned.1.call-start = ((), (), s32[]{:S(2)}) async-start(), calls=%async_computation.3 | async-start | bytes 2359296 | tf_op jit(solution)/shard_map/reduce_scatter | solution.py:27
  256.1 21.8 %copy-start.1 = (f32[128,8192]{0,1:T(8,128)S(1)}, f32[128,8192]{0,1:T(8,128)}, u32[]{:S(2)}) copy-start(f32[128,8192]{0,1:T(8,128)} %all-reduce.2.cloned.1.call-done) | copy-start | bytes 12582916
Sparse Core Ops, SparseCore 0:
  9.5 42.8 all-gather.1
  228.9 27.1 all-reduce.1
  342.5 68.9 reduce-scatter.1
where the time goes:
time: 427 us; the launch traced here: 420 us
  matrix products  194 us (45%)
  waiting for transfers between devices  142 us (33%)
  local copies, waits for them, and re-layouts  65.2 us (15%)
  between operations  13.3 us (3%)
  other arithmetic  5.42 us (1%)
    dot_general x1, matrix products, per_device(): up_part = jnp.dot(piece, up_weight, preferred_element_type=jnp.float32)  91.5 us
    reduce_scatter x1, waiting for transfers between devices, per_device(): lax.psum_scatter(jnp.dot(hidden, down_weight, preferred_element_type=jnp....  69.1 us
    mul x3, local copies, waits for them, and re-layouts, dequantize(): scaled = blocks * scales[:, None, :, None]  65.2 us
    dot_general x1, matrix products, per_device(): jnp.dot(hidden, down_weight, preferred_element_type=jnp.float32)  64.5 us
    all_gather x1, waiting for transfers between devices, per_device(): piece = lax.all_gather(activations, 'hid', axis=0, tiled=True)  45.1 us
    dot_general x1, matrix products, per_device(): gate_part = jnp.dot(piece, gate_weight, preferred_element_type=jnp.float32)  37.5 us
    psum x1, waiting for transfers between devices, per_device(): summed = lax.psum(partial_value, 'wid')  27.3 us
  transfers between devices with their start and end apart: 3, of which 3 were waited for; matrix products, arithmetic and copies ran while one was open for 0% of the time, Pallas kernels for 0%

commit v1 on v0

v1 whole, which is shorter than its diff:
```python
import functools

import jax
import jax.numpy as jnp
from jax import lax
from jax.experimental import pallas as pl
from jax.experimental.pallas import tpu as pltpu
from jax.sharding import PartitionSpec as P

BLOCK = 128
MIB = 1024 * 1024


def ring_order(n):
    if n % 2:
        return list(range(n))
    return list(range(0, n, 2)) + list(range(n - 1, 0, -2))


def scaled(quant_ref, scales_ref, k, col, width):
    pieces = []
    for j in range(width // BLOCK):
        block = quant_ref[k * BLOCK:(k + 1) * BLOCK, j * BLOCK:(j + 1) * BLOCK].astype(jnp.float32)
        pieces.append((block * scales_ref[k, col + j]).astype(jnp.bfloat16))
    return jnp.concatenate(pieces, axis=1) if len(pieces) > 1 else pieces[0]


def tile_dot(x_ref, quant_ref, scales_ref, col, width):
    blocks = quant_ref.shape[0] // BLOCK
    per = 2 if blocks % 2 == 0 else 1
    total = None
    for k in range(0, blocks, per):
        weight = [scaled(quant_ref, scales_ref, k + i, col, width) for i in range(per)]
        weight = jnp.concatenate(weight, axis=0) if per > 1 else weight[0]
        part = jnp.dot(x_ref[:, k * BLOCK:(k + per) * BLOCK], weight, preferred_element_type=jnp.float32)
        total = part if total is None else total + part
    return total


def gate_up_kernel(first, tile, pieces, *refs):
    xs = refs[:pieces]
    gs, us, gq, uq, g_out, u_out, send, x = refs[pieces:]
    rows = xs[0].shape[0]

    @pl.when(pl.program_id(0) == 0)
    def _():
        for i in range(pieces):
            x[i * rows:(i + 1) * rows, :] = xs[i][...]

    col = (first + pl.program_id(0)) * (tile // BLOCK)
    g = tile_dot(x, gq, gs, col, tile)
    g_out[...] = g
    send[0] = g.astype(jnp.bfloat16)
    u = tile_dot(x, uq, us, col, tile)
    u_out[...] = u
    send[1] = u.astype(jnp.bfloat16)


def gate_up(xs, gate_scales, up_scales, gate_quant, up_quant, start, chunk, tile):
    depth = gate_quant.shape[0]
    rows = xs[0].shape[0] * len(xs)
    first = start // tile
    weight_spec = pl.BlockSpec((depth, tile), lambda i: (0, first + i))
    vmem = pl.BlockSpec(memory_space=pltpu.VMEM)
    smem = pl.BlockSpec(memory_space=pltpu.SMEM)
    return pl.pallas_call(
        functools.partial(gate_up_kernel, first, tile, len(xs)),
        grid=(chunk // tile,),
        in_specs=[vmem] * len(xs) + [smem, smem, weight_spec, weight_spec],
        out_specs=[
            pl.BlockSpec((rows, tile), lambda i: (0, i)),
            pl.BlockSpec((rows, tile), lambda i: (0, i)),
            pl.BlockSpec((2, rows, tile), lambda i: (0, 0, i)),
        ],
        out_shape=[
            jax.ShapeDtypeStruct((rows, chunk), jnp.float32),
            jax.ShapeDtypeStruct((rows, chunk), jnp.float32),
            jax.ShapeDtypeStruct((2, rows, chunk), jnp.bfloat16),
        ],
        scratch_shapes=[pltpu.VMEM((rows, depth), jnp.bfloat16)],
        compiler_params=pltpu.CompilerParams(vmem_limit_bytes=48 * MIB),
        cost_estimate=pl.CostEstimate(
            flops=4 * rows * depth * chunk, bytes_accessed=4 * depth * chunk, transcendentals=0
        ),
        name="gate_up",
    )(*xs, gate_scales, up_scales, gate_quant, up_quant)


def down_kernel(first, tile, chunks, *refs):
    parts = refs[:3 * chunks]
    ds, dq, out, hidden = refs[3 * chunks:]

    @pl.when(pl.program_id(0) == 0)
    def _():
        at = 0
        for c in range(chunks):
            g_ref, u_ref, other = parts[3 * c:3 * c + 3]
            width = g_ref.shape[1]
            step = min(width, 512)
            for j in range(0, width, step):
                g = g_ref[:, j:j + step] + other[0, :, j:j + step].astype(jnp.float32)
                u = u_ref[:, j:j + step] + other[1, :, j:j + step].astype(jnp.float32)
                value = (g / (1.0 + jnp.exp(-g))) * u
                hidden[:, at + j:at + j + step] = value.astype(jnp.bfloat16)
            at += width

    col = (first + pl.program_id(0)) * (tile // BLOCK)
    out[...] = tile_dot(hidden, dq, ds, col, tile)


def down(parts, down_scales, down_quant, start, chunk, tile):
    depth = down_quant.shape[0]
    rows = parts[0].shape[0]
    first = start // tile
    vmem = pl.BlockSpec(memory_space=pltpu.VMEM)
    return pl.pallas_call(
        functools.partial(down_kernel, first, tile, len(parts) // 3),
        grid=(chunk // tile,),
        in_specs=[vmem] * len(parts)
        + [pl.BlockSpec(memory_space=pltpu.SMEM), pl.BlockSpec((depth, tile), lambda i: (0, first + i))],
        out_specs=pl.BlockSpec((rows, tile), lambda i: (0, i)),
        out_shape=jax.ShapeDtypeStruct((rows, chunk), jnp.float32),
        scratch_shapes=[pltpu.VMEM((rows, depth), jnp.bfloat16)],
        compiler_params=pltpu.CompilerParams(vmem_limit_bytes=48 * MIB),
        cost_estimate=pl.CostEstimate(
            flops=2 * rows * depth * chunk, bytes_accessed=2 * depth * chunk, transcendentals=0
        ),
        name="down",
    )(*parts, down_scales, down_quant)


def per_device(n, widths, activations, gate_quant, gate_scales, up_quant, up_scales, down_quant, down_scales):
    order = ring_order(n)
    forward = [(order[i], order[(i + 1) % n]) for i in range(n)]
    backward = [(b, a) for a, b in forward]
    ahead, behind = n // 2, n - 1 - n // 2

    blocks = [activations] + [None] * (n - 1)
    fw = bw = activations
    for step in range(1, ahead + 1):
        fw = lax.ppermute(fw, "hid", forward)
        blocks[n - step] = fw
        if step <= behind:
            bw = lax.ppermute(bw, "hid", backward)
            blocks[step] = bw

    hidden_units = gate_quant.shape[1]
    chunk = min(hidden_units, 1024)
    parts = []
    for start in range(0, hidden_units, chunk):
        g, u, send = gate_up(
            blocks, gate_scales, up_scales, gate_quant, up_quant, start, chunk, min(chunk, 256)
        )
        other = lax.ppermute(send, "wid", [(i, widths - 1 - i) for i in range(widths)])
        parts += [g, u, other]

    total = down(parts, down_scales, down_quant, 0, down_quant.shape[1], 256)

    rows = activations.shape[0]

    def mine(r):
        r = r % n
        return total[r * rows:(r + 1) * rows]

    fw, bw = mine(ahead), mine(-behind)
    for step in range(1, ahead + 1):
        got_fw = lax.ppermute(fw.astype(jnp.bfloat16), "hid", forward)
        fw = got_fw.astype(jnp.float32) + mine(ahead - step)
        if step <= behind:
            got_bw = lax.ppermute(bw.astype(jnp.bfloat16), "hid", backward)
            bw = got_bw.astype(jnp.float32)
            if step < behind:
                bw = bw + mine(step - behind)
    return ((fw + bw) if behind else fw).astype(jnp.bfloat16)


def solution(mesh):
    return jax.shard_map(
        functools.partial(per_device, mesh.shape["hid"], mesh.shape["wid"]),
        mesh=mesh,
        in_specs=(
            P(("group", "hid"), "wid"),
            P("wid", "hid"),
            P("wid", "hid"),
            P("wid", "hid"),
            P("wid", "hid"),
            P("hid", "wid"),
            P("hid", "wid"),
        ),
        out_specs=P(("group", "hid"), "wid"),
        check_vma=False,
    )
```

time: 427 us -> 108 us (0.25); the launches traced: 420 us -> 108 us
  matrix products: 194 us -> 0 us
  waiting for transfers between devices: 142 us -> 30.8 us
  local copies, waits for them, and re-layouts: 65.2 us -> 2.37 us
  Pallas kernels: 0 us -> 53 us
  starting transfers between devices: 0.08 us -> 18.5 us
  between operations: 13.3 us -> 0.11 us
    dot_general x3 -> x0, matrix products: 194 us -> none  [the longest x1 91.5 us: per_device(): up_part = jnp.dot(piece, up_weight, preferred_element_type=jnp.float32)]
    reduce_scatter x1 -> x0, waiting for transfers between devices: 69.1 us -> none  [per_device(): lax.psum_scatter(jnp.dot(hidden, down_weight, preferred_element_type=jnp....]
    mul x3 -> x0, local copies, waits for them, and re-layouts: 65.2 us -> none  [dequantize(): scaled = blocks * scales[:, None, :, None]]
    pallas_call x0 -> x5, Pallas kernels: none -> 53 us  [the longest x4 32 us: gate_up(): pl.pallas_call(functools.partial(gate_up_kernel, first, tile, len(xs)), g...]
    all_gather x1 -> x0, waiting for transfers between devices: 45.1 us -> none  [per_device(): piece = lax.all_gather(activations, 'hid', axis=0, tiled=True)]
    ppermute x0 -> x18, waiting for transfers between devices: none -> 30.8 us  [the longest x4 13.3 us: per_device(): got_fw = lax.ppermute(fw.astype(jnp.bfloat16), 'hid', forward)]
    psum x1 -> x0, waiting for transfers between devices: 27.3 us -> none  [per_device(): summed = lax.psum(partial_value, 'wid')]
    ppermute x0 -> x18, starting transfers between devices: none -> 18.5 us  [the longest x4 8.71 us: per_device(): fw = lax.ppermute(fw, 'hid', forward)]
  transfers between devices with their start and end apart: 3 -> 18, of which waited for: 3 -> 11; matrix products, arithmetic and copies ran while one was open for 0% -> 0% of each run, Pallas kernels for 0% -> 22%
where the time goes in v1:
time: 108 us
  Pallas kernels  53 us (49%)
  waiting for transfers between devices  30.8 us (29%)
  starting transfers between devices  18.5 us (17%)
  other arithmetic  2.74 us (3%)
  local copies, waits for them, and re-layouts  2.37 us (2%)
    pallas_call x4, Pallas kernels, gate_up(): pl.pallas_call(functools.partial(gate_up_kernel, first, tile, len(xs)), g...  32 us
    pallas_call x1, Pallas kernels, down(): pl.pallas_call(functools.partial(down_kernel, first, tile, len(parts) //...  21 us
    ppermute x4, waiting for transfers between devices, per_device(): got_fw = lax.ppermute(fw.astype(jnp.bfloat16), 'hid', forward)  13.3 us
    ppermute x4, waiting for transfers between devices, per_device(): fw = lax.ppermute(fw, 'hid', forward)  12.9 us
    ppermute x4, starting transfers between devices, per_device(): fw = lax.ppermute(fw, 'hid', forward)  8.71 us
    ppermute x4, starting transfers between devices, per_device(): got_fw = lax.ppermute(fw.astype(jnp.bfloat16), 'hid', forward)  7.04 us
    ppermute x3, waiting for transfers between devices, per_device(): got_bw = lax.ppermute(bw.astype(jnp.bfloat16), 'hid', backward)  3.07 us
    unnamed x12, local copies, waits for them, and re-layouts  2.35 us
  transfers between devices with their start and end apart: 18, of which 11 were waited for; matrix products, arithmetic and copies ran while one was open for 0% of the time, Pallas kernels for 22%

profile of v1, /device:TPU:0, one launch (start us, length us, event | category | flops | bytes accessed | tf_op | source)
XLA Modules:
  0.0 107.6 jit_solution(7701674846940353762)
XLA Ops:
  0.0 3.0 %collective-permute-start.3 = (bf16[16,4096]{1,0:T(8,128)(2,1)}, bf16[16,4096]{1,0:T(8,128)(2,1)S(1)}, u32[]{:S(2)}, u32[]{:S(2)}) collective-permute-start(bf16[16,4096]{1,0:T(8,128)(2,1)} %refs_0_.7), channel_id=1, source_target_pairs={{0,4},{4,8},{8,12},{12,14},{14,10},{10,6},{6,2},{2,0},{1,5},{5,9},... | collective-permute-start | bytes 393224 | tf_op jit(solution)/shard_map/ppermute | solution.py:141
  3.0 0.0 collective-permute-start
  3.0 3.6 %collective-permute-done.3.refs_7_ = bf16[16,4096]{1,0:T(8,128)(2,1)S(1)} collective-permute-done((bf16[16,4096]{1,0:T(8,128)(2,1)}, bf16[16,4096]{1,0:T(8,128)(2,1)S(1)}, u32[]{:S(2)}, u32[]{:S(2)}) %collective-permute-start.3) | collective-permute-done | bytes 131104 | tf_op jit(solution)/shard_map/ppermute | solution.py:141
  6.7 1.8 %collective-permute-start.4 = (bf16[16,4096]{1,0:T(8,128)(2,1)S(1)}, bf16[16,4096]{1,0:T(8,128)(2,1)S(1)}, u32[]{:S(2)}, u32[]{:S(2)}) collective-permute-start(bf16[16,4096]{1,0:T(8,128)(2,1)S(1)} %collective-permute-done.3.refs_7_), channel_id=1, source_target_pairs={{0,4},{4,8},{8,12},{12,14},{14,10},{10,6},{6,2},{2,0},{1,5},{5,9},... | collective-permute-start | bytes 393224 | tf_op jit(solution)/shard_map/ppermute | solution.py:141
  8.5 0.0 collective-permute-done.refs_1_
  8.5 0.2 collective-permute-start.1
  8.7 2.9 %collective-permute-done.4.refs_6_ = bf16[16,4096]{1,0:T(8,128)(2,1)S(1)} collective-permute-done((bf16[16,4096]{1,0:T(8,128)(2,1)S(1)}, bf16[16,4096]{1,0:T(8,128)(2,1)S(1)}, u32[]{:S(2)}, u32[]{:S(2)}) %collective-permute-start.4) | collective-permute-done | bytes 131104 | tf_op jit(solution)/shard_map/ppermute | solution.py:141
  11.6 1.8 %collective-permute-start.5 = (bf16[16,4096]{1,0:T(8,128)(2,1)S(1)}, bf16[16,4096]{1,0:T(8,128)(2,1)S(1)}, u32[]{:S(2)}, u32[]{:S(2)}) collective-permute-start(bf16[16,4096]{1,0:T(8,128)(2,1)S(1)} %collective-permute-done.4.refs_6_), channel_id=1, source_target_pairs={{0,4},{4,8},{8,12},{12,14},{14,10},{10,6},{6,2},{2,0},{1,5},{5,9},... | collective-permute-start | bytes 393224 | tf_op jit(solution)/shard_map/ppermute | solution.py:141
  13.4 0.0 collective-permute-done.1.refs_2_
  13.4 0.2 collective-permute-start.2
  13.7 3.4 %collective-permute-done.5.refs_5_ = bf16[16,4096]{1,0:T(8,128)(2,1)S(1)} collective-permute-done((bf16[16,4096]{1,0:T(8,128)(2,1)S(1)}, bf16[16,4096]{1,0:T(8,128)(2,1)S(1)}, u32[]{:S(2)}, u32[]{:S(2)}) %collective-permute-start.5) | collective-permute-done | bytes 131104 | tf_op jit(solution)/shard_map/ppermute | solution.py:141
  17.0 2.1 %collective-permute-start.6 = (bf16[16,4096]{1,0:T(8,128)(2,1)S(1)}, bf16[16,4096]{1,0:T(8,128)(2,1)S(1)}, u32[]{:S(2)}, u32[]{:S(2)}) collective-permute-start(bf16[16,4096]{1,0:T(8,128)(2,1)S(1)} %collective-permute-done.5.refs_5_), channel_id=1, source_target_pairs={{0,4},{4,8},{8,12},{12,14},{14,10},{10,6},{6,2},{2,0},{1,5},{5,9},... | collective-permute-start | bytes 393224 | tf_op jit(solution)/shard_map/ppermute | solution.py:141
  19.1 0.0 collective-permute-done.2.refs_3_
  19.1 3.0 %collective-permute-done.6.refs_4_ = bf16[16,4096]{1,0:T(8,128)(2,1)S(1)} collective-permute-done((bf16[16,4096]{1,0:T(8,128)(2,1)S(1)}, bf16[16,4096]{1,0:T(8,128)(2,1)S(1)}, u32[]{:S(2)}, u32[]{:S(2)}) %collective-permute-start.6) | collective-permute-done | bytes 131104 | tf_op jit(solution)/shard_map/ppermute | solution.py:141
  22.1 0.9 copy-done
  23.0 0.7 copy-done.1
  23.7 0.7 copy-done.2
  24.4 8.0 %gate_up.7 = (f32[128,1024]{1,0:T(8,128)S(1)}, f32[128,1024]{1,0:T(8,128)S(1)}, bf16[2,128,1024]{2,1,0:T(8,128)(2,1)S(1)}) custom-call(bf16[16,4096]{1,0:T(8,128)(2,1)S(1)} %copy-done, bf16[16,4096]{1,0:T(8,128)(2,1)S(1)} %collective-permute-done.refs_1_, bf16[16,4096]{1,0:T(8,128)(2,1)S(1)} %collective-permute-done.1.refs_2_, ...), custom_call_target="tpu_custom_call" | custom-call | flops 2147483648 | bytes 16777216 | tf_op jit(solution)/shard_map/gate_up/pallas_call | solution.py:66
  32.4 0.1 collective-permute-start.10
  32.5 8.0 %gate_up.6 = (f32[128,1024]{1,0:T(8,128)S(1)}, f32[128,1024]{1,0:T(8,128)S(1)}, bf16[2,128,1024]{2,1,0:T(8,128)(2,1)S(1)}) custom-call(bf16[16,4096]{1,0:T(8,128)(2,1)S(1)} %copy-done, bf16[16,4096]{1,0:T(8,128)(2,1)S(1)} %collective-permute-done.refs_1_, bf16[16,4096]{1,0:T(8,128)(2,1)S(1)} %collective-permute-done.1.refs_2_, ...), custom_call_target="tpu_custom_call" | custom-call | flops 2147483648 | bytes 16777216 | tf_op jit(solution)/shard_map/gate_up/pallas_call | solution.py:66
  40.6 0.5 collective-permute-start.9
  41.1 8.0 %gate_up.5 = (f32[128,1024]{1,0:T(8,128)S(1)}, f32[128,1024]{1,0:T(8,128)S(1)}, bf16[2,128,1024]{2,1,0:T(8,128)(2,1)S(1)}) custom-call(bf16[16,4096]{1,0:T(8,128)(2,1)S(1)} %copy-done, bf16[16,4096]{1,0:T(8,128)(2,1)S(1)} %collective-permute-done.refs_1_, bf16[16,4096]{1,0:T(8,128)(2,1)S(1)} %collective-permute-done.1.refs_2_, ...), custom_call_target="tpu_custom_call" | custom-call | flops 2147483648 | bytes 16777216 | tf_op jit(solution)/shard_map/gate_up/pallas_call | solution.py:66
  49.1 0.0 copy-start.3
  49.1 0.1 collective-permute-start.8
  49.2 8.0 %gate_up.4 = (f32[128,1024]{1,0:T(8,128)S(1)}, f32[128,1024]{1,0:T(8,128)S(1)}, bf16[2,128,1024]{2,1,0:T(8,128)(2,1)S(1)}) custom-call(bf16[16,4096]{1,0:T(8,128)(2,1)S(1)} %copy-done, bf16[16,4096]{1,0:T(8,128)(2,1)S(1)} %collective-permute-done.refs_1_, bf16[16,4096]{1,0:T(8,128)(2,1)S(1)} %collective-permute-done.1.refs_2_, ...), custom_call_target="tpu_custom_call" | custom-call | flops 2147483648 | bytes 16777216 | tf_op jit(solution)/shard_map/gate_up/pallas_call | solution.py:66
  57.2 0.5 collective-permute-start.7
  57.8 0.0 collective-permute-done.10.refs_11_
  57.8 0.0 collective-permute-done.9.refs_8_
  57.8 0.0 collective-permute-done.8.refs_5_
  57.8 1.5 %collective-permute-done.7.refs_2_ = bf16[2,128,1024]{2,1,0:T(8,128)(2,1)S(1)} collective-permute-done((bf16[2,128,1024]{2,1,0:T(8,128)(2,1)S(1)}, bf16[2,128,1024]{2,1,0:T(8,128)(2,1)S(1)}, u32[]{:S(2)}, u32[]{:S(2)}) %collective-permute-start.7) | collective-permute-done | bytes 524320 | tf_op jit(solution)/shard_map/ppermute | solution.py:154
  59.3 21.0 %down.1 = f32[128,4096]{1,0:T(8,128)} custom-call(f32[128,1024]{1,0:T(8,128)S(1)} %get-tuple-element.17.refs_0_, f32[128,1024]{1,0:T(8,128)S(1)} %get-tuple-element.18.refs_1_, bf16[2,128,1024]{2,1,0:T(8,128)(2,1)S(1)} %collective-permute-done.7.refs_2_, f32[128,1024]{1,0:T(8,128)S(1)} %get-tuple-element.20.refs_3_, ...), custom_call_target="tpu_custom_call" | custom-call | flops 4294967296 | bytes 33554432 | tf_op jit(solution)/shard_map/down/pallas_call | solution.py:116
  80.3 1.9 %convert.4 = bf16[128,4096]{1,0:T(8,128)(2,1)S(1)} convert(f32[128,4096]{1,0:T(8,128)} %down.1) | non-fusion elementwise | flops 524288 | bytes 3145728 | tf_op jit(solution)/shard_map/convert.1
  82.2 2.1 %collective-permute-start.11 = (bf16[16,4096]{1,0:T(8,128)(2,1)S(1)}, bf16[16,4096]{1,0:T(8,128)(2,1)S(1)}, u32[]{:S(2)}, u32[]{:S(2)}) collective-permute-start(bf16[16,4096]{1,0:T(8,128)(2,1)S(1)} %get-tuple-element.33), channel_id=1, source_target_pairs={{0,4},{4,8},{8,12},{12,14},{14,10},{10,6},{6,2},{2,0},{1,5},{5,9},... | collective-permute-start | bytes 393224 | tf_op jit(solution)/shard_map/ppermute | solution.py:167
  84.3 0.1 collective-permute-start.15
  84.4 4.0 %collective-permute-done.11 = bf16[16,4096]{1,0:T(8,128)(2,1)S(1)} collective-permute-done((bf16[16,4096]{1,0:T(8,128)(2,1)S(1)}, bf16[16,4096]{1,0:T(8,128)(2,1)S(1)}, u32[]{:S(2)}, u32[]{:S(2)}) %collective-permute-start.11) | collective-permute-done | bytes 131104 | tf_op jit(solution)/shard_map/ppermute | solution.py:167
  88.4 1.8 %collective-permute-start.12 = (bf16[16,4096]{1,0:T(8,128)(2,1)S(1)}, bf16[16,4096]{1,0:T(8,128)(2,1)S(1)}, u32[]{:S(2)}, u32[]{:S(2)}) collective-permute-start(bf16[16,4096]{1,0:T(8,128)(2,1)S(1)} %fusion.6), channel_id=1, source_target_pairs={{0,4},{4,8},{8,12},{12,14},{14,10},{10,6},{6,2},{2,0},{1,5},{5,9},... | collective-permute-start | bytes 393224 | tf_op jit(solution)/shard_map/ppermute | solution.py:167
  90.2 3.5 %collective-permute-done.12 = bf16[16,4096]{1,0:T(8,128)(2,1)S(1)} collective-permute-done((bf16[16,4096]{1,0:T(8,128)(2,1)S(1)}, bf16[16,4096]{1,0:T(8,128)(2,1)S(1)}, u32[]{:S(2)}, u32[]{:S(2)}) %collective-permute-start.12) | collective-permute-done | bytes 131104 | tf_op jit(solution)/shard_map/ppermute | solution.py:167
  93.6 0.1 fusion.5
  93.7 1.6 %collective-permute-start.13 = (bf16[16,4096]{1,0:T(8,128)(2,1)S(1)}, bf16[16,4096]{1,0:T(8,128)(2,1)S(1)}, u32[]{:S(2)}, u32[]{:S(2)}) collective-permute-start(bf16[16,4096]{1,0:T(8,128)(2,1)S(1)} %get-tuple-element.31), channel_id=1, source_target_pairs={{0,4},{4,8},{8,12},{12,14},{14,10},{10,6},{6,2},{2,0},{1,5},{5,9},... | collective-permute-start | bytes 393224 | tf_op jit(solution)/shard_map/ppermute | solution.py:167
  95.2 0.5 collective-permute-start.16
  95.8 2.9 %collective-permute-done.13 = bf16[16,4096]{1,0:T(8,128)(2,1)S(1)} collective-permute-done((bf16[16,4096]{1,0:T(8,128)(2,1)S(1)}, bf16[16,4096]{1,0:T(8,128)(2,1)S(1)}, u32[]{:S(2)}, u32[]{:S(2)}) %collective-permute-start.13) | collective-permute-done | bytes 131104 | tf_op jit(solution)/shard_map/ppermute | solution.py:167
  98.7 1.5 %collective-permute-done.16 = bf16[16,4096]{1,0:T(8,128)(2,1)S(1)} collective-permute-done((bf16[16,4096]{1,0:T(8,128)(2,1)S(1)}, bf16[16,4096]{1,0:T(8,128)(2,1)S(1)}, u32[]{:S(2)}, u32[]{:S(2)}) %collective-permute-start.16) | collective-permute-done | bytes 131104 | tf_op jit(solution)/shard_map/ppermute | solution.py:170
  100.2 0.1 fusion.4
  100.3 1.6 %collective-permute-start.14 = (bf16[16,4096]{1,0:T(8,128)(2,1)S(1)}, bf16[16,4096]{1,0:T(8,128)(2,1)S(1)}, u32[]{:S(2)}, u32[]{:S(2)}) collective-permute-start(bf16[16,4096]{1,0:T(8,128)(2,1)S(1)} %get-tuple-element.29), channel_id=1, source_target_pairs={{0,4},{4,8},{8,12},{12,14},{14,10},{10,6},{6,2},{2,0},{1,5},{5,9},... | collective-permute-start | bytes 393224 | tf_op jit(solution)/shard_map/ppermute | solution.py:167
  101.9 0.5 collective-permute-start.17
  102.4 2.9 %collective-permute-done.14 = bf16[16,4096]{1,0:T(8,128)(2,1)S(1)} collective-permute-done((bf16[16,4096]{1,0:T(8,128)(2,1)S(1)}, bf16[16,4096]{1,0:T(8,128)(2,1)S(1)}, u32[]{:S(2)}, u32[]{:S(2)}) %collective-permute-start.14) | collective-permute-done | bytes 131104 | tf_op jit(solution)/shard_map/ppermute | solution.py:167
  105.3 1.6 %collective-permute-done.17 = bf16[16,4096]{1,0:T(8,128)(2,1)S(1)} collective-permute-done((bf16[16,4096]{1,0:T(8,128)(2,1)S(1)}, bf16[16,4096]{1,0:T(8,128)(2,1)S(1)}, u32[]{:S(2)}, u32[]{:S(2)}) %collective-permute-start.17) | collective-permute-done | bytes 131104 | tf_op jit(solution)/shard_map/ppermute | solution.py:170
  106.9 0.7 fusion.3
  (11 shorter events, 0.1 us)
Async XLA Ops:
  0.0 6.7 %collective-permute-start.3 = (bf16[16,4096]{1,0:T(8,128)(2,1)}, bf16[16,4096]{1,0:T(8,128)(2,1)S(1)}, u32[]{:S(2)}, u32[]{:S(2)}) collective-permute-start(bf16[16,4096]{1,0:T(8,128)(2,1)} %refs_0_.7), channel_id=1, source_target_pairs={{0,4},{4,8},{8,12},{12,14},{14,10},{10,6},{6,2},{2,0},{1,5},{5,9},... | collective-permute-start | bytes 393224 | tf_op jit(solution)/shard_map/ppermute | solution.py:141
  3.0 5.5 %collective-permute-start = (bf16[16,4096]{1,0:T(8,128)(2,1)}, bf16[16,4096]{1,0:T(8,128)(2,1)S(1)}, u32[]{:S(2)}, u32[]{:S(2)}) collective-permute-start(bf16[16,4096]{1,0:T(8,128)(2,1)} %refs_0_.7), channel_id=1, source_target_pairs={{4,0},{8,4},{12,8},{14,12},{10,14},{6,10},{2,6},{0,2},{5,1},{9,5},... | collective-permute-start | bytes 393224 | tf_op jit(solution)/shard_map/ppermute | solution.py:144
  6.7 5.0 %collective-permute-start.4 = (bf16[16,4096]{1,0:T(8,128)(2,1)S(1)}, bf16[16,4096]{1,0:T(8,128)(2,1)S(1)}, u32[]{:S(2)}, u32[]{:S(2)}) collective-permute-start(bf16[16,4096]{1,0:T(8,128)(2,1)S(1)} %collective-permute-done.3.refs_7_), channel_id=1, source_target_pairs={{0,4},{4,8},{8,12},{12,14},{14,10},{10,6},{6,2},{2,0},{1,5},{5,9},... | collective-permute-start | bytes 393224 | tf_op jit(solution)/shard_map/ppermute | solution.py:141
  8.5 5.0 %collective-permute-start.1 = (bf16[16,4096]{1,0:T(8,128)(2,1)S(1)}, bf16[16,4096]{1,0:T(8,128)(2,1)S(1)}, u32[]{:S(2)}, u32[]{:S(2)}) collective-permute-start(bf16[16,4096]{1,0:T(8,128)(2,1)S(1)} %collective-permute-done.refs_1_), channel_id=1, source_target_pairs={{4,0},{8,4},{12,8},{14,12},{10,14},{6,10},{2,6},{0,2},{5,1},{9,5},... | collective-permute-start | bytes 393224 | tf_op jit(solution)/shard_map/ppermute | solution.py:144
  11.6 5.4 %collective-permute-start.5 = (bf16[16,4096]{1,0:T(8,128)(2,1)S(1)}, bf16[16,4096]{1,0:T(8,128)(2,1)S(1)}, u32[]{:S(2)}, u32[]{:S(2)}) collective-permute-start(bf16[16,4096]{1,0:T(8,128)(2,1)S(1)} %collective-permute-done.4.refs_6_), channel_id=1, source_target_pairs={{0,4},{4,8},{8,12},{12,14},{14,10},{10,6},{6,2},{2,0},{1,5},{5,9},... | collective-permute-start | bytes 393224 | tf_op jit(solution)/shard_map/ppermute | solution.py:141
  13.4 5.7 %collective-permute-start.2 = (bf16[16,4096]{1,0:T(8,128)(2,1)S(1)}, bf16[16,4096]{1,0:T(8,128)(2,1)S(1)}, u32[]{:S(2)}, u32[]{:S(2)}) collective-permute-start(bf16[16,4096]{1,0:T(8,128)(2,1)S(1)} %collective-permute-done.1.refs_2_), channel_id=1, source_target_pairs={{4,0},{8,4},{12,8},{14,12},{10,14},{6,10},{2,6},{0,2},{5,1},{9,5},... | collective-permute-start | bytes 393224 | tf_op jit(solution)/shard_map/ppermute | solution.py:144
  17.0 5.1 %collective-permute-start.6 = (bf16[16,4096]{1,0:T(8,128)(2,1)S(1)}, bf16[16,4096]{1,0:T(8,128)(2,1)S(1)}, u32[]{:S(2)}, u32[]{:S(2)}) collective-permute-start(bf16[16,4096]{1,0:T(8,128)(2,1)S(1)} %collective-permute-done.5.refs_5_), channel_id=1, source_target_pairs={{0,4},{4,8},{8,12},{12,14},{14,10},{10,6},{6,2},{2,0},{1,5},{5,9},... | collective-permute-start | bytes 393224 | tf_op jit(solution)/shard_map/ppermute | solution.py:141
  22.1 0.9 copy-start
  23.0 0.7 copy-start.1
  23.7 0.7 copy-start.2
  32.4 25.3 %collective-permute-start.10 = (bf16[2,128,1024]{2,1,0:T(8,128)(2,1)S(1)}, bf16[2,128,1024]{2,1,0:T(8,128)(2,1)S(1)}, u32[]{:S(2)}, u32[]{:S(2)}) collective-permute-start(bf16[2,128,1024]{2,1,0:T(8,128)(2,1)S(1)} %get-tuple-element.28), channel_id=1, source_target_pairs={{0,1},{1,0},{2,3},{3,2},{4,5},{5,4},{6,7},{7,6},{8,9},{9,8},{10,11... | collective-permute-start | bytes 1572872 | tf_op jit(solution)/shard_map/ppermute | solution.py:154
  40.6 17.2 %collective-permute-start.9 = (bf16[2,128,1024]{2,1,0:T(8,128)(2,1)S(1)}, bf16[2,128,1024]{2,1,0:T(8,128)(2,1)S(1)}, u32[]{:S(2)}, u32[]{:S(2)}) collective-permute-start(bf16[2,128,1024]{2,1,0:T(8,128)(2,1)S(1)} %get-tuple-element.25), channel_id=1, source_target_pairs={{0,1},{1,0},{2,3},{3,2},{4,5},{5,4},{6,7},{7,6},{8,9},{9,8},{10,11... | collective-permute-start | bytes 1572872 | tf_op jit(solution)/shard_map/ppermute | solution.py:154
  49.1 10.2 %copy-start.3 = (f32[32,32]{1,0:T(8,128)S(1)}, f32[32,32]{1,0:T(8,128)}, u32[]{:S(2)}) copy-start(f32[32,32]{1,0:T(8,128)} %refs_12_.1) | copy-start | bytes 12292
  49.1 8.7 %collective-permute-start.8 = (bf16[2,128,1024]{2,1,0:T(8,128)(2,1)S(1)}, bf16[2,128,1024]{2,1,0:T(8,128)(2,1)S(1)}, u32[]{:S(2)}, u32[]{:S(2)}) collective-permute-start(bf16[2,128,1024]{2,1,0:T(8,128)(2,1)S(1)} %get-tuple-element.22), channel_id=1, source_target_pairs={{0,1},{1,0},{2,3},{3,2},{4,5},{5,4},{6,7},{7,6},{8,9},{9,8},{10,11... | collective-permute-start | bytes 1572872 | tf_op jit(solution)/shard_map/ppermute | solution.py:154
  57.2 2.1 %collective-permute-start.7 = (bf16[2,128,1024]{2,1,0:T(8,128)(2,1)S(1)}, bf16[2,128,1024]{2,1,0:T(8,128)(2,1)S(1)}, u32[]{:S(2)}, u32[]{:S(2)}) collective-permute-start(bf16[2,128,1024]{2,1,0:T(8,128)(2,1)S(1)} %get-tuple-element.19), channel_id=1, source_target_pairs={{0,1},{1,0},{2,3},{3,2},{4,5},{5,4},{6,7},{7,6},{8,9},{9,8},{10,11... | collective-permute-start | bytes 1572872 | tf_op jit(solution)/shard_map/ppermute | solution.py:154
  57.8 1.5 %copy-start.5 = (bf16[2,128,1024]{2,1,0:T(8,128)(2,1)}, bf16[2,128,1024]{2,1,0:T(8,128)(2,1)S(1)}, u32[]{:S(2)}) copy-start(bf16[2,128,1024]{2,1,0:T(8,128)(2,1)S(1)} %collective-permute-done.10.refs_11_) | copy-start | bytes 1572868
  80.3 8.0 %copy-start.4 = (f32[128,4096]{1,0:T(8,128)S(1)}, f32[128,4096]{1,0:T(8,128)}, u32[]{:S(2)}) copy-start(f32[128,4096]{1,0:T(8,128)} %down.1) | copy-start | bytes 6291460
  82.2 6.1 %collective-permute-start.11 = (bf16[16,4096]{1,0:T(8,128)(2,1)S(1)}, bf16[16,4096]{1,0:T(8,128)(2,1)S(1)}, u32[]{:S(2)}, u32[]{:S(2)}) collective-permute-start(bf16[16,4096]{1,0:T(8,128)(2,1)S(1)} %get-tuple-element.33), channel_id=1, source_target_pairs={{0,4},{4,8},{8,12},{12,14},{14,10},{10,6},{6,2},{2,0},{1,5},{5,9},... | collective-permute-start | bytes 393224 | tf_op jit(solution)/shard_map/ppermute | solution.py:167
  84.3 5.9 %collective-permute-start.15 = (bf16[16,4096]{1,0:T(8,128)(2,1)S(1)}, bf16[16,4096]{1,0:T(8,128)(2,1)S(1)}, u32[]{:S(2)}, u32[]{:S(2)}) collective-permute-start(bf16[16,4096]{1,0:T(8,128)(2,1)S(1)} %get-tuple-element.34), channel_id=1, source_target_pairs={{4,0},{8,4},{12,8},{14,12},{10,14},{6,10},{2,6},{0,2},{5,1},{9,5},... | collective-permute-start | bytes 393224 | tf_op jit(solution)/shard_map/ppermute | solution.py:170
  88.4 5.3 %collective-permute-start.12 = (bf16[16,4096]{1,0:T(8,128)(2,1)S(1)}, bf16[16,4096]{1,0:T(8,128)(2,1)S(1)}, u32[]{:S(2)}, u32[]{:S(2)}) collective-permute-start(bf16[16,4096]{1,0:T(8,128)(2,1)S(1)} %fusion.6), channel_id=1, source_target_pairs={{0,4},{4,8},{8,12},{12,14},{14,10},{10,6},{6,2},{2,0},{1,5},{5,9},... | collective-permute-start | bytes 393224 | tf_op jit(solution)/shard_map/ppermute | solution.py:167
  93.7 5.0 %collective-permute-start.13 = (bf16[16,4096]{1,0:T(8,128)(2,1)S(1)}, bf16[16,4096]{1,0:T(8,128)(2,1)S(1)}, u32[]{:S(2)}, u32[]{:S(2)}) collective-permute-start(bf16[16,4096]{1,0:T(8,128)(2,1)S(1)} %get-tuple-element.31), channel_id=1, source_target_pairs={{0,4},{4,8},{8,12},{12,14},{14,10},{10,6},{6,2},{2,0},{1,5},{5,9},... | collective-permute-start | bytes 393224 | tf_op jit(solution)/shard_map/ppermute | solution.py:167
  95.2 5.0 %collective-permute-start.16 = (bf16[16,4096]{1,0:T(8,128)(2,1)S(1)}, bf16[16,4096]{1,0:T(8,128)(2,1)S(1)}, u32[]{:S(2)}, u32[]{:S(2)}) collective-permute-start(bf16[16,4096]{1,0:T(8,128)(2,1)S(1)} %get-tuple-element.32), channel_id=1, source_target_pairs={{4,0},{8,4},{12,8},{14,12},{10,14},{6,10},{2,6},{0,2},{5,1},{9,5},... | collective-permute-start | bytes 393224 | tf_op jit(solution)/shard_map/ppermute | solution.py:170
  100.3 5.0 %collective-permute-start.14 = (bf16[16,4096]{1,0:T(8,128)(2,1)S(1)}, bf16[16,4096]{1,0:T(8,128)(2,1)S(1)}, u32[]{:S(2)}, u32[]{:S(2)}) collective-permute-start(bf16[16,4096]{1,0:T(8,128)(2,1)S(1)} %get-tuple-element.29), channel_id=1, source_target_pairs={{0,4},{4,8},{8,12},{12,14},{14,10},{10,6},{6,2},{2,0},{1,5},{5,9},... | collective-permute-start | bytes 393224 | tf_op jit(solution)/shard_map/ppermute | solution.py:167
  101.9 5.0 %collective-permute-start.17 = (bf16[16,4096]{1,0:T(8,128)(2,1)S(1)}, bf16[16,4096]{1,0:T(8,128)(2,1)S(1)}, u32[]{:S(2)}, u32[]{:S(2)}) collective-permute-start(bf16[16,4096]{1,0:T(8,128)(2,1)S(1)} %get-tuple-element.30), channel_id=1, source_target_pairs={{4,0},{8,4},{12,8},{14,12},{10,14},{6,10},{2,6},{0,2},{5,1},{9,5},... | collective-permute-start | bytes 393224 | tf_op jit(solution)/shard_map/ppermute | solution.py:170

commit v2 on v0

v2 whole, which is shorter than its diff:
```python
import functools

import jax
import jax.numpy as jnp
from jax import lax
from jax.experimental import pallas as pl
from jax.experimental.pallas import tpu as pltpu
from jax.sharding import PartitionSpec as P

BLOCK = 128
MIB = 1024 * 1024
VMEM_LIMIT = 16 * MIB
VMEM = pl.BlockSpec(memory_space=pltpu.VMEM)
SMEM = pl.BlockSpec(memory_space=pltpu.SMEM)
ANY = pl.BlockSpec(memory_space=pl.ANY)


def ring_order(n):
    if n % 2:
        return list(range(n))
    return list(range(0, n, 2)) + list(range(n - 1, 0, -2))


def scaled(quant, scales_ref, k, col, width):
    pieces = []
    for j in range(width // BLOCK):
        block = quant[k * BLOCK:(k + 1) * BLOCK, j * BLOCK:(j + 1) * BLOCK]
        pieces.append((block.astype(jnp.float32) * scales_ref[k, col + j]).astype(jnp.bfloat16))
    return jnp.concatenate(pieces, axis=1) if len(pieces) > 1 else pieces[0]


def tile_dot(x_ref, quant, scales_ref, col):
    depth, width = quant.shape
    blocks = depth // BLOCK
    per = 2 if blocks % 2 == 0 else 1
    total = None
    for k in range(0, blocks, per):
        weight = [scaled(quant, scales_ref, k + i, col, width) for i in range(per)]
        weight = jnp.concatenate(weight, axis=0) if per > 1 else weight[0]
        part = jnp.dot(x_ref[:, k * BLOCK:(k + per) * BLOCK], weight, preferred_element_type=jnp.float32)
        total = part if total is None else total + part
    return total


class Tiles:
    def __init__(self, quant, buffers, sems, first, count):
        self.quant, self.buffers, self.sems = quant, buffers, sems
        self.first, self.count = first, count
        self.slots, _, self.width = buffers.shape

    def copy(self, i):
        start = (self.first + i) * self.width
        if not isinstance(i, int):
            start = pl.multiple_of(start, self.width)
        slot = lax.rem(i, self.slots)
        return pltpu.make_async_copy(
            self.quant.at[:, pl.ds(start, self.width)], self.buffers.at[slot], self.sems.at[slot]
        )

    def begin(self):
        for i in range(min(self.count, self.slots)):
            self.copy(i).start()

    def get(self, i):
        self.copy(i).wait()
        return self.buffers.at[lax.rem(i, self.slots)]

    def advance(self, i):
        @pl.when(i + self.slots < self.count)
        def _():
            self.copy(i + self.slots).start()


def tile_copies(quant, first, staged, sems):
    count, _, width = staged.shape
    return [
        pltpu.make_async_copy(
            quant.at[:, (first + i) * width:(first + i + 1) * width], staged.at[i], sems.at[i]
        )
        for i in range(count)
    ]


def in_vmem(array):
    return pltpu.with_memory_space_constraint(array, pltpu.VMEM)


def stage_kernel(first, *refs):
    quant, staged, token, sems = refs
    copies = tile_copies(quant, first, staged, sems)
    for copy in copies:
        copy.start()
    token[...] = jnp.zeros_like(token)
    for copy in copies:
        copy.wait()


def stage(quant, first, count, tile):
    depth = quant.shape[0]
    return pl.pallas_call(
        functools.partial(stage_kernel, first),
        in_specs=[ANY],
        out_specs=[VMEM, VMEM],
        out_shape=[pltpu.VMEM((count, depth, tile), quant.dtype), pltpu.VMEM((16, BLOCK), jnp.bfloat16)],
        scratch_shapes=[pltpu.SemaphoreType.DMA((count,))],
        compiler_params=pltpu.CompilerParams(vmem_limit_bytes=VMEM_LIMIT),
        cost_estimate=pl.CostEstimate(
            flops=0, bytes_accessed=2 * count * depth * tile, transcendentals=0
        ),
        name="stage",
    )(quant)


def gate_up_kernel(first, tiles, places, keep_x, stage_next, *refs):
    refs = list(refs)
    xs = [refs.pop(0) for _ in places]
    gs, us, gq, uq, _ = [refs.pop(0) for _ in range(5)]
    dq = refs.pop(0) if stage_next else None
    own, send = refs.pop(0), refs.pop(0)
    x = refs.pop(0) if keep_x else xs[0]
    staged = refs.pop(0) if stage_next else None
    buffers, sems, staged_sems = refs
    tile = gq.shape[2]
    ups = Tiles(uq, buffers, sems, first, tiles)
    ups.begin()
    if keep_x:
        for ref, (row, col) in zip(xs, places):
            x[row:row + ref.shape[0], col:col + ref.shape[1]] = ref[...]
    copies = tile_copies(dq, 0, staged, staged_sems) if stage_next else []

    @pl.loop(0, tiles)
    def _(i):
        col = (first + i) * (tile // BLOCK)
        g = tile_dot(x, gq.at[first + i], gs, col)
        own[0, i] = g
        send[0, i] = g.astype(jnp.bfloat16)
        u = tile_dot(x, ups.get(i), us, col)
        own[1, i] = u
        send[1, i] = u.astype(jnp.bfloat16)
        ups.advance(i)

        @pl.when(i == max(tiles - ups.slots, 1) - 1)
        def _():
            for copy in copies:
                copy.start()

    for copy in copies:
        copy.wait()


def gate_up(xs, places, rows, gate_scales, up_scales, gate_tiles, up_quant, first, end, slots, down_quant, stage_next, token):
    _, depth, tile = gate_tiles.shape
    tiles = end - first
    keep_x = len(xs) > 1
    out_shape = [
        pltpu.VMEM((2, tiles, rows, tile), jnp.float32),
        jax.ShapeDtypeStruct((2, tiles, rows, tile), jnp.bfloat16),
    ]
    if keep_x:
        out_shape.append(pltpu.VMEM((rows, depth), jnp.bfloat16))
    if stage_next:
        out_shape.append(pltpu.VMEM((stage_next, down_quant.shape[0], tile), down_quant.dtype))
    return pl.pallas_call(
        functools.partial(gate_up_kernel, first, tiles, places[:len(xs)], keep_x, stage_next),
        in_specs=[VMEM] * len(xs) + [SMEM, SMEM, VMEM, ANY, ANY] + [ANY] * (stage_next > 0),
        out_specs=[VMEM] * len(out_shape),
        out_shape=out_shape,
        scratch_shapes=[
            pltpu.VMEM((slots, depth, tile), jnp.bfloat16),
            pltpu.SemaphoreType.DMA((slots,)),
            pltpu.SemaphoreType.DMA((max(stage_next, 1),)),
        ],
        compiler_params=pltpu.CompilerParams(
            vmem_limit_bytes=max(VMEM_LIMIT, slots * depth * tile * 2 + 3 * rows * depth + 3 * MIB)
        ),
        cost_estimate=pl.CostEstimate(
            flops=4 * rows * depth * tile * tiles, bytes_accessed=4 * depth * tile * tiles, transcendentals=0
        ),
        name="gate_up",
    )(*xs, gate_scales, up_scales, in_vmem(gate_tiles), up_quant, token, *([down_quant] if stage_next else []))


def down_kernel(parts_of, *refs):
    refs = list(refs)
    parts = [(refs.pop(0), refs.pop(0)) for _ in range(parts_of)]
    ds, resident, dq, out, hidden, buffers, sems = refs
    kept, _, tile = resident.shape
    tiles = out.shape[0]
    downs = Tiles(dq, buffers, sems, kept, tiles - kept)
    downs.begin()
    at = 0
    for own, other in parts:
        for i in range(own.shape[1]):
            g = own[0, i] + other[0, i].astype(jnp.float32)
            u = own[1, i] + other[1, i].astype(jnp.float32)
            width = own.shape[3]
            hidden[:, at:at + width] = ((g / (1.0 + jnp.exp(-g))) * u).astype(jnp.bfloat16)
            at += width

    @pl.loop(0, kept)
    def _(i):
        out[i] = tile_dot(hidden, resident.at[i], ds, i * (tile // BLOCK))

    @pl.loop(0, tiles - kept)
    def _(i):
        out[kept + i] = tile_dot(hidden, downs.get(i), ds, (kept + i) * (tile // BLOCK))
        downs.advance(i)


def down(parts, down_scales, resident, down_quant, slots):
    depth, width = down_quant.shape
    tile = resident.shape[2]
    rows = parts[0].shape[2]
    return pl.pallas_call(
        functools.partial(down_kernel, len(parts) // 2),
        in_specs=[VMEM] * len(parts) + [SMEM, VMEM, ANY],
        out_specs=VMEM,
        out_shape=pltpu.VMEM((width // tile, rows, tile), jnp.float32),
        scratch_shapes=[
            pltpu.VMEM((rows, depth), jnp.bfloat16),
            pltpu.VMEM((slots, depth, tile), jnp.bfloat16),
            pltpu.SemaphoreType.DMA((slots,)),
        ],
        compiler_params=pltpu.CompilerParams(
            vmem_limit_bytes=max(VMEM_LIMIT, slots * depth * tile * 2 + 14 * rows * depth - 4 * MIB)
        ),
        cost_estimate=pl.CostEstimate(
            flops=2 * rows * depth * width, bytes_accessed=2 * depth * width, transcendentals=0
        ),
        name="down",
    )(*parts, down_scales, in_vmem(resident), down_quant)


def gather_rows(own, n, shift, beside):
    rows, width = own.shape
    if n == 8:
        half = width // 2
        two_back, two_ahead = shift(own, 2), shift(own, -2)
        one_back, one_ahead = shift(own, 1), shift(own, -1)
        two_back, two_ahead, beside = lax.optimization_barrier((two_back, two_ahead, beside))
        three_back, three_ahead = shift(two_back, 1), shift(two_ahead, -1)
        left, right = shift(two_back[:, :half], 2), shift(two_ahead[:, half:], -2)
        blocks = [own, one_ahead, two_ahead, three_ahead, left, right, three_back, two_back, one_back]
        at = [0, 1, 2, 3, 4, 4, 5, 6, 7]
        return blocks, [(r * rows, half if i == 5 else 0) for i, r in enumerate(at)], beside
    blocks = [own] + [None] * (n - 1)
    fw = bw = own
    for step in range(1, n // 2 + 1):
        fw = shift(fw, 1)
        blocks[n - step] = fw
        if step <= n - 1 - n // 2:
            bw = shift(bw, -1)
            blocks[step] = bw
    return [jnp.concatenate(blocks, axis=0)], [(0, 0)], beside


def scatter_sums(total, n, rows, shift):
    def mine(r):
        r = r % n
        return total[:, r * rows:(r + 1) * rows]

    def sent(value, by):
        return shift(value.astype(jnp.bfloat16), by).astype(jnp.float32)

    if n == 8:
        half = total.shape[0] // 2
        far_left, far_right = sent(mine(4)[:half], 2), sent(mine(4)[half:], -2)
        third, fifth = sent(mine(3), 1), sent(mine(5), -1)
        first, last = sent(mine(1), 1), sent(mine(7), -1)
        ahead, behind = mine(2) + third, mine(6) + fifth
        ahead = jnp.concatenate([ahead[:half] + far_left, ahead[half:]], axis=0)
        behind = jnp.concatenate([behind[:half], behind[half:] + far_right], axis=0)
        return mine(0) + first + last + sent(ahead, 2) + sent(behind, -2)
    ahead, behind = n // 2, n - 1 - n // 2
    fw, bw = mine(ahead), mine(-behind)
    for step in range(1, ahead + 1):
        fw = sent(fw, 1) + mine(ahead - step)
        if step <= behind:
            bw = sent(bw, -1)
            if step < behind:
                bw = bw + mine(step - behind)
    return (fw + bw) if behind else fw


def per_device(n, widths, activations, gate_quant, gate_scales, up_quant, up_scales, down_quant, down_scales):
    order = ring_order(n)

    def shift(value, by):
        return lax.ppermute(value, "hid", [(order[i], order[(i + by) % n]) for i in range(n)])

    rows = activations.shape[0]
    gate_quant, up_quant, down_quant = (
        pltpu.with_memory_space_constraint(a, pltpu.HBM) for a in (gate_quant, up_quant, down_quant)
    )
    hidden_units, width = gate_quant.shape[1], down_quant.shape[1]
    tile = min(hidden_units, 512)
    tiles = hidden_units // tile
    cuts = [0, tiles // 2, tiles] if tiles > 2 else [0, tiles]
    gate_tiles, token = stage(gate_quant, 0, tiles, tile)
    xs, places, token = gather_rows(activations, n, shift, token)
    parts = []
    for start, end in zip(cuts[:-1], cuts[1:]):
        stage_next = min(2, width // tile) if end == tiles else 0
        outs = gate_up(
            xs, places, n * rows, gate_scales, up_scales, gate_tiles, up_quant, start, end, 2, down_quant, stage_next, token
        )
        if len(xs) > 1:
            xs = [outs[2]]
        other = lax.ppermute(outs[1], "wid", [(i, widths - 1 - i) for i in range(widths)])
        parts += [outs[0], other]
    total = down(parts, down_scales, outs[-1], down_quant, 3)
    result = scatter_sums(total, n, rows, shift).astype(jnp.bfloat16)
    return result.transpose(1, 0, 2).reshape(rows, width)


def solution(mesh):
    return jax.shard_map(
        functools.partial(per_device, mesh.shape["hid"], mesh.shape["wid"]),
        mesh=mesh,
        in_specs=(
            P(("group", "hid"), "wid"),
            P("wid", "hid"),
            P("wid", "hid"),
            P("wid", "hid"),
            P("wid", "hid"),
            P("hid", "wid"),
            P("hid", "wid"),
        ),
        out_specs=P(("group", "hid"), "wid"),
        check_vma=False,
    )
```

time: 427 us -> 83.6 us (0.20); the launches traced: 420 us -> 83.4 us
  matrix products: 194 us -> 0 us
  waiting for transfers between devices: 142 us -> 16 us
  local copies, waits for them, and re-layouts: 65.2 us -> 1.75 us
  Pallas kernels: 0 us -> 42.5 us
  starting transfers between devices: 0.08 us -> 22.5 us
  between operations: 13.3 us -> 0.21 us
  other arithmetic: 5.42 us -> 0.37 us
    dot_general x3 -> x0, matrix products: 194 us -> none  [the longest x1 91.5 us: per_device(): up_part = jnp.dot(piece, up_weight, preferred_element_type=jnp.float32)]
    reduce_scatter x1 -> x0, waiting for transfers between devices: 69.1 us -> none  [per_device(): lax.psum_scatter(jnp.dot(hidden, down_weight, preferred_element_type=jnp....]
    mul x3 -> x0, local copies, waits for them, and re-layouts: 65.2 us -> none  [dequantize(): scaled = blocks * scales[:, None, :, None]]
    all_gather x1 -> x0, waiting for transfers between devices: 45.1 us -> none  [per_device(): piece = lax.all_gather(activations, 'hid', axis=0, tiled=True)]
    pallas_call x0 -> x4, Pallas kernels: none -> 42.5 us  [the longest x2 21.4 us: gate_up(): pl.pallas_call(functools.partial(gate_up_kernel, first, tiles, places[:le...]
    psum x1 -> x0, waiting for transfers between devices: 27.3 us -> none  [per_device(): summed = lax.psum(partial_value, 'wid')]
    ppermute x0 -> x18, starting transfers between devices: none -> 22.5 us  [the longest x16 21.9 us: shift(): lax.ppermute(value, 'hid', [(order[i], order[(i + by) % n]) for i in rang...]
    ppermute x0 -> x18, waiting for transfers between devices: none -> 16 us  [the longest x16 13.5 us: shift(): lax.ppermute(value, 'hid', [(order[i], order[(i + by) % n]) for i in rang...]
  transfers between devices with their start and end apart: 3 -> 18, of which waited for: 3 -> 7; matrix products, arithmetic and copies ran while one was open for 0% -> 0% of each run, Pallas kernels for 0% -> 27%
where the time goes in v2:
time: 83.6 us; the launch traced here: 83.4 us
  Pallas kernels  42.5 us (51%)
  starting transfers between devices  22.5 us (27%)
  waiting for transfers between devices  16 us (19%)
  local copies, waits for them, and re-layouts  1.75 us (2%)
    ppermute x16, starting transfers between devices, shift(): lax.ppermute(value, 'hid', [(order[i], order[(i + by) % n]) for i in rang...  21.9 us
    pallas_call x2, Pallas kernels, gate_up(): pl.pallas_call(functools.partial(gate_up_kernel, first, tiles, places[:le...  21.4 us
    ppermute x16, waiting for transfers between devices, shift(): lax.ppermute(value, 'hid', [(order[i], order[(i + by) % n]) for i in rang...  13.5 us
    pallas_call x1, Pallas kernels, stage(): pl.pallas_call(functools.partial(stage_kernel, first), in_specs=[ANY], ou...  10.8 us
    pallas_call x1, Pallas kernels, down(): pl.pallas_call(functools.partial(down_kernel, len(parts) // 2), in_specs=...  10.3 us
    ppermute x2, waiting for transfers between devices, per_device(): lax.ppermute(outs[1], 'wid', [(i, widths - 1 - i) for i in range(widths)])  2.5 us
  transfers between devices with their start and end apart: 18, of which 7 were waited for; matrix products, arithmetic and copies ran while one was open for 0% of the time, Pallas kernels for 27%

profile of v2, /device:TPU:0, one launch (start us, length us, event | category | flops | bytes accessed | tf_op | source)
XLA Modules:
  0.0 83.4 jit_solution(18439636349500015516)
XLA Ops:
  0.0 4.1 %collective-permute-start.1 = (bf16[16,4096]{1,0:T(8,128)(2,1)}, bf16[16,4096]{1,0:T(8,128)(2,1)S(1)}, u32[]{:S(2)}, u32[]{:S(2)}) collective-permute-start(bf16[16,4096]{1,0:T(8,128)(2,1)} %refs_0_.3), channel_id=1, source_target_pairs={{0,8},{4,12},{8,14},{12,10},{14,6},{10,2},{6,0},{2,4},{1,9},{5,13}... | collective-permute-start | bytes 393224 | tf_op jit(solution)/shard_map/ppermute | solution.py:289
  4.1 0.0 collective-permute-start.2
  4.1 1.8 %collective-permute-start = (bf16[16,4096]{1,0:T(8,128)(2,1)}, bf16[16,4096]{1,0:T(8,128)(2,1)S(1)}, u32[]{:S(2)}, u32[]{:S(2)}) collective-permute-start(bf16[16,4096]{1,0:T(8,128)(2,1)} %refs_0_.3), channel_id=1, source_target_pairs={{0,2},{4,0},{8,4},{12,8},{14,12},{10,14},{6,10},{2,6},{1,3},{5,1},... | collective-permute-start | bytes 393224 | tf_op jit(solution)/shard_map/ppermute | solution.py:289
  6.0 0.2 collective-permute-start.7
  6.1 10.8 %stage.1 = (bf16[8,4096,512]{2,1,0:T(8,128)(2,1)S(1)}, bf16[16,128]{1,0:T(8,128)(2,1)S(1)}) custom-call(bf16[4096,4096]{1,0:T(8,128)(2,1)} %refs_0_.2), custom_call_target="tpu_custom_call" | custom-call | bytes 33554432 | tf_op jit(solution)/shard_map/stage/pallas_call | solution.py:100
  17.0 0.0 copy-start.5
  17.0 0.0 collective-permute-done.1.refs_7_
  17.0 0.0 collective-permute-done.2.refs_2_
  17.0 1.9 %collective-permute-start.3 = (bf16[16,4096]{1,0:T(8,128)(2,1)S(1)}, bf16[16,4096]{1,0:T(8,128)(2,1)S(1)}, u32[]{:S(2)}, u32[]{:S(2)}) collective-permute-start(bf16[16,4096]{1,0:T(8,128)(2,1)S(1)} %collective-permute-done.2.refs_2_), channel_id=1, source_target_pairs={{0,2},{4,0},{8,4},{12,8},{14,12},{10,14},{6,10},{2,6},{1,3},{5,1},... | collective-permute-start | bytes 393224 | tf_op jit(solution)/shard_map/ppermute | solution.py:289
  18.9 0.2 collective-permute-start.6
  19.1 3.0 %collective-permute-start.4 = (bf16[16,2048]{1,0:T(8,128)(2,1)S(1)}, bf16[16,2048]{1,0:T(8,128)(2,1)S(1)}, u32[]{:S(2)}, u32[]{:S(2)}) collective-permute-start(bf16[16,2048]{1,0:T(8,128)(2,1)S(1)} %slice.57), channel_id=1, source_target_pairs={{0,8},{4,12},{8,14},{12,10},{14,6},{10,2},{6,0},{2,4},{1,9},{5,13}... | collective-permute-start | bytes 196616 | tf_op jit(solution)/shard_map/ppermute | solution.py:289
  22.0 0.0 collective-permute-done.refs_1_
  22.1 0.0 collective-permute-start.5
  22.1 0.0 collective-permute-done.7.refs_8_
  22.1 4.1 %collective-permute-done.4.refs_4_ = bf16[16,2048]{1,0:T(8,128)(2,1)S(1)} collective-permute-done((bf16[16,2048]{1,0:T(8,128)(2,1)S(1)}, bf16[16,2048]{1,0:T(8,128)(2,1)S(1)}, u32[]{:S(2)}, u32[]{:S(2)}) %collective-permute-start.4) | collective-permute-done | bytes 65568 | tf_op jit(solution)/shard_map/ppermute | solution.py:289
  26.2 1.1 %collective-permute-done.5.refs_5_ = bf16[16,2048]{1,0:T(8,128)(2,1)S(1)} collective-permute-done((bf16[16,2048]{1,0:T(8,128)(2,1)S(1)}, bf16[16,2048]{1,0:T(8,128)(2,1)S(1)}, u32[]{:S(2)}, u32[]{:S(2)}) %collective-permute-start.5) | collective-permute-done | bytes 65568 | tf_op jit(solution)/shard_map/ppermute | solution.py:289
  27.2 0.0 collective-permute-done.3.refs_3_
  27.2 0.0 collective-permute-done.6.refs_6_
  27.2 0.0 copy-done.2
  27.2 0.0 copy-done.3
  27.3 9.7 %gate_up.2 = (f32[2,4,128,512]{3,2,1,0:T(8,128)S(1)}, bf16[2,4,128,512]{3,2,1,0:T(8,128)(2,1)S(1)}, bf16[128,4096]{1,0:T(8,128)(2,1)S(1)}) custom-call(bf16[16,4096]{1,0:T(8,128)(2,1)S(1)} %copy-done.1, bf16[16,4096]{1,0:T(8,128)(2,1)S(1)} %collective-permute-done.refs_1_, bf16[16,4096]{1,0:T(8,128)(2,1)S(1)} %collective-permute-done.2.refs_2_, ...), custom_call_target="tpu_custom_call" | custom-call | flops 4294967296 | bytes 33554432 | tf_op jit(solution)/shard_map/gate_up/pallas_call | solution.py:163
  37.0 1.0 %copy-done = bf16[128,4096]{1,0:T(8,128)(2,1)} copy-done((bf16[128,4096]{1,0:T(8,128)(2,1)}, bf16[128,4096]{1,0:T(8,128)(2,1)S(1)}, u32[]{:S(2)}) %copy-start) | copy-done | bytes 1048600
  37.9 0.0 collective-permute-start.8
  38.0 11.7 %gate_up.3 = (f32[2,4,128,512]{3,2,1,0:T(8,128)S(1)}, bf16[2,4,128,512]{3,2,1,0:T(8,128)(2,1)}, bf16[2,4096,512]{2,1,0:T(8,128)(2,1)S(1)}) custom-call(bf16[128,4096]{1,0:T(8,128)(2,1)} %copy-done, f32[32,32]{1,0:T(8,128)} %refs_1_.1, f32[32,32]{1,0:T(8,128)} %refs_2_.1, bf16[8,4096,512]{2,1,0:T(8,128)(2,1)S(1)} %get-tuple-element.19.refs_11_.refs_3_, ...), custom_call_target="tpu_custom_call" | custom-call | flops 4294967296 | bytes 33554432 | tf_op jit(solution)/shard_map/gate_up/pallas_call | solution.py:163
  49.7 0.6 collective-permute-start.9
  50.3 0.0 collective-permute-done.8.refs_1_
  50.3 2.5 %collective-permute-done.9.refs_3_ = bf16[2,4,128,512]{3,2,1,0:T(8,128)(2,1)S(1)} collective-permute-done((bf16[2,4,128,512]{3,2,1,0:T(8,128)(2,1)}, bf16[2,4,128,512]{3,2,1,0:T(8,128)(2,1)S(1)}, u32[]{:S(2)}, u32[]{:S(2)}) %collective-permute-start.9) | collective-permute-done | bytes 1048608 | tf_op jit(solution)/shard_map/ppermute | solution.py:309
  52.8 10.3 %down.1 = f32[8,128,512]{2,1,0:T(8,128)S(1)} custom-call(f32[2,4,128,512]{3,2,1,0:T(8,128)S(1)} %get-tuple-element.21.refs_0_, bf16[2,4,128,512]{3,2,1,0:T(8,128)(2,1)S(1)} %collective-permute-done.8.refs_1_, f32[2,4,128,512]{3,2,1,0:T(8,128)S(1)} %get-tuple-element.24.refs_2_, bf16[2,4,128,512]{3,2,1,0:T(8,128)(2,1)S(1)} %collective-permute-done.9.refs_3_, ...), custom_call_target="tpu_custom_call" | custom-call | flops 4294967296 | bytes 33554432 | tf_op jit(solution)/shard_map/down/pallas_call | solution.py:214
  63.1 0.1 convert.22
  63.3 1.6 %collective-permute-start.12 = (bf16[8,16,512]{2,1,0:T(8,128)(2,1)S(1)}, bf16[8,16,512]{2,1,0:T(8,128)(2,1)S(1)}, u32[]{:S(2)}, u32[]{:S(2)}) collective-permute-start(bf16[8,16,512]{2,1,0:T(8,128)(2,1)S(1)} %get-tuple-element.31), channel_id=1, source_target_pairs={{0,4},{4,8},{8,12},{12,14},{14,10},{10,6},{6,2},{2,0},{1,5},{5,9},... | collective-permute-start | bytes 393224 | tf_op jit(solution)/shard_map/ppermute | solution.py:289
  64.9 0.4 collective-permute-start.15
  65.4 1.6 %collective-permute-start.16 = (bf16[4,16,512]{2,1,0:T(8,128)(2,1)S(1)}, bf16[4,16,512]{2,1,0:T(8,128)(2,1)S(1)}, u32[]{:S(2)}, u32[]{:S(2)}) collective-permute-start(bf16[4,16,512]{2,1,0:T(8,128)(2,1)S(1)} %get-tuple-element.34), channel_id=1, source_target_pairs={{0,6},{4,2},{8,0},{12,4},{14,8},{10,12},{6,14},{2,10},{1,7},{5,3},... | collective-permute-start | bytes 196616 | tf_op jit(solution)/shard_map/ppermute | solution.py:289
  67.0 1.4 %collective-permute-start.13 = (bf16[4,16,512]{2,1,0:T(8,128)(2,1)S(1)}, bf16[4,16,512]{2,1,0:T(8,128)(2,1)S(1)}, u32[]{:S(2)}, u32[]{:S(2)}) collective-permute-start(bf16[4,16,512]{2,1,0:T(8,128)(2,1)S(1)} %get-tuple-element.33), channel_id=1, source_target_pairs={{0,8},{4,12},{8,14},{12,10},{14,6},{10,2},{6,0},{2,4},{1,9},{5,13}... | collective-permute-start | bytes 196616 | tf_op jit(solution)/shard_map/ppermute | solution.py:289
  68.4 0.5 collective-permute-start.11
  68.9 0.2 collective-permute-done.12
  69.1 2.1 %collective-permute-start.10 = (bf16[8,16,512]{2,1,0:T(8,128)(2,1)S(1)}, bf16[8,16,512]{2,1,0:T(8,128)(2,1)S(1)}, u32[]{:S(2)}, u32[]{:S(2)}) collective-permute-start(bf16[8,16,512]{2,1,0:T(8,128)(2,1)S(1)} %get-tuple-element.29), channel_id=1, source_target_pairs={{0,4},{4,8},{8,12},{12,14},{14,10},{10,6},{6,2},{2,0},{1,5},{5,9},... | collective-permute-start | bytes 393224 | tf_op jit(solution)/shard_map/ppermute | solution.py:289
  71.2 0.5 collective-permute-done.15
  71.7 0.1 slice_add_fusion.1
  71.8 3.2 %collective-permute-done.16 = bf16[4,16,512]{2,1,0:T(8,128)(2,1)S(1)} collective-permute-done((bf16[4,16,512]{2,1,0:T(8,128)(2,1)S(1)}, bf16[4,16,512]{2,1,0:T(8,128)(2,1)S(1)}, u32[]{:S(2)}, u32[]{:S(2)}) %collective-permute-start.16) | collective-permute-done | bytes 65568 | tf_op jit(solution)/shard_map/ppermute | solution.py:289
  75.1 0.1 collective-permute-start.17
  75.2 0.0 collective-permute-done.13
  75.2 3.0 %collective-permute-start.14 = (bf16[8,16,512]{2,1,0:T(8,128)(2,1)S(1)}, bf16[8,16,512]{2,1,0:T(8,128)(2,1)S(1)}, u32[]{:S(2)}, u32[]{:S(2)}) collective-permute-start(bf16[8,16,512]{2,1,0:T(8,128)(2,1)S(1)} %pad_maximum_fusion), channel_id=1, source_target_pairs={{0,8},{4,12},{8,14},{12,10},{14,6},{10,2},{6,0},{2,4},{1,9},{5,13}... | collective-permute-start | bytes 393224 | tf_op jit(solution)/shard_map/ppermute | solution.py:289
  78.2 0.0 collective-permute-done.11
  78.2 0.0 collective-permute-done.10
  78.2 4.4 %collective-permute-done.17 = bf16[8,16,512]{2,1,0:T(8,128)(2,1)S(1)} collective-permute-done((bf16[8,16,512]{2,1,0:T(8,128)(2,1)S(1)}, bf16[8,16,512]{2,1,0:T(8,128)(2,1)S(1)}, u32[]{:S(2)}, u32[]{:S(2)}) %collective-permute-start.17) | collective-permute-done | bytes 131104 | tf_op jit(solution)/shard_map/ppermute | solution.py:289
  82.6 0.0 collective-permute-done.14
  82.6 0.1 fusion.4
  82.7 0.7 copy.9
  (18 shorter events, 0.2 us)
Async XLA Ops:
  0.0 27.2 %copy-start.1 = (bf16[16,4096]{1,0:T(8,128)(2,1)S(1)}, bf16[16,4096]{1,0:T(8,128)(2,1)}, u32[]{:S(2)}) copy-start(bf16[16,4096]{1,0:T(8,128)(2,1)} %refs_0_.3) | copy-start | bytes 393220
  0.0 27.2 %copy-start.2 = (f32[32,32]{1,0:T(8,128)S(1)}, f32[32,32]{1,0:T(8,128)}, u32[]{:S(2)}) copy-start(f32[32,32]{1,0:T(8,128)} %refs_1_.1) | copy-start | bytes 12292
  0.0 27.2 %copy-start.3 = (f32[32,32]{1,0:T(8,128)S(1)}, f32[32,32]{1,0:T(8,128)}, u32[]{:S(2)}) copy-start(f32[32,32]{1,0:T(8,128)} %refs_2_.1) | copy-start | bytes 12292
  0.0 17.0 %collective-permute-start.1 = (bf16[16,4096]{1,0:T(8,128)(2,1)}, bf16[16,4096]{1,0:T(8,128)(2,1)S(1)}, u32[]{:S(2)}, u32[]{:S(2)}) collective-permute-start(bf16[16,4096]{1,0:T(8,128)(2,1)} %refs_0_.3), channel_id=1, source_target_pairs={{0,8},{4,12},{8,14},{12,10},{14,6},{10,2},{6,0},{2,4},{1,9},{5,13}... | collective-permute-start | bytes 393224 | tf_op jit(solution)/shard_map/ppermute | solution.py:289
  4.1 12.9 %collective-permute-start.2 = (bf16[16,4096]{1,0:T(8,128)(2,1)}, bf16[16,4096]{1,0:T(8,128)(2,1)S(1)}, u32[]{:S(2)}, u32[]{:S(2)}) collective-permute-start(bf16[16,4096]{1,0:T(8,128)(2,1)} %refs_0_.3), channel_id=1, source_target_pairs={{0,6},{4,2},{8,0},{12,4},{14,8},{10,12},{6,14},{2,10},{1,7},{5,3},... | collective-permute-start | bytes 393224 | tf_op jit(solution)/shard_map/ppermute | solution.py:289
  4.1 17.9 %collective-permute-start = (bf16[16,4096]{1,0:T(8,128)(2,1)}, bf16[16,4096]{1,0:T(8,128)(2,1)S(1)}, u32[]{:S(2)}, u32[]{:S(2)}) collective-permute-start(bf16[16,4096]{1,0:T(8,128)(2,1)} %refs_0_.3), channel_id=1, source_target_pairs={{0,2},{4,0},{8,4},{12,8},{14,12},{10,14},{6,10},{2,6},{1,3},{5,1},... | collective-permute-start | bytes 393224 | tf_op jit(solution)/shard_map/ppermute | solution.py:289
  6.0 16.1 %collective-permute-start.7 = (bf16[16,4096]{1,0:T(8,128)(2,1)}, bf16[16,4096]{1,0:T(8,128)(2,1)S(1)}, u32[]{:S(2)}, u32[]{:S(2)}) collective-permute-start(bf16[16,4096]{1,0:T(8,128)(2,1)} %refs_0_.3), channel_id=1, source_target_pairs={{0,4},{4,8},{8,12},{12,14},{14,10},{10,6},{6,2},{2,0},{1,5},{5,9},... | collective-permute-start | bytes 393224 | tf_op jit(solution)/shard_map/ppermute | solution.py:289
  17.0 20.0 %copy-start.5 = (bf16[16,128]{1,0:T(8,128)(2,1)}, bf16[16,128]{1,0:T(8,128)(2,1)S(1)}, u32[]{:S(2)}) copy-start(bf16[16,128]{1,0:T(8,128)(2,1)S(1)} %get-tuple-element.20.refs_13_.refs_5_) | copy-start | bytes 12292
  17.0 10.2 %collective-permute-start.3 = (bf16[16,4096]{1,0:T(8,128)(2,1)S(1)}, bf16[16,4096]{1,0:T(8,128)(2,1)S(1)}, u32[]{:S(2)}, u32[]{:S(2)}) collective-permute-start(bf16[16,4096]{1,0:T(8,128)(2,1)S(1)} %collective-permute-done.2.refs_2_), channel_id=1, source_target_pairs={{0,2},{4,0},{8,4},{12,8},{14,12},{10,14},{6,10},{2,6},{1,3},{5,1},... | collective-permute-start | bytes 393224 | tf_op jit(solution)/shard_map/ppermute | solution.py:289
  18.9 8.3 %collective-permute-start.6 = (bf16[16,4096]{1,0:T(8,128)(2,1)S(1)}, bf16[16,4096]{1,0:T(8,128)(2,1)S(1)}, u32[]{:S(2)}, u32[]{:S(2)}) collective-permute-start(bf16[16,4096]{1,0:T(8,128)(2,1)S(1)} %collective-permute-done.1.refs_7_), channel_id=1, source_target_pairs={{0,4},{4,8},{8,12},{12,14},{14,10},{10,6},{6,2},{2,0},{1,5},{5,9},... | collective-permute-start | bytes 393224 | tf_op jit(solution)/shard_map/ppermute | solution.py:289
  19.1 7.1 %collective-permute-start.4 = (bf16[16,2048]{1,0:T(8,128)(2,1)S(1)}, bf16[16,2048]{1,0:T(8,128)(2,1)S(1)}, u32[]{:S(2)}, u32[]{:S(2)}) collective-permute-start(bf16[16,2048]{1,0:T(8,128)(2,1)S(1)} %slice.57), channel_id=1, source_target_pairs={{0,8},{4,12},{8,14},{12,10},{14,6},{10,2},{6,0},{2,4},{1,9},{5,13}... | collective-permute-start | bytes 196616 | tf_op jit(solution)/shard_map/ppermute | solution.py:289
  22.1 5.2 %collective-permute-start.5 = (bf16[16,2048]{1,0:T(8,128)(2,1)S(1)}, bf16[16,2048]{1,0:T(8,128)(2,1)S(1)}, u32[]{:S(2)}, u32[]{:S(2)}) collective-permute-start(bf16[16,2048]{1,0:T(8,128)(2,1)S(1)} %slice.58), channel_id=1, source_target_pairs={{0,6},{4,2},{8,0},{12,4},{14,8},{10,12},{6,14},{2,10},{1,7},{5,3},... | collective-permute-start | bytes 196616 | tf_op jit(solution)/shard_map/ppermute | solution.py:289
  37.0 1.0 %copy-start = (bf16[128,4096]{1,0:T(8,128)(2,1)}, bf16[128,4096]{1,0:T(8,128)(2,1)S(1)}, u32[]{:S(2)}) copy-start(bf16[128,4096]{1,0:T(8,128)(2,1)S(1)} %get-tuple-element.23.refs_0_) | copy-start | bytes 3145732
  37.9 12.3 %collective-permute-start.8 = (bf16[2,4,128,512]{3,2,1,0:T(8,128)(2,1)S(1)}, bf16[2,4,128,512]{3,2,1,0:T(8,128)(2,1)S(1)}, u32[]{:S(2)}, u32[]{:S(2)}) collective-permute-start(bf16[2,4,128,512]{3,2,1,0:T(8,128)(2,1)S(1)} %get-tuple-element.22), channel_id=1, source_target_pairs={{0,1},{1,0},{2,3},{3,2},{4,5},{5,4},{6,7},{7,6},{8,9},{9,8},{10,11... | collective-permute-start | bytes 3145736 | tf_op jit(solution)/shard_map/ppermute | solution.py:309
  38.0 14.8 %copy-start.4 = (f32[32,32]{1,0:T(8,128)S(1)}, f32[32,32]{1,0:T(8,128)}, u32[]{:S(2)}) copy-start(f32[32,32]{1,0:T(8,128)} %refs_4_.3) | copy-start | bytes 12292
  49.7 3.1 %collective-permute-start.9 = (bf16[2,4,128,512]{3,2,1,0:T(8,128)(2,1)}, bf16[2,4,128,512]{3,2,1,0:T(8,128)(2,1)S(1)}, u32[]{:S(2)}, u32[]{:S(2)}) collective-permute-start(bf16[2,4,128,512]{3,2,1,0:T(8,128)(2,1)} %get-tuple-element.25), channel_id=1, source_target_pairs={{0,1},{1,0},{2,3},{3,2},{4,5},{5,4},{6,7},{7,6},{8,9},{9,8},{10,11... | collective-permute-start | bytes 3145736 | tf_op jit(solution)/shard_map/ppermute | solution.py:309
  63.3 5.8 %collective-permute-start.12 = (bf16[8,16,512]{2,1,0:T(8,128)(2,1)S(1)}, bf16[8,16,512]{2,1,0:T(8,128)(2,1)S(1)}, u32[]{:S(2)}, u32[]{:S(2)}) collective-permute-start(bf16[8,16,512]{2,1,0:T(8,128)(2,1)S(1)} %get-tuple-element.31), channel_id=1, source_target_pairs={{0,4},{4,8},{8,12},{12,14},{14,10},{10,6},{6,2},{2,0},{1,5},{5,9},... | collective-permute-start | bytes 393224 | tf_op jit(solution)/shard_map/ppermute | solution.py:289
  64.9 6.8 %collective-permute-start.15 = (bf16[8,16,512]{2,1,0:T(8,128)(2,1)S(1)}, bf16[8,16,512]{2,1,0:T(8,128)(2,1)S(1)}, u32[]{:S(2)}, u32[]{:S(2)}) collective-permute-start(bf16[8,16,512]{2,1,0:T(8,128)(2,1)S(1)} %get-tuple-element.30), channel_id=1, source_target_pairs={{0,2},{4,0},{8,4},{12,8},{14,12},{10,14},{6,10},{2,6},{1,3},{5,1},... | collective-permute-start | bytes 393224 | tf_op jit(solution)/shard_map/ppermute | solution.py:289
  65.4 9.7 %collective-permute-start.16 = (bf16[4,16,512]{2,1,0:T(8,128)(2,1)S(1)}, bf16[4,16,512]{2,1,0:T(8,128)(2,1)S(1)}, u32[]{:S(2)}, u32[]{:S(2)}) collective-permute-start(bf16[4,16,512]{2,1,0:T(8,128)(2,1)S(1)} %get-tuple-element.34), channel_id=1, source_target_pairs={{0,6},{4,2},{8,0},{12,4},{14,8},{10,12},{6,14},{2,10},{1,7},{5,3},... | collective-permute-start | bytes 196616 | tf_op jit(solution)/shard_map/ppermute | solution.py:289
  67.0 8.2 %collective-permute-start.13 = (bf16[4,16,512]{2,1,0:T(8,128)(2,1)S(1)}, bf16[4,16,512]{2,1,0:T(8,128)(2,1)S(1)}, u32[]{:S(2)}, u32[]{:S(2)}) collective-permute-start(bf16[4,16,512]{2,1,0:T(8,128)(2,1)S(1)} %get-tuple-element.33), channel_id=1, source_target_pairs={{0,8},{4,12},{8,14},{12,10},{14,6},{10,2},{6,0},{2,4},{1,9},{5,13}... | collective-permute-start | bytes 196616 | tf_op jit(solution)/shard_map/ppermute | solution.py:289
  68.4 9.8 %collective-permute-start.11 = (bf16[8,16,512]{2,1,0:T(8,128)(2,1)S(1)}, bf16[8,16,512]{2,1,0:T(8,128)(2,1)S(1)}, u32[]{:S(2)}, u32[]{:S(2)}) collective-permute-start(bf16[8,16,512]{2,1,0:T(8,128)(2,1)S(1)} %get-tuple-element.32), channel_id=1, source_target_pairs={{0,2},{4,0},{8,4},{12,8},{14,12},{10,14},{6,10},{2,6},{1,3},{5,1},... | collective-permute-start | bytes 393224 | tf_op jit(solution)/shard_map/ppermute | solution.py:289
  69.1 9.1 %collective-permute-start.10 = (bf16[8,16,512]{2,1,0:T(8,128)(2,1)S(1)}, bf16[8,16,512]{2,1,0:T(8,128)(2,1)S(1)}, u32[]{:S(2)}, u32[]{:S(2)}) collective-permute-start(bf16[8,16,512]{2,1,0:T(8,128)(2,1)S(1)} %get-tuple-element.29), channel_id=1, source_target_pairs={{0,4},{4,8},{8,12},{12,14},{14,10},{10,6},{6,2},{2,0},{1,5},{5,9},... | collective-permute-start | bytes 393224 | tf_op jit(solution)/shard_map/ppermute | solution.py:289
  75.1 7.5 %collective-permute-start.17 = (bf16[8,16,512]{2,1,0:T(8,128)(2,1)S(1)}, bf16[8,16,512]{2,1,0:T(8,128)(2,1)S(1)}, u32[]{:S(2)}, u32[]{:S(2)}) collective-permute-start(bf16[8,16,512]{2,1,0:T(8,128)(2,1)S(1)} %pad_maximum_fusion.1), channel_id=1, source_target_pairs={{0,6},{4,2},{8,0},{12,4},{14,8},{10,12},{6,14},{2,10},{1,7},{5,3},... | collective-permute-start | bytes 393224 | tf_op jit(solution)/shard_map/ppermute | solution.py:289
  75.2 7.4 %collective-permute-start.14 = (bf16[8,16,512]{2,1,0:T(8,128)(2,1)S(1)}, bf16[8,16,512]{2,1,0:T(8,128)(2,1)S(1)}, u32[]{:S(2)}, u32[]{:S(2)}) collective-permute-start(bf16[8,16,512]{2,1,0:T(8,128)(2,1)S(1)} %pad_maximum_fusion), channel_id=1, source_target_pairs={{0,8},{4,12},{8,14},{12,10},{14,6},{10,2},{6,0},{2,4},{1,9},{5,13}... | collective-permute-start | bytes 393224 | tf_op jit(solution)/shard_map/ppermute | solution.py:289

commit v3 on v2

--- a/solution.py
+++ b/solution.py
@@ -10,6 +10,7 @@
 BLOCK = 128
 MIB = 1024 * 1024
 VMEM_LIMIT = 16 * MIB
+KEPT = 2
 VMEM = pl.BlockSpec(memory_space=pltpu.VMEM)
 SMEM = pl.BlockSpec(memory_space=pltpu.SMEM)
 ANY = pl.BlockSpec(memory_space=pl.ANY)
@@ -57,8 +58,14 @@
             self.quant.at[:, pl.ds(start, self.width)], self.buffers.at[slot], self.sems.at[slot]
         )
 
-    def begin(self):
-        for i in range(min(self.count, self.slots)):
+    def start(self, i):
+        if isinstance(i, int):
+            if i < min(self.count, self.slots):
+                self.copy(i).start()
+            return
+
+        @pl.when(i < min(self.count, self.slots))
+        def _():
             self.copy(i).start()
 
     def get(self, i):
@@ -71,11 +78,11 @@
             self.copy(i + self.slots).start()
 
 
-def tile_copies(quant, first, staged, sems):
-    count, _, width = staged.shape
+def tile_copies(quant, first, staged, at, count, sems):
+    width = staged.shape[2]
     return [
         pltpu.make_async_copy(
-            quant.at[:, (first + i) * width:(first + i + 1) * width], staged.at[i], sems.at[i]
+            quant.at[:, (first + i) * width:(first + i + 1) * width], staged.at[at + i], sems.at[i]
         )
         for i in range(count)
     ]
@@ -85,9 +92,9 @@
     return pltpu.with_memory_space_constraint(array, pltpu.VMEM)
 
 
-def stage_kernel(first, *refs):
-    quant, staged, token, sems = refs
-    copies = tile_copies(quant, first, staged, sems)
+def stage_kernel(first, at, count, *refs):
+    quant, staged, token, sems = refs[0], refs[-3], refs[-2], refs[-1]
+    copies = tile_copies(quant, first, staged, at, count, sems)
     for copy in copies:
         copy.start()
     token[...] = jnp.zeros_like(token)
@@ -95,60 +102,67 @@
         copy.wait()
 
 
-def stage(quant, first, count, tile):
+def stage(quant, first, tile, total, at, count, filled=None, after=()):
     depth = quant.shape[0]
+    more = list(after) if filled is None else [in_vmem(filled), *after]
     return pl.pallas_call(
-        functools.partial(stage_kernel, first),
-        in_specs=[ANY],
+        functools.partial(stage_kernel, first, at, count),
+        in_specs=[ANY] + ([] if filled is None else [VMEM]) + [ANY] * len(after),
         out_specs=[VMEM, VMEM],
-        out_shape=[pltpu.VMEM((count, depth, tile), quant.dtype), pltpu.VMEM((16, BLOCK), jnp.bfloat16)],
+        out_shape=[pltpu.VMEM((total, depth, tile), quant.dtype), pltpu.VMEM((16, BLOCK), jnp.bfloat16)],
+        input_output_aliases={} if filled is None else {1: 0},
         scratch_shapes=[pltpu.SemaphoreType.DMA((count,))],
         compiler_params=pltpu.CompilerParams(vmem_limit_bytes=VMEM_LIMIT),
         cost_estimate=pl.CostEstimate(
             flops=0, bytes_accessed=2 * count * depth * tile, transcendentals=0
         ),
         name="stage",
-    )(quant)
-
-
-def gate_up_kernel(first, tiles, places, keep_x, stage_next, *refs):
+    )(quant, *more)
+
+
+def gate_up_kernel(first, tiles, places, keep_x, *refs):
     refs = list(refs)
     xs = [refs.pop(0) for _ in places]
     gs, us, gq, uq, _ = [refs.pop(0) for _ in range(5)]
-    dq = refs.pop(0) if stage_next else None
     own, send = refs.pop(0), refs.pop(0)
     x = refs.pop(0) if keep_x else xs[0]
-    staged = refs.pop(0) if stage_next else None
-    buffers, sems, staged_sems = refs
+    buffers, sems = refs
     tile = gq.shape[2]
     ups = Tiles(uq, buffers, sems, first, tiles)
-    ups.begin()
+    ups.start(0)
     if keep_x:
         for ref, (row, col) in zip(xs, places):
             x[row:row + ref.shape[0], col:col + ref.shape[1]] = ref[...]
-    copies = tile_copies(dq, 0, staged, staged_sems) if stage_next else []
-
-    @pl.loop(0, tiles)
-    def _(i):
-        col = (first + i) * (tile // BLOCK)
-        g = tile_dot(x, gq.at[first + i], gs, col)
+
+    def gate(i):
+        g = tile_dot(x, gq.at[first + i], gs, (first + i) * (tile // BLOCK))
         own[0, i] = g
         send[0, i] = g.astype(jnp.bfloat16)
-        u = tile_dot(x, ups.get(i), us, col)
+
+    def up(i):
+        u = tile_dot(x, ups.get(i), us, (first + i) * (tile // BLOCK))
         own[1, i] = u
         send[1, i] = u.astype(jnp.bfloat16)
         ups.advance(i)
 
-        @pl.when(i == max(tiles - ups.slots, 1) - 1)
-        def _():
-            for copy in copies:
-                copy.start()
-
-    for copy in copies:
-        copy.wait()
-
-
-def gate_up(xs, places, rows, gate_scales, up_scales, gate_tiles, up_quant, first, end, slots, down_quant, stage_next, token):
+    lead = min(ups.slots, tiles)
+
+    @pl.loop(0, tiles + lead)
+    def _(i):
+        @pl.when(i >= lead)
+        def _():
+            up(i - lead)
+
+        @pl.when(i < tiles)
+        def _():
+            gate(i)
+
+        @pl.when(i < lead)
+        def _():
+            ups.start(i + 1)
+
+
+def gate_up(xs, places, rows, gate_scales, up_scales, gate_tiles, up_quant, first, end, slots, token):
     _, depth, tile = gate_tiles.shape
     tiles = end - first
     keep_x = len(xs) > 1
@@ -158,17 +172,14 @@
     ]
     if keep_x:
         out_shape.append(pltpu.VMEM((rows, depth), jnp.bfloat16))
-    if stage_next:
-        out_shape.append(pltpu.VMEM((stage_next, down_quant.shape[0], tile), down_quant.dtype))
     return pl.pallas_call(
-        functools.partial(gate_up_kernel, first, tiles, places[:len(xs)], keep_x, stage_next),
-        in_specs=[VMEM] * len(xs) + [SMEM, SMEM, VMEM, ANY, ANY] + [ANY] * (stage_next > 0),
+        functools.partial(gate_up_kernel, first, tiles, places[:len(xs)], keep_x),
+        in_specs=[VMEM] * len(xs) + [SMEM, SMEM, VMEM, ANY, ANY],
         out_specs=[VMEM] * len(out_shape),
         out_shape=out_shape,
         scratch_shapes=[
             pltpu.VMEM((slots, depth, tile), jnp.bfloat16),
             pltpu.SemaphoreType.DMA((slots,)),
-            pltpu.SemaphoreType.DMA((max(stage_next, 1),)),
         ],
         compiler_params=pltpu.CompilerParams(
             vmem_limit_bytes=max(VMEM_LIMIT, slots * depth * tile * 2 + 3 * rows * depth + 3 * MIB)
@@ -177,29 +188,71 @@
             flops=4 * rows * depth * tile * tiles, bytes_accessed=4 * depth * tile * tiles, transcendentals=0
         ),
         name="gate_up",
-    )(*xs, gate_scales, up_scales, in_vmem(gate_tiles), up_quant, token, *([down_quant] if stage_next else []))
-
-
-def down_kernel(parts_of, *refs):
+    )(*xs, gate_scales, up_scales, in_vmem(gate_tiles), up_quant, token)
+
+
+def activate(parts, hidden, at):
+    for own, other in parts:
+        width = own.shape[3]
+        for i in range(own.shape[1]):
+            g = own[0, i] + other[0, i].astype(jnp.float32)
+            u = own[1, i] + other[1, i].astype(jnp.float32)
+            hidden[:, at:at + width] = ((g / (1.0 + jnp.exp(-g))) * u).astype(jnp.bfloat16)
+            at += width
+
+
+def prepare_kernel(parts_of, *refs):
     refs = list(refs)
+    quant = refs.pop(0)
     parts = [(refs.pop(0), refs.pop(0)) for _ in range(parts_of)]
-    ds, resident, dq, out, hidden, buffers, sems = refs
+    staged, hidden, sems = refs[-3:]
+    copies = tile_copies(quant, 0, staged, 0, staged.shape[0], sems)
+    for copy in copies:
+        copy.start()
+    activate(parts, hidden, 0)
+    for copy in copies:
+        copy.wait()
+
+
+def prepare(down_quant, parts, tile, kept, after):
+    depth = down_quant.shape[0]
+    rows = parts[0].shape[2]
+    units = sum(own.shape[1] * own.shape[3] for own in parts[::2])
+    return pl.pallas_call(
+        functools.partial(prepare_kernel, len(parts) // 2),
+        in_specs=[ANY] + [VMEM] * len(parts) + [ANY],
+        out_specs=[VMEM, VMEM],
+        out_shape=[
+            pltpu.VMEM((kept, depth, tile), down_quant.dtype),
+            pltpu.VMEM((rows, units), jnp.bfloat16),
+        ],
+        scratch_shapes=[pltpu.SemaphoreType.DMA((kept,))],
+        compiler_params=pltpu.CompilerParams(vmem_limit_bytes=VMEM_LIMIT),
+        cost_estimate=pl.CostEstimate(
+            flops=0, bytes_accessed=2 * kept * depth * tile, transcendentals=rows * units
+        ),
+        name="prepare",
+    )(down_quant, *parts, after)
+
+
+def down_kernel(*refs):
+    early, own, other, ds, resident, dq, out, hidden, buffers, sems = refs
     kept, _, tile = resident.shape
     tiles = out.shape[0]
     downs = Tiles(dq, buffers, sems, kept, tiles - kept)
-    downs.begin()
-    at = 0
-    for own, other in parts:
-        for i in range(own.shape[1]):
-            g = own[0, i] + other[0, i].astype(jnp.float32)
-            u = own[1, i] + other[1, i].astype(jnp.float32)
-            width = own.shape[3]
-            hidden[:, at:at + width] = ((g / (1.0 + jnp.exp(-g))) * u).astype(jnp.bfloat16)
-            at += width
+    downs.start(0)
+    units = early.shape[1]
+    hidden[:, :units] = early[...]
+    activate([(own, other)], hidden, units)
+    downs.start(1)
 
     @pl.loop(0, kept)
     def _(i):
         out[i] = tile_dot(hidden, resident.at[i], ds, i * (tile // BLOCK))
+        downs.start(i + 2)
+
+    for i in range(kept + 2, downs.slots):
+        downs.start(i)
 
     @pl.loop(0, tiles - kept)
     def _(i):
@@ -207,13 +260,13 @@
         downs.advance(i)
 
 
-def down(parts, down_scales, resident, down_quant, slots):
+def down(early, own, other, down_scales, resident, down_quant, slots):
     depth, width = down_quant.shape
     tile = resident.shape[2]
-    rows = parts[0].shape[2]
+    rows = own.shape[2]
     return pl.pallas_call(
-        functools.partial(down_kernel, len(parts) // 2),
-        in_specs=[VMEM] * len(parts) + [SMEM, VMEM, ANY],
+        down_kernel,
+        in_specs=[VMEM, VMEM, VMEM, SMEM, VMEM, ANY],
         out_specs=VMEM,
         out_shape=pltpu.VMEM((width // tile, rows, tile), jnp.float32),
         scratch_shapes=[
@@ -228,7 +281,7 @@
             flops=2 * rows * depth * width, bytes_accessed=2 * depth * width, transcendentals=0
         ),
         name="down",
-    )(*parts, down_scales, in_vmem(resident), down_quant)
+    )(early, own, other, down_scales, in_vmem(resident), down_quant)
 
 
 def gather_rows(own, n, shift, beside):
@@ -242,7 +295,7 @@
         left, right = shift(two_back[:, :half], 2), shift(two_ahead[:, half:], -2)
         blocks = [own, one_ahead, two_ahead, three_ahead, left, right, three_back, two_back, one_back]
         at = [0, 1, 2, 3, 4, 4, 5, 6, 7]
-        return blocks, [(r * rows, half if i == 5 else 0) for i, r in enumerate(at)], beside
+        return blocks, [(r * rows, half if i == 5 else 0) for i, r in enumerate(at)], beside, (two_back,)
     blocks = [own] + [None] * (n - 1)
     fw = bw = own
     for step in range(1, n // 2 + 1):
@@ -251,7 +304,7 @@
         if step <= n - 1 - n // 2:
             bw = shift(bw, -1)
             blocks[step] = bw
-    return [jnp.concatenate(blocks, axis=0)], [(0, 0)], beside
+    return [jnp.concatenate(blocks, axis=0)], [(0, 0)], beside, ()
 
 
 def scatter_sums(total, n, rows, shift):
@@ -293,22 +346,25 @@
         pltpu.with_memory_space_constraint(a, pltpu.HBM) for a in (gate_quant, up_quant, down_quant)
     )
     hidden_units, width = gate_quant.shape[1], down_quant.shape[1]
-    tile = min(hidden_units, 512)
+    tile = min(hidden_units // 2, 512)
     tiles = hidden_units // tile
-    cuts = [0, tiles // 2, tiles] if tiles > 2 else [0, tiles]
-    gate_tiles, token = stage(gate_quant, 0, tiles, tile)
-    xs, places, token = gather_rows(activations, n, shift, token)
+    cuts = [0, tiles * 3 // 4, tiles]
+    early = tiles * 3 // 4
+    gate_tiles, token = stage(gate_quant, 0, tile, tiles, 0, early)
+    xs, places, token, second = gather_rows(activations, n, shift, token)
+    if early < tiles:
+        gate_tiles, token = stage(gate_quant, early, tile, tiles, early, tiles - early, gate_tiles, (token, *second))
     parts = []
     for start, end in zip(cuts[:-1], cuts[1:]):
-        stage_next = min(2, width // tile) if end == tiles else 0
         outs = gate_up(
-            xs, places, n * rows, gate_scales, up_scales, gate_tiles, up_quant, start, end, 2, down_quant, stage_next, token
+            xs, places, n * rows, gate_scales, up_scales, gate_tiles, up_quant, start, end, 2, token
         )
         if len(xs) > 1:
             xs = [outs[2]]
         other = lax.ppermute(outs[1], "wid", [(i, widths - 1 - i) for i in range(widths)])
         parts += [outs[0], other]
-    total = down(parts, down_scales, outs[-1], down_quant, 3)
+    resident, hidden = prepare(down_quant, parts[:-2], tile, min(KEPT, width // tile), outs[0])
+    total = down(hidden, *parts[-2:], down_scales, resident, down_quant, 3)
     result = scatter_sums(total, n, rows, shift).astype(jnp.bfloat16)
     return result.transpose(1, 0, 2).reshape(rows, width)
 

time: 83.6 us -> 78.3 us (0.937)
  waiting for transfers between devices: 16 us -> 8.97 us
  Pallas kernels: 42.5 us -> 45.5 us
  local copies, waits for them, and re-layouts: 1.75 us -> 0.76 us
    pallas_call x2 -> x4, Pallas kernels: 21.1 us -> 25.7 us  [the longest x2 11.9 us: stage(): pl.pallas_call(functools.partial(stage_kernel, first, at, count), in_spec...]
    ppermute x16, waiting for transfers between devices: 13.5 us -> 8.97 us  [shift(): lax.ppermute(value, 'hid', [(order[i], order[(i + by) % n]) for i in rang...]
    ppermute x2, waiting for transfers between devices: 2.5 us -> 0.01 us  [per_device(): lax.ppermute(outs[1], 'wid', [(i, widths - 1 - i) for i in range(widths)])]
    pallas_call x2, Pallas kernels: 21.4 us -> 19.8 us  [gate_up(): pl.pallas_call(functools.partial(gate_up_kernel, first, tiles, places[:le...]
    unnamed x12 -> x8, local copies, waits for them, and re-layouts: 1 us -> 0.02 us
  transfers between devices with their start and end apart: 18 -> 18, of which waited for: 7 -> 6; matrix products, arithmetic and copies ran while one was open for 0% -> 0% of each run, Pallas kernels for 27% -> 27%
where the time goes in v3:
time: 78.3 us; the launch traced here: 78.1 us
  Pallas kernels  45.5 us (58%)
  starting transfers between devices  22.3 us (28%)
  waiting for transfers between devices  8.97 us (11%)
    ppermute x16, starting transfers between devices, shift(): lax.ppermute(value, 'hid', [(order[i], order[(i + by) % n]) for i in rang...  21.7 us
    pallas_call x2, Pallas kernels, gate_up(): pl.pallas_call(functools.partial(gate_up_kernel, first, tiles, places[:le...  19.8 us
    pallas_call x2, Pallas kernels, stage(): pl.pallas_call(functools.partial(stage_kernel, first, at, count), in_spec...  11.9 us
    pallas_call x1, Pallas kernels, down(): pl.pallas_call(down_kernel, in_specs=[VMEM, VMEM, VMEM, SMEM, VMEM, ANY],...  10.3 us
    ppermute x16, waiting for transfers between devices, shift(): lax.ppermute(value, 'hid', [(order[i], order[(i + by) % n]) for i in rang...  8.97 us
    pallas_call x1, Pallas kernels, prepare(): pl.pallas_call(functools.partial(prepare_kernel, len(parts) // 2), in_spe...  3.51 us
  transfers between devices with their start and end apart: 18, of which 6 were waited for; matrix products, arithmetic and copies ran while one was open for 0% of the time, Pallas kernels for 27%

profile of v3, /device:TPU:0, one launch (start us, length us, event | category | flops | bytes accessed | tf_op | source)
XLA Modules:
  0.0 78.1 jit_solution(1821378695800341506)
XLA Ops:
  0.0 4.0 %collective-permute-start.1 = (bf16[16,4096]{1,0:T(8,128)(2,1)}, bf16[16,4096]{1,0:T(8,128)(2,1)S(1)}, u32[]{:S(2)}, u32[]{:S(2)}) collective-permute-start(bf16[16,4096]{1,0:T(8,128)(2,1)} %refs_0_.6), channel_id=1, source_target_pairs={{0,8},{4,12},{8,14},{12,10},{14,6},{10,2},{6,0},{2,4},{1,9},{5,13}... | collective-permute-start | bytes 393224 | tf_op jit(solution)/shard_map/ppermute | solution.py:342
  4.0 0.0 collective-permute-start.2
  4.0 1.9 %collective-permute-start = (bf16[16,4096]{1,0:T(8,128)(2,1)}, bf16[16,4096]{1,0:T(8,128)(2,1)S(1)}, u32[]{:S(2)}, u32[]{:S(2)}) collective-permute-start(bf16[16,4096]{1,0:T(8,128)(2,1)} %refs_0_.6), channel_id=1, source_target_pairs={{0,2},{4,0},{8,4},{12,8},{14,12},{10,14},{6,10},{2,6},{1,3},{5,1},... | collective-permute-start | bytes 393224 | tf_op jit(solution)/shard_map/ppermute | solution.py:342
  5.9 0.2 collective-permute-start.7
  6.1 8.4 %stage.2 = (bf16[8,4096,512]{2,1,0:T(8,128)(2,1)S(1)}, bf16[16,128]{1,0:T(8,128)(2,1)S(1)}) custom-call(bf16[4096,4096]{1,0:T(8,128)(2,1)} %refs_0_.5), custom_call_target="tpu_custom_call" | custom-call | bytes 25165824 | tf_op jit(solution)/shard_map/stage/pallas_call | solution.py:108
  14.4 0.0 collective-permute-done.1.refs_3_.refs_7_
  14.5 0.0 collective-permute-done.2.refs_2_
  14.5 2.0 %collective-permute-start.6 = (bf16[16,4096]{1,0:T(8,128)(2,1)S(1)}, bf16[16,4096]{1,0:T(8,128)(2,1)S(1)}, u32[]{:S(2)}, u32[]{:S(2)}) collective-permute-start(bf16[16,4096]{1,0:T(8,128)(2,1)S(1)} %collective-permute-done.1.refs_3_.refs_7_), channel_id=1, source_target_pairs={{0,4},{4,8},{8,12},{12,14},{14,10},{10,6},{6,2},{2,0},{1,5},{5,9},... | collective-permute-start | bytes 393224 | tf_op jit(solution)/shard_map/ppermute | solution.py:342
  16.4 0.1 collective-permute-start.3
  16.6 3.0 %collective-permute-start.4 = (bf16[16,2048]{1,0:T(8,128)(2,1)S(1)}, bf16[16,2048]{1,0:T(8,128)(2,1)S(1)}, u32[]{:S(2)}, u32[]{:S(2)}) collective-permute-start(bf16[16,2048]{1,0:T(8,128)(2,1)S(1)} %slice.57), channel_id=1, source_target_pairs={{0,8},{4,12},{8,14},{12,10},{14,6},{10,2},{6,0},{2,4},{1,9},{5,13}... | collective-permute-start | bytes 196616 | tf_op jit(solution)/shard_map/ppermute | solution.py:342
  19.5 0.0 collective-permute-done.refs_1_
  19.5 0.0 collective-permute-start.5
  19.6 0.0 copy-start.2
  19.6 3.5 %stage.3 = (bf16[8,4096,512]{2,1,0:T(8,128)(2,1)S(1)}, bf16[16,128]{1,0:T(8,128)(2,1)S(1)}) custom-call(bf16[4096,4096]{1,0:T(8,128)(2,1)} %refs_0_.5, bf16[8,4096,512]{2,1,0:T(8,128)(2,1)S(1)} %get-tuple-element.22.refs_1_, bf16[16,128]{1,0:T(8,128)(2,1)S(1)} %get-tuple-element.23.refs_2_, ...), custom_call_target="tpu_custom_call", output_to_operand_aliasing={{0}: (1, {})} | custom-call | bytes 8388608 | tf_op jit(solution)/shard_map/stage/pallas_call | solution.py:108
  23.1 0.0 collective-permute-done.7.refs_8_
  23.1 0.0 collective-permute-done.4.refs_4_
  23.1 1.6 %collective-permute-done.5.refs_5_ = bf16[16,2048]{1,0:T(8,128)(2,1)S(1)} collective-permute-done((bf16[16,2048]{1,0:T(8,128)(2,1)S(1)}, bf16[16,2048]{1,0:T(8,128)(2,1)S(1)}, u32[]{:S(2)}, u32[]{:S(2)}) %collective-permute-start.5) | collective-permute-done | bytes 65568 | tf_op jit(solution)/shard_map/ppermute | solution.py:342
  24.7 0.0 collective-permute-done.6.refs_6_
  24.7 0.0 collective-permute-done.3.refs_3_
  24.7 14.1 %gate_up.2 = (f32[2,6,128,512]{3,2,1,0:T(8,128)S(1)}, bf16[2,6,128,512]{3,2,1,0:T(8,128)(2,1)}, bf16[128,4096]{1,0:T(8,128)(2,1)S(1)}) custom-call(bf16[16,4096]{1,0:T(8,128)(2,1)S(1)} %copy-done, bf16[16,4096]{1,0:T(8,128)(2,1)S(1)} %collective-permute-done.refs_1_, bf16[16,4096]{1,0:T(8,128)(2,1)S(1)} %collective-permute-done.2.refs_2_, ...), custom_call_target="tpu_custom_call" | custom-call | flops 6442450944 | bytes 50331648 | tf_op jit(solution)/shard_map/gate_up/pallas_call | solution.py:175
  38.8 0.1 collective-permute-start.8
  38.9 5.7 %gate_up.3 = (f32[2,2,128,512]{3,2,1,0:T(8,128)S(1)}, bf16[2,2,128,512]{3,2,1,0:T(8,128)(2,1)S(1)}) custom-call(bf16[128,4096]{1,0:T(8,128)(2,1)S(1)} %get-tuple-element.28.refs_0_, f32[32,32]{1,0:T(8,128)S(1)} %copy-done.1, f32[32,32]{1,0:T(8,128)S(1)} %copy-done.2, bf16[8,4096,512]{2,1,0:T(8,128)(2,1)S(1)} %get-tuple-element.24.refs_11_.refs_3_, ...), custom_call_target="tpu_custom_call" | custom-call | flops 2147483648 | bytes 16777216 | tf_op jit(solution)/shard_map/gate_up/pallas_call | solution.py:175
  44.6 0.6 collective-permute-start.9
  45.2 0.0 collective-permute-done.8.refs_2_
  45.2 3.5 %prepare.1 = (bf16[2,4096,512]{2,1,0:T(8,128)(2,1)S(1)}, bf16[128,3072]{1,0:T(8,128)(2,1)S(1)}) custom-call(bf16[4096,4096]{1,0:T(8,128)(2,1)} %refs_5_.1, f32[2,6,128,512]{3,2,1,0:T(8,128)S(1)} %get-tuple-element.26.refs_1_, bf16[2,6,128,512]{3,2,1,0:T(8,128)(2,1)S(1)} %collective-permute-done.8.refs_2_, ...), custom_call_target="tpu_custom_call" | custom-call | bytes 8388608 | tf_op jit(solution)/shard_map/prepare/pallas_call | solution.py:221
  48.7 0.0 collective-permute-done.9.refs_2_
  48.7 0.0 copy-done.3
  48.7 10.3 %down.1 = f32[8,128,512]{2,1,0:T(8,128)S(1)} custom-call(bf16[128,3072]{1,0:T(8,128)(2,1)S(1)} %get-tuple-element.30.refs_0_, f32[2,2,128,512]{3,2,1,0:T(8,128)S(1)} %get-tuple-element.29.refs_3_.refs_1_, bf16[2,2,128,512]{3,2,1,0:T(8,128)(2,1)S(1)} %collective-permute-done.9.refs_2_, f32[32,32]{1,0:T(8,128)S(1)} %copy-done.3, ...), custom_call_target="tpu_custom_call" | custom-call | flops 4294967296 | bytes 33554432 | tf_op jit(solution)/shard_map/down/pallas_call | solution.py:267
  59.0 0.1 convert.22
  59.2 1.6 %collective-permute-start.12 = (bf16[8,16,512]{2,1,0:T(8,128)(2,1)S(1)}, bf16[8,16,512]{2,1,0:T(8,128)(2,1)S(1)}, u32[]{:S(2)}, u32[]{:S(2)}) collective-permute-start(bf16[8,16,512]{2,1,0:T(8,128)(2,1)S(1)} %get-tuple-element.37), channel_id=1, source_target_pairs={{0,4},{4,8},{8,12},{12,14},{14,10},{10,6},{6,2},{2,0},{1,5},{5,9},... | collective-permute-start | bytes 393224 | tf_op jit(solution)/shard_map/ppermute | solution.py:342
  60.8 0.4 collective-permute-start.15
  61.3 2.6 %collective-permute-start.13 = (bf16[4,16,512]{2,1,0:T(8,128)(2,1)S(1)}, bf16[4,16,512]{2,1,0:T(8,128)(2,1)S(1)}, u32[]{:S(2)}, u32[]{:S(2)}) collective-permute-start(bf16[4,16,512]{2,1,0:T(8,128)(2,1)S(1)} %get-tuple-element.39), channel_id=1, source_target_pairs={{0,8},{4,12},{8,14},{12,10},{14,6},{10,2},{6,0},{2,4},{1,9},{5,13}... | collective-permute-start | bytes 196616 | tf_op jit(solution)/shard_map/ppermute | solution.py:342
  63.9 0.4 collective-permute-start.16
  64.3 1.6 %collective-permute-start.10 = (bf16[8,16,512]{2,1,0:T(8,128)(2,1)S(1)}, bf16[8,16,512]{2,1,0:T(8,128)(2,1)S(1)}, u32[]{:S(2)}, u32[]{:S(2)}) collective-permute-start(bf16[8,16,512]{2,1,0:T(8,128)(2,1)S(1)} %get-tuple-element.35), channel_id=1, source_target_pairs={{0,4},{4,8},{8,12},{12,14},{14,10},{10,6},{6,2},{2,0},{1,5},{5,9},... | collective-permute-start | bytes 393224 | tf_op jit(solution)/shard_map/ppermute | solution.py:342
  65.9 0.0 collective-permute-done.12
  65.9 0.4 collective-permute-start.11
  66.3 0.0 collective-permute-done.15
  66.3 0.1 slice_add_fusion.1
  66.4 1.2 %collective-permute-done.13 = bf16[4,16,512]{2,1,0:T(8,128)(2,1)S(1)} collective-permute-done((bf16[4,16,512]{2,1,0:T(8,128)(2,1)S(1)}, bf16[4,16,512]{2,1,0:T(8,128)(2,1)S(1)}, u32[]{:S(2)}, u32[]{:S(2)}) %collective-permute-start.13) | collective-permute-done | bytes 65568 | tf_op jit(solution)/shard_map/ppermute | solution.py:342
  67.6 2.3 %collective-permute-start.14 = (bf16[8,16,512]{2,1,0:T(8,128)(2,1)S(1)}, bf16[8,16,512]{2,1,0:T(8,128)(2,1)S(1)}, u32[]{:S(2)}, u32[]{:S(2)}) collective-permute-start(bf16[8,16,512]{2,1,0:T(8,128)(2,1)S(1)} %pad_maximum_fusion), channel_id=1, source_target_pairs={{0,8},{4,12},{8,14},{12,10},{14,6},{10,2},{6,0},{2,4},{1,9},{5,13}... | collective-permute-start | bytes 393224 | tf_op jit(solution)/shard_map/ppermute | solution.py:342
  69.9 0.2 collective-permute-done.16
  70.1 1.2 %collective-permute-start.17 = (bf16[8,16,512]{2,1,0:T(8,128)(2,1)S(1)}, bf16[8,16,512]{2,1,0:T(8,128)(2,1)S(1)}, u32[]{:S(2)}, u32[]{:S(2)}) collective-permute-start(bf16[8,16,512]{2,1,0:T(8,128)(2,1)S(1)} %pad_maximum_fusion.1), channel_id=1, source_target_pairs={{0,6},{4,2},{8,0},{12,4},{14,8},{10,12},{6,14},{2,10},{1,7},{5,3},... | collective-permute-start | bytes 393224 | tf_op jit(solution)/shard_map/ppermute | solution.py:342
  71.3 0.0 collective-permute-done.10
  71.3 1.4 %collective-permute-done.11 = bf16[8,16,512]{2,1,0:T(8,128)(2,1)S(1)} collective-permute-done((bf16[8,16,512]{2,1,0:T(8,128)(2,1)S(1)}, bf16[8,16,512]{2,1,0:T(8,128)(2,1)S(1)}, u32[]{:S(2)}, u32[]{:S(2)}) %collective-permute-start.11) | collective-permute-done | bytes 131104 | tf_op jit(solution)/shard_map/ppermute | solution.py:342
  72.7 1.8 %collective-permute-done.14 = bf16[8,16,512]{2,1,0:T(8,128)(2,1)S(1)} collective-permute-done((bf16[8,16,512]{2,1,0:T(8,128)(2,1)S(1)}, bf16[8,16,512]{2,1,0:T(8,128)(2,1)S(1)}, u32[]{:S(2)}, u32[]{:S(2)}) %collective-permute-start.14) | collective-permute-done | bytes 131104 | tf_op jit(solution)/shard_map/ppermute | solution.py:342
  74.6 2.8 %collective-permute-done.17 = bf16[8,16,512]{2,1,0:T(8,128)(2,1)S(1)} collective-permute-done((bf16[8,16,512]{2,1,0:T(8,128)(2,1)S(1)}, bf16[8,16,512]{2,1,0:T(8,128)(2,1)S(1)}, u32[]{:S(2)}, u32[]{:S(2)}) %collective-permute-start.17) | collective-permute-done | bytes 131104 | tf_op jit(solution)/shard_map/ppermute | solution.py:342
  77.3 0.1 fusion.4
  77.4 0.7 copy.10
  (16 shorter events, 0.2 us)
Async XLA Ops:
  0.0 14.4 %collective-permute-start.1 = (bf16[16,4096]{1,0:T(8,128)(2,1)}, bf16[16,4096]{1,0:T(8,128)(2,1)S(1)}, u32[]{:S(2)}, u32[]{:S(2)}) collective-permute-start(bf16[16,4096]{1,0:T(8,128)(2,1)} %refs_0_.6), channel_id=1, source_target_pairs={{0,8},{4,12},{8,14},{12,10},{14,6},{10,2},{6,0},{2,4},{1,9},{5,13}... | collective-permute-start | bytes 393224 | tf_op jit(solution)/shard_map/ppermute | solution.py:342
  4.0 10.4 %collective-permute-start.2 = (bf16[16,4096]{1,0:T(8,128)(2,1)}, bf16[16,4096]{1,0:T(8,128)(2,1)S(1)}, u32[]{:S(2)}, u32[]{:S(2)}) collective-permute-start(bf16[16,4096]{1,0:T(8,128)(2,1)} %refs_0_.6), channel_id=1, source_target_pairs={{0,6},{4,2},{8,0},{12,4},{14,8},{10,12},{6,14},{2,10},{1,7},{5,3},... | collective-permute-start | bytes 393224 | tf_op jit(solution)/shard_map/ppermute | solution.py:342
  4.0 15.5 %collective-permute-start = (bf16[16,4096]{1,0:T(8,128)(2,1)}, bf16[16,4096]{1,0:T(8,128)(2,1)S(1)}, u32[]{:S(2)}, u32[]{:S(2)}) collective-permute-start(bf16[16,4096]{1,0:T(8,128)(2,1)} %refs_0_.6), channel_id=1, source_target_pairs={{0,2},{4,0},{8,4},{12,8},{14,12},{10,14},{6,10},{2,6},{1,3},{5,1},... | collective-permute-start | bytes 393224 | tf_op jit(solution)/shard_map/ppermute | solution.py:342
  5.9 17.2 %collective-permute-start.7 = (bf16[16,4096]{1,0:T(8,128)(2,1)}, bf16[16,4096]{1,0:T(8,128)(2,1)S(1)}, u32[]{:S(2)}, u32[]{:S(2)}) collective-permute-start(bf16[16,4096]{1,0:T(8,128)(2,1)} %refs_0_.6), channel_id=1, source_target_pairs={{0,4},{4,8},{8,12},{12,14},{14,10},{10,6},{6,2},{2,0},{1,5},{5,9},... | collective-permute-start | bytes 393224 | tf_op jit(solution)/shard_map/ppermute | solution.py:342
  14.5 10.2 %collective-permute-start.6 = (bf16[16,4096]{1,0:T(8,128)(2,1)S(1)}, bf16[16,4096]{1,0:T(8,128)(2,1)S(1)}, u32[]{:S(2)}, u32[]{:S(2)}) collective-permute-start(bf16[16,4096]{1,0:T(8,128)(2,1)S(1)} %collective-permute-done.1.refs_3_.refs_7_), channel_id=1, source_target_pairs={{0,4},{4,8},{8,12},{12,14},{14,10},{10,6},{6,2},{2,0},{1,5},{5,9},... | collective-permute-start | bytes 393224 | tf_op jit(solution)/shard_map/ppermute | solution.py:342
  16.4 8.3 %collective-permute-start.3 = (bf16[16,4096]{1,0:T(8,128)(2,1)S(1)}, bf16[16,4096]{1,0:T(8,128)(2,1)S(1)}, u32[]{:S(2)}, u32[]{:S(2)}) collective-permute-start(bf16[16,4096]{1,0:T(8,128)(2,1)S(1)} %collective-permute-done.2.refs_2_), channel_id=1, source_target_pairs={{0,2},{4,0},{8,4},{12,8},{14,12},{10,14},{6,10},{2,6},{1,3},{5,1},... | collective-permute-start | bytes 393224 | tf_op jit(solution)/shard_map/ppermute | solution.py:342
  16.6 6.6 %collective-permute-start.4 = (bf16[16,2048]{1,0:T(8,128)(2,1)S(1)}, bf16[16,2048]{1,0:T(8,128)(2,1)S(1)}, u32[]{:S(2)}, u32[]{:S(2)}) collective-permute-start(bf16[16,2048]{1,0:T(8,128)(2,1)S(1)} %slice.57), channel_id=1, source_target_pairs={{0,8},{4,12},{8,14},{12,10},{14,6},{10,2},{6,0},{2,4},{1,9},{5,13}... | collective-permute-start | bytes 196616 | tf_op jit(solution)/shard_map/ppermute | solution.py:342
  19.5 5.2 %collective-permute-start.5 = (bf16[16,2048]{1,0:T(8,128)(2,1)S(1)}, bf16[16,2048]{1,0:T(8,128)(2,1)S(1)}, u32[]{:S(2)}, u32[]{:S(2)}) collective-permute-start(bf16[16,2048]{1,0:T(8,128)(2,1)S(1)} %slice.58), channel_id=1, source_target_pairs={{0,6},{4,2},{8,0},{12,4},{14,8},{10,12},{6,14},{2,10},{1,7},{5,3},... | collective-permute-start | bytes 196616 | tf_op jit(solution)/shard_map/ppermute | solution.py:342
  19.6 5.2 %copy-start = (bf16[16,4096]{1,0:T(8,128)(2,1)S(1)}, bf16[16,4096]{1,0:T(8,128)(2,1)}, u32[]{:S(2)}) copy-start(bf16[16,4096]{1,0:T(8,128)(2,1)} %refs_0_.6) | copy-start | bytes 393220
  19.6 5.2 %copy-start.1 = (f32[32,32]{1,0:T(8,128)S(1)}, f32[32,32]{1,0:T(8,128)}, u32[]{:S(2)}) copy-start(f32[32,32]{1,0:T(8,128)} %refs_1_.1) | copy-start | bytes 12292
  19.6 5.2 %copy-start.2 = (f32[32,32]{1,0:T(8,128)S(1)}, f32[32,32]{1,0:T(8,128)}, u32[]{:S(2)}) copy-start(f32[32,32]{1,0:T(8,128)} %refs_2_.1) | copy-start | bytes 12292
  38.8 6.3 %collective-permute-start.8 = (bf16[2,6,128,512]{3,2,1,0:T(8,128)(2,1)}, bf16[2,6,128,512]{3,2,1,0:T(8,128)(2,1)S(1)}, u32[]{:S(2)}, u32[]{:S(2)}) collective-permute-start(bf16[2,6,128,512]{3,2,1,0:T(8,128)(2,1)} %get-tuple-element.27), channel_id=1, source_target_pairs={{0,1},{1,0},{2,3},{3,2},{4,5},{5,4},{6,7},{7,6},{8,9},{9,8},{10,11... | collective-permute-start | bytes 4718600 | tf_op jit(solution)/shard_map/ppermute | solution.py:364
  44.6 4.1 %collective-permute-start.9 = (bf16[2,2,128,512]{3,2,1,0:T(8,128)(2,1)S(1)}, bf16[2,2,128,512]{3,2,1,0:T(8,128)(2,1)S(1)}, u32[]{:S(2)}, u32[]{:S(2)}) collective-permute-start(bf16[2,2,128,512]{3,2,1,0:T(8,128)(2,1)S(1)} %get-tuple-element.31), channel_id=1, source_target_pairs={{0,1},{1,0},{2,3},{3,2},{4,5},{5,4},{6,7},{7,6},{8,9},{9,8},{10,11... | collective-permute-start | bytes 1572872 | tf_op jit(solution)/shard_map/ppermute | solution.py:364
  45.2 3.5 %copy-start.3 = (f32[32,32]{1,0:T(8,128)S(1)}, f32[32,32]{1,0:T(8,128)}, u32[]{:S(2)}) copy-start(f32[32,32]{1,0:T(8,128)} %refs_3_.1) | copy-start | bytes 12292
  59.2 6.7 %collective-permute-start.12 = (bf16[8,16,512]{2,1,0:T(8,128)(2,1)S(1)}, bf16[8,16,512]{2,1,0:T(8,128)(2,1)S(1)}, u32[]{:S(2)}, u32[]{:S(2)}) collective-permute-start(bf16[8,16,512]{2,1,0:T(8,128)(2,1)S(1)} %get-tuple-element.37), channel_id=1, source_target_pairs={{0,4},{4,8},{8,12},{12,14},{14,10},{10,6},{6,2},{2,0},{1,5},{5,9},... | collective-permute-start | bytes 393224 | tf_op jit(solution)/shard_map/ppermute | solution.py:342
  60.8 5.5 %collective-permute-start.15 = (bf16[8,16,512]{2,1,0:T(8,128)(2,1)S(1)}, bf16[8,16,512]{2,1,0:T(8,128)(2,1)S(1)}, u32[]{:S(2)}, u32[]{:S(2)}) collective-permute-start(bf16[8,16,512]{2,1,0:T(8,128)(2,1)S(1)} %get-tuple-element.36), channel_id=1, source_target_pairs={{0,2},{4,0},{8,4},{12,8},{14,12},{10,14},{6,10},{2,6},{1,3},{5,1},... | collective-permute-start | bytes 393224 | tf_op jit(solution)/shard_map/ppermute | solution.py:342
  61.3 6.3 %collective-permute-start.13 = (bf16[4,16,512]{2,1,0:T(8,128)(2,1)S(1)}, bf16[4,16,512]{2,1,0:T(8,128)(2,1)S(1)}, u32[]{:S(2)}, u32[]{:S(2)}) collective-permute-start(bf16[4,16,512]{2,1,0:T(8,128)(2,1)S(1)} %get-tuple-element.39), channel_id=1, source_target_pairs={{0,8},{4,12},{8,14},{12,10},{14,6},{10,2},{6,0},{2,4},{1,9},{5,13}... | collective-permute-start | bytes 196616 | tf_op jit(solution)/shard_map/ppermute | solution.py:342
  63.9 6.2 %collective-permute-start.16 = (bf16[4,16,512]{2,1,0:T(8,128)(2,1)S(1)}, bf16[4,16,512]{2,1,0:T(8,128)(2,1)S(1)}, u32[]{:S(2)}, u32[]{:S(2)}) collective-permute-start(bf16[4,16,512]{2,1,0:T(8,128)(2,1)S(1)} %get-tuple-element.40), channel_id=1, source_target_pairs={{0,6},{4,2},{8,0},{12,4},{14,8},{10,12},{6,14},{2,10},{1,7},{5,3},... | collective-permute-start | bytes 196616 | tf_op jit(solution)/shard_map/ppermute | solution.py:342
  64.3 7.0 %collective-permute-start.10 = (bf16[8,16,512]{2,1,0:T(8,128)(2,1)S(1)}, bf16[8,16,512]{2,1,0:T(8,128)(2,1)S(1)}, u32[]{:S(2)}, u32[]{:S(2)}) collective-permute-start(bf16[8,16,512]{2,1,0:T(8,128)(2,1)S(1)} %get-tuple-element.35), channel_id=1, source_target_pairs={{0,4},{4,8},{8,12},{12,14},{14,10},{10,6},{6,2},{2,0},{1,5},{5,9},... | collective-permute-start | bytes 393224 | tf_op jit(solution)/shard_map/ppermute | solution.py:342
  65.9 6.9 %collective-permute-start.11 = (bf16[8,16,512]{2,1,0:T(8,128)(2,1)S(1)}, bf16[8,16,512]{2,1,0:T(8,128)(2,1)S(1)}, u32[]{:S(2)}, u32[]{:S(2)}) collective-permute-start(bf16[8,16,512]{2,1,0:T(8,128)(2,1)S(1)} %get-tuple-element.38), channel_id=1, source_target_pairs={{0,2},{4,0},{8,4},{12,8},{14,12},{10,14},{6,10},{2,6},{1,3},{5,1},... | collective-permute-start | bytes 393224 | tf_op jit(solution)/shard_map/ppermute | solution.py:342
  67.6 6.9 %collective-permute-start.14 = (bf16[8,16,512]{2,1,0:T(8,128)(2,1)S(1)}, bf16[8,16,512]{2,1,0:T(8,128)(2,1)S(1)}, u32[]{:S(2)}, u32[]{:S(2)}) collective-permute-start(bf16[8,16,512]{2,1,0:T(8,128)(2,1)S(1)} %pad_maximum_fusion), channel_id=1, source_target_pairs={{0,8},{4,12},{8,14},{12,10},{14,6},{10,2},{6,0},{2,4},{1,9},{5,13}... | collective-permute-start | bytes 393224 | tf_op jit(solution)/shard_map/ppermute | solution.py:342
  70.1 7.2 %collective-permute-start.17 = (bf16[8,16,512]{2,1,0:T(8,128)(2,1)S(1)}, bf16[8,16,512]{2,1,0:T(8,128)(2,1)S(1)}, u32[]{:S(2)}, u32[]{:S(2)}) collective-permute-start(bf16[8,16,512]{2,1,0:T(8,128)(2,1)S(1)} %pad_maximum_fusion.1), channel_id=1, source_target_pairs={{0,6},{4,2},{8,0},{12,4},{14,8},{10,12},{6,14},{2,10},{1,7},{5,3},... | collective-permute-start | bytes 393224 | tf_op jit(solution)/shard_map/ppermute | solution.py:342

commit v4 on v0

v4 whole, which is shorter than its diff:
```python
import functools

import jax
import jax.numpy as jnp
from jax import lax
from jax.experimental import pallas as pl
from jax.experimental.pallas import tpu as pltpu
from jax.sharding import PartitionSpec as P

BLOCK = 128
MIB = 1024 * 1024
VMEM = pl.BlockSpec(memory_space=pltpu.VMEM)
SMEM = pl.BlockSpec(memory_space=pltpu.SMEM)
ANY = pl.BlockSpec(memory_space=pl.ANY)


def ring_order(n):
    if n % 2:
        return list(range(n))
    return list(range(0, n, 2)) + list(range(n - 1, 0, -2))


def scaled(quant, scales_ref, k, row, col, width):
    pieces = []
    for j in range(width // BLOCK):
        block = quant[k * BLOCK:(k + 1) * BLOCK, j * BLOCK:(j + 1) * BLOCK]
        pieces.append((block.astype(jnp.float32) * scales_ref[row + k, col + j]).astype(jnp.bfloat16))
    return jnp.concatenate(pieces, axis=1) if len(pieces) > 1 else pieces[0]


def tile_dot(x_ref, quant, scales_ref, row, col):
    depth, width = quant.shape
    blocks = depth // BLOCK
    per = 2 if blocks % 2 == 0 else 1
    total = None
    for k in range(0, blocks, per):
        weight = [scaled(quant, scales_ref, k + i, row, col, width) for i in range(per)]
        weight = jnp.concatenate(weight, axis=0) if per > 1 else weight[0]
        part = jnp.dot(x_ref[:, k * BLOCK:(k + per) * BLOCK], weight, preferred_element_type=jnp.float32)
        total = part if total is None else total + part
    return total


def tile_copy(quant, i, store, slot, sem):
    depth, width = quant.shape[0], store.shape[2]
    start = i * width if isinstance(i, int) else pl.multiple_of(i * width, width)
    return pltpu.make_async_copy(quant.at[:, pl.ds(start, width)], store.at[slot, pl.ds(0, depth)], sem)


def in_vmem(array):
    return pltpu.with_memory_space_constraint(array, pltpu.VMEM)


def limit(rows, depth):
    return pltpu.CompilerParams(vmem_limit_bytes=max(13 * MIB, 6 * MIB + 4 * rows * depth))


def stage_kernel(first, count, *refs):
    quant, store, token, sems = refs[0], refs[-3], refs[-2], refs[-1]
    copies = [tile_copy(quant, first + i, store, first + i, sems.at[i]) for i in range(count)]
    for copy in copies:
        copy.start()
    token[...] = jnp.zeros_like(token)
    for copy in copies:
        copy.wait()


def stage(quant, tile, count, rows, slots):
    depth = quant.shape[0]
    return pl.pallas_call(
        functools.partial(stage_kernel, 0, count),
        in_specs=[ANY],
        out_specs=[VMEM, VMEM],
        out_shape=[pltpu.VMEM((slots, depth, tile), quant.dtype), pltpu.VMEM((16, BLOCK), jnp.bfloat16)],
        scratch_shapes=[pltpu.SemaphoreType.DMA((count,))],
        compiler_params=limit(rows, depth),
        cost_estimate=pl.CostEstimate(
            flops=0, bytes_accessed=2 * count * depth * tile, transcendentals=0
        ),
        name="stage",
    )(quant)


def gate_up_kernel(first, tiles, gate_at, spare, rest, places, downs, *refs):
    refs = list(refs)
    xs = [refs.pop(0) for _ in places]
    scales, _, uq, nq, _ = [refs.pop(0) for _ in range(5)]
    store, own, send = refs.pop(0), refs.pop(0), refs.pop(0)
    x = refs.pop(0) if len(places) > 1 else xs[0]
    sems, next_sems = refs
    tile = store.shape[2]
    blocks = scales.shape[0] // 2

    def slot_of(i):
        return jnp.where(i < 2, spare + i, i - 2)

    def up_copy(i):
        return tile_copy(uq, first + i, store, slot_of(i), sems.at[i])

    copies = [(0, tile_copy(nq, i, store, i, next_sems.at[i])) for i in range(downs)]
    for i in range(rest):
        at = tiles - rest + i
        copies.append((at, tile_copy(nq, first + tiles + i, store, at, next_sems.at[i])))
        copies.append((tiles + i, tile_copy(uq, first + tiles + i, store, spare + i, next_sems.at[rest + i])))
    if rest:
        for i in range(min(2, tiles)):
            up_copy(jnp.int32(i)).start()
    if len(places) > 1:
        for ref, (row, col) in zip(xs, places):
            x[row:row + ref.shape[0], col:col + ref.shape[1]] = ref[...]

    @pl.loop(0, 2 * tiles)
    def _(step):
        part = jnp.where(step < tiles, 0, 1)
        i = step - part * tiles
        slot = jnp.where(step < tiles, gate_at + i, slot_of(i))

        if rest:
            @pl.when(step >= tiles)
            def _():
                up_copy(i).wait()

        value = tile_dot(x, store.at[slot], scales, part * blocks, (first + i) * (tile // BLOCK))
        own[part, i] = value
        send[part, i] = value.astype(jnp.bfloat16)

        if rest:
            @pl.when(step + 2 < tiles)
            def _():
                up_copy(step + 2).start()

        for at, copy in copies:
            pl.when(step == at)(copy.start)

    for _, copy in copies:
        copy.wait()


def gate_up(xs, places, rows, scales, store, up_quant, next_quant, first, end, gate_at, spare, rest, downs, token):
    slots, depth, tile = store.shape
    tiles = end - first
    out_shape = [
        pltpu.VMEM(store.shape, store.dtype),
        pltpu.VMEM((2, tiles, rows, tile), jnp.float32),
        jax.ShapeDtypeStruct((2, tiles, rows, tile), jnp.bfloat16),
    ]
    if len(xs) > 1:
        out_shape.append(pltpu.VMEM((rows, depth), jnp.bfloat16))
    return pl.pallas_call(
        functools.partial(gate_up_kernel, first, tiles, gate_at, spare, rest, places[:len(xs)], downs),
        in_specs=[VMEM] * len(xs) + [SMEM, VMEM, ANY, ANY, ANY],
        out_specs=[VMEM] * len(out_shape),
        out_shape=out_shape,
        input_output_aliases={len(xs) + 1: 0},
        scratch_shapes=[
            pltpu.SemaphoreType.DMA((tiles,)),
            pltpu.SemaphoreType.DMA((max(downs, 2 * rest, 1),)),
        ],
        compiler_params=limit(rows, depth),
        cost_estimate=pl.CostEstimate(
            flops=4 * rows * depth * tile * tiles, bytes_accessed=4 * depth * tile * tiles, transcendentals=0
        ),
        name="gate_up",
    )(*xs, scales, in_vmem(store), up_quant, next_quant, token)


def activate(own, other, hidden, at):
    width = own.shape[3]
    for i in range(own.shape[1]):
        g = own[0, i] + other[0, i].astype(jnp.float32)
        u = own[1, i] + other[1, i].astype(jnp.float32)
        hidden[:, at:at + width] = ((g / (1.0 + jnp.exp(-g))) * u).astype(jnp.bfloat16)
        at += width


def prepare_kernel(downs, kept, dq, own, other, _, after, store, hidden, sems):
    copies = [tile_copy(dq, downs + i, store, downs + i, sems.at[i]) for i in range(kept)]
    for copy in copies:
        copy.start()
    activate(own, other, hidden, 0)
    for copy in copies:
        copy.wait()


def prepare(down_quant, own, other, store, downs, kept, after):
    rows, units = own.shape[2], own.shape[1] * own.shape[3]
    tile = store.shape[2]
    return pl.pallas_call(
        functools.partial(prepare_kernel, downs, kept),
        in_specs=[ANY, VMEM, VMEM, VMEM, ANY],
        out_specs=[VMEM, VMEM],
        out_shape=[pltpu.VMEM(store.shape, store.dtype), pltpu.VMEM((rows, units), jnp.bfloat16)],
        input_output_aliases={3: 0},
        scratch_shapes=[pltpu.SemaphoreType.DMA((kept,))],
        compiler_params=limit(rows, store.shape[1]),
        cost_estimate=pl.CostEstimate(
            flops=0, bytes_accessed=2 * kept * down_quant.shape[0] * tile, transcendentals=rows * units
        ),
        name="prepare",
    )(down_quant, own, other, in_vmem(store), after)


def down_kernel(kept, early, own, other, scales, _, dq, store, out, hidden, sems):
    slots, _, tile = store.shape
    tiles, depth = out.shape[0], dq.shape[0]

    def copy(i):
        return tile_copy(dq, i, store, lax.rem(i, slots), sems.at[lax.rem(i, slots)])

    for i in range(kept, min(kept + 2, tiles)):
        copy(jnp.int32(i)).start()
    units = early.shape[1]
    hidden[:, :units] = early[...]
    activate(own, other, hidden, units)

    @pl.loop(0, tiles)
    def _(i):
        @pl.when(i >= kept)
        def _():
            copy(i).wait()

        quant = store.at[lax.rem(i, slots), pl.ds(0, depth)]
        out[i] = tile_dot(hidden, quant, scales, 0, i * (tile // BLOCK))

        @pl.when(i + kept + 2 < tiles)
        def _():
            copy(i + kept + 2).start()


def down(early, own, other, scales, store, down_quant, kept):
    depth, width = down_quant.shape
    slots, _, tile = store.shape
    rows = own.shape[2]
    return pl.pallas_call(
        functools.partial(down_kernel, kept),
        in_specs=[VMEM, VMEM, VMEM, SMEM, VMEM, ANY],
        out_specs=[VMEM, VMEM],
        out_shape=[
            pltpu.VMEM(store.shape, store.dtype),
            pltpu.VMEM((width // tile, rows, tile), jnp.float32),
        ],
        input_output_aliases={4: 0},
        scratch_shapes=[pltpu.VMEM((rows, depth), jnp.bfloat16), pltpu.SemaphoreType.DMA((slots,))],
        compiler_params=limit(rows, store.shape[1]),
        cost_estimate=pl.CostEstimate(
            flops=2 * rows * depth * width, bytes_accessed=2 * depth * width, transcendentals=0
        ),
        name="down",
    )(early, own, other, scales, in_vmem(store), down_quant)[1]


def gather_rows(own, n, shift, beside):
    rows, width = own.shape
    if n == 8:
        half = width // 2
        two_back, two_ahead = shift(own, 2), shift(own, -2)
        one_back, one_ahead = shift(own, 1), shift(own, -1)
        two_back, two_ahead, beside = lax.optimization_barrier((two_back, two_ahead, beside))
        three_back, three_ahead = shift(two_back, 1), shift(two_ahead, -1)
        left, right = shift(two_back[:, :half], 2), shift(two_ahead[:, half:], -2)
        blocks = [own, one_ahead, two_ahead, three_ahead, left, right, three_back, two_back, one_back]
        at = [0, 1, 2, 3, 4, 4, 5, 6, 7]
        return blocks, [(r * rows, half if i == 5 else 0) for i, r in enumerate(at)], beside
    blocks = [own] + [None] * (n - 1)
    fw = bw = own
    for step in range(1, n // 2 + 1):
        fw = shift(fw, 1)
        blocks[n - step] = fw
        if step <= n - 1 - n // 2:
            bw = shift(bw, -1)
            blocks[step] = bw
    return [jnp.concatenate(blocks, axis=0)], [(0, 0)], beside


def scatter_sums(total, n, rows, shift):
    def mine(r):
        r = r % n
        return total[:, r * rows:(r + 1) * rows]

    def sent(value, by):
        return shift(value.astype(jnp.bfloat16), by).astype(jnp.float32)

    if n == 8:
        half = total.shape[0] // 2
        far_right, far_left = sent(mine(4)[half:], -2), sent(mine(4)[:half], 2)
        fifth, third = sent(mine(5), -1), sent(mine(3), 1)
        last, first = sent(mine(7), -1), sent(mine(1), 1)
        behind, ahead = mine(6) + fifth, mine(2) + third
        behind = jnp.concatenate([behind[:half], behind[half:] + far_right], axis=0)
        ahead = jnp.concatenate([ahead[:half] + far_left, ahead[half:]], axis=0)
        return mine(0) + last + first + sent(behind, -2) + sent(ahead, 2)
    ahead, behind = n // 2, n - 1 - n // 2
    fw, bw = mine(ahead), mine(-behind)
    for step in range(1, ahead + 1):
        fw = sent(fw, 1) + mine(ahead - step)
        if step <= behind:
            bw = sent(bw, -1)
            if step < behind:
                bw = bw + mine(step - behind)
    return (fw + bw) if behind else fw


def per_device(n, widths, activations, gate_quant, gate_scales, up_quant, up_scales, down_quant, down_scales):
    order = ring_order(n)

    def shift(value, by):
        return lax.ppermute(value, "hid", [(order[i], order[(i + by) % n]) for i in range(n)])

    rows = activations.shape[0]
    gate_quant, up_quant, down_quant = (
        pltpu.with_memory_space_constraint(a, pltpu.HBM) for a in (gate_quant, up_quant, down_quant)
    )
    hidden_units, width = gate_quant.shape[1], down_quant.shape[1]
    tile = min(hidden_units // 2, 512)
    tiles = hidden_units // tile
    early = tiles * 3 // 4
    rest, slots = tiles - early, early + 2
    scales = jnp.concatenate([gate_scales, up_scales], axis=0)
    store, token = stage(gate_quant, tile, early, n * rows, slots)
    xs, places, token = gather_rows(activations, n, shift, token)
    downs = min(2, early - rest)
    parts = []
    for start, end, at, more, ahead in ((0, early, 0, rest, 0), (early, tiles, early - rest, 0, downs)):
        store, own, send, *kept_x = gate_up(
            xs, places, n * rows, scales, store, up_quant, down_quant if start else gate_quant,
            start, end, at, early, more, ahead, token,
        )
        xs = kept_x or xs
        parts.append((own, lax.ppermute(send, "wid", [(i, widths - 1 - i) for i in range(widths)])))
    more = min(2, slots - 2 - downs)
    store, hidden = prepare(down_quant, *parts[0], store, downs, more, parts[1][0])
    total = down(hidden, *parts[1], down_scales, store, down_quant, downs + more)
    result = scatter_sums(total, n, rows, shift).astype(jnp.bfloat16)
    return result.transpose(1, 0, 2).reshape(rows, width)


def solution(mesh):
    return jax.shard_map(
        functools.partial(per_device, mesh.shape["hid"], mesh.shape["wid"]),
        mesh=mesh,
        in_specs=(
            P(("group", "hid"), "wid"),
            P("wid", "hid"),
            P("wid", "hid"),
            P("wid", "hid"),
            P("wid", "hid"),
            P("hid", "wid"),
            P("hid", "wid"),
        ),
        out_specs=P(("group", "hid"), "wid"),
        check_vma=False,
    )
```

time: 427 us -> 76.7 us (0.18); the launches traced: 420 us -> 76.6 us
  matrix products: 194 us -> 0 us
  waiting for transfers between devices: 142 us -> 12.1 us
  local copies, waits for them, and re-layouts: 65.2 us -> 0.77 us
  Pallas kernels: 0 us -> 40.3 us
  starting transfers between devices: 0.08 us -> 22.8 us
  between operations: 13.3 us -> 0.19 us
  other arithmetic: 5.42 us -> 0.37 us
    dot_general x3 -> x0, matrix products: 194 us -> none  [the longest x1 91.5 us: per_device(): up_part = jnp.dot(piece, up_weight, preferred_element_type=jnp.float32)]
    reduce_scatter x1 -> x0, waiting for transfers between devices: 69.1 us -> none  [per_device(): lax.psum_scatter(jnp.dot(hidden, down_weight, preferred_element_type=jnp....]
    mul x3 -> x0, local copies, waits for them, and re-layouts: 65.2 us -> none  [dequantize(): scaled = blocks * scales[:, None, :, None]]
    all_gather x1 -> x0, waiting for transfers between devices: 45.1 us -> none  [per_device(): piece = lax.all_gather(activations, 'hid', axis=0, tiled=True)]
    pallas_call x0 -> x5, Pallas kernels: none -> 40.3 us  [the longest x2 19.9 us: gate_up(): pl.pallas_call(functools.partial(gate_up_kernel, first, tiles, gate_at, s...]
    psum x1 -> x0, waiting for transfers between devices: 27.3 us -> none  [per_device(): summed = lax.psum(partial_value, 'wid')]
    ppermute x0 -> x18, starting transfers between devices: none -> 22.8 us  [the longest x16 22.2 us: shift(): lax.ppermute(value, 'hid', [(order[i], order[(i + by) % n]) for i in rang...]
    ppermute x0 -> x18, waiting for transfers between devices: none -> 12.1 us  [the longest x16 12.1 us: shift(): lax.ppermute(value, 'hid', [(order[i], order[(i + by) % n]) for i in rang...]
  transfers between devices with their start and end apart: 3 -> 18, of which waited for: 3 -> 6; matrix products, arithmetic and copies ran while one was open for 0% -> 0% of each run, Pallas kernels for 0% -> 23%
where the time goes in v4:
time: 76.7 us; the launch traced here: 76.6 us
  Pallas kernels  40.3 us (53%)
  starting transfers between devices  22.8 us (30%)
  waiting for transfers between devices  12.1 us (16%)
  local copies, waits for them, and re-layouts  0.77 us (1%)
    ppermute x16, starting transfers between devices, shift(): lax.ppermute(value, 'hid', [(order[i], order[(i + by) % n]) for i in rang...  22.2 us
    pallas_call x2, Pallas kernels, gate_up(): pl.pallas_call(functools.partial(gate_up_kernel, first, tiles, gate_at, s...  19.9 us
    ppermute x16, waiting for transfers between devices, shift(): lax.ppermute(value, 'hid', [(order[i], order[(i + by) % n]) for i in rang...  12.1 us
    pallas_call x1, Pallas kernels, down(): pl.pallas_call(functools.partial(down_kernel, kept), in_specs=[VMEM, VMEM...  8.48 us
    pallas_call x1, Pallas kernels, stage(): pl.pallas_call(functools.partial(stage_kernel, 0, count), in_specs=[ANY],...  8.37 us
    pallas_call x1, Pallas kernels, prepare(): pl.pallas_call(functools.partial(prepare_kernel, downs, kept), in_specs=[...  3.51 us
  transfers between devices with their start and end apart: 18, of which 6 were waited for; matrix products, arithmetic and copies ran while one was open for 0% of the time, Pallas kernels for 23%

profile of v4, /device:TPU:0, one launch (start us, length us, event | category | flops | bytes accessed | tf_op | source)
XLA Modules:
  0.0 76.6 jit_solution(5531002610813602140)
XLA Ops:
  0.0 4.0 %collective-permute-start.2 = (bf16[16,4096]{1,0:T(8,128)(2,1)}, bf16[16,4096]{1,0:T(8,128)(2,1)S(1)}, u32[]{:S(2)}, u32[]{:S(2)}) collective-permute-start(bf16[16,4096]{1,0:T(8,128)(2,1)} %refs_0_.3), channel_id=1, source_target_pairs={{0,6},{4,2},{8,0},{12,4},{14,8},{10,12},{6,14},{2,10},{1,7},{5,3},... | collective-permute-start | bytes 393224 | tf_op jit(solution)/shard_map/ppermute | solution.py:307
  4.0 0.1 collective-permute-start.1
  4.2 1.8 %collective-permute-start = (bf16[16,4096]{1,0:T(8,128)(2,1)}, bf16[16,4096]{1,0:T(8,128)(2,1)S(1)}, u32[]{:S(2)}, u32[]{:S(2)}) collective-permute-start(bf16[16,4096]{1,0:T(8,128)(2,1)} %refs_0_.3), channel_id=1, source_target_pairs={{0,2},{4,0},{8,4},{12,8},{14,12},{10,14},{6,10},{2,6},{1,3},{5,1},... | collective-permute-start | bytes 393224 | tf_op jit(solution)/shard_map/ppermute | solution.py:307
  6.0 0.2 collective-permute-start.7
  6.2 8.4 %stage.1 = (bf16[8,4096,512]{2,1,0:T(8,128)(2,1)S(1)}, bf16[16,128]{1,0:T(8,128)(2,1)S(1)}) custom-call(bf16[4096,4096]{1,0:T(8,128)(2,1)} %refs_12_.1), custom_call_target="tpu_custom_call" | custom-call | bytes 25165824 | tf_op jit(solution)/shard_map/stage/pallas_call | solution.py:70
  14.6 0.0 collective-permute-done.2.refs_2_
  14.6 0.0 collective-permute-done.1.refs_7_
  14.6 1.8 %collective-permute-start.3 = (bf16[16,4096]{1,0:T(8,128)(2,1)S(1)}, bf16[16,4096]{1,0:T(8,128)(2,1)S(1)}, u32[]{:S(2)}, u32[]{:S(2)}) collective-permute-start(bf16[16,4096]{1,0:T(8,128)(2,1)S(1)} %collective-permute-done.2.refs_2_), channel_id=1, source_target_pairs={{0,2},{4,0},{8,4},{12,8},{14,12},{10,14},{6,10},{2,6},{1,3},{5,1},... | collective-permute-start | bytes 393224 | tf_op jit(solution)/shard_map/ppermute | solution.py:307
  16.4 0.2 collective-permute-start.6
  16.7 0.0 copy-done.2
  16.7 2.9 %collective-permute-start.4 = (bf16[16,2048]{1,0:T(8,128)(2,1)S(1)}, bf16[16,2048]{1,0:T(8,128)(2,1)S(1)}, u32[]{:S(2)}, u32[]{:S(2)}) collective-permute-start(bf16[16,2048]{1,0:T(8,128)(2,1)S(1)} %slice.57), channel_id=1, source_target_pairs={{0,8},{4,12},{8,14},{12,10},{14,6},{10,2},{6,0},{2,4},{1,9},{5,13}... | collective-permute-start | bytes 196616 | tf_op jit(solution)/shard_map/ppermute | solution.py:307
  19.6 0.0 collective-permute-done.refs_1_
  19.6 0.1 collective-permute-start.5
  19.7 0.0 copy-done.3
  19.7 0.0 collective-permute-done.7.refs_8_
  19.7 4.0 %collective-permute-done.4.refs_4_ = bf16[16,2048]{1,0:T(8,128)(2,1)S(1)} collective-permute-done((bf16[16,2048]{1,0:T(8,128)(2,1)S(1)}, bf16[16,2048]{1,0:T(8,128)(2,1)S(1)}, u32[]{:S(2)}, u32[]{:S(2)}) %collective-permute-start.4) | collective-permute-done | bytes 65568 | tf_op jit(solution)/shard_map/ppermute | solution.py:307
  23.7 1.1 %collective-permute-done.5.refs_5_ = bf16[16,2048]{1,0:T(8,128)(2,1)S(1)} collective-permute-done((bf16[16,2048]{1,0:T(8,128)(2,1)S(1)}, bf16[16,2048]{1,0:T(8,128)(2,1)S(1)}, u32[]{:S(2)}, u32[]{:S(2)}) %collective-permute-start.5) | collective-permute-done | bytes 65568 | tf_op jit(solution)/shard_map/ppermute | solution.py:307
  24.8 0.0 collective-permute-done.3.refs_3_
  24.8 0.0 collective-permute-done.6.refs_6_
  24.8 14.6 %gate_up.2 = (bf16[8,4096,512]{2,1,0:T(8,128)(2,1)S(1)}, f32[2,6,128,512]{3,2,1,0:T(8,128)S(1)}, bf16[2,6,128,512]{3,2,1,0:T(8,128)(2,1)S(1)}, bf16[128,4096]{1,0:T(8,128)(2,1)S(1)}) custom-call(bf16[16,4096]{1,0:T(8,128)(2,1)S(1)} %copy-done, bf16[16,4096]{1,0:T(8,128)(2,1)S(1)} %collective-permute-done.refs_1_, ...), custom_call_target="tpu_custom_call", output_to_operand_aliasing={{0}: (10, {})} | custom-call | flops 6442450944 | bytes 50331648 | tf_op jit(solution)/shard_map/gate_up/pallas_call | solution.py:149
  39.4 0.1 collective-permute-start.8
  39.4 5.4 %gate_up.3 = (bf16[8,4096,512]{2,1,0:T(8,128)(2,1)S(1)}, f32[2,2,128,512]{3,2,1,0:T(8,128)S(1)}, bf16[2,2,128,512]{3,2,1,0:T(8,128)(2,1)S(1)}) custom-call(bf16[128,4096]{1,0:T(8,128)(2,1)S(1)} %get-tuple-element.27.refs_0_, f32[64,32]{1,0:T(8,128)S(1)} %constant_dynamic-update-slice_fusion.refs_9_.refs_1_, ...), custom_call_target="tpu_custom_call", output_to_operand_aliasing={{0}: (2, {})} | custom-call | flops 2147483648 | bytes 16777216 | tf_op jit(solution)/shard_map/gate_up/pallas_call | solution.py:149
  44.8 0.6 collective-permute-start.9
  45.4 0.0 collective-permute-done.8.other
  45.4 3.5 %prepare.1 = (bf16[8,4096,512]{2,1,0:T(8,128)(2,1)S(1)}, bf16[128,3072]{1,0:T(8,128)(2,1)S(1)}) custom-call(bf16[4096,4096]{1,0:T(8,128)(2,1)} %dq.3, f32[2,6,128,512]{3,2,1,0:T(8,128)S(1)} %get-tuple-element.25.own, bf16[2,6,128,512]{3,2,1,0:T(8,128)(2,1)S(1)} %collective-permute-done.8.other, ...), custom_call_target="tpu_custom_call", output_to_operand_aliasing={{0}: (3, {})} | custom-call | bytes 8388608 | tf_op jit(solution)/shard_map/prepare/pallas_call | solution.py:188
  48.9 0.0 collective-permute-done.9.other
  48.9 0.0 copy-done.1
  48.9 8.5 %down.1 = (bf16[8,4096,512]{2,1,0:T(8,128)(2,1)S(1)}, f32[8,128,512]{2,1,0:T(8,128)S(1)}) custom-call(bf16[128,3072]{1,0:T(8,128)(2,1)S(1)} %get-tuple-element.31.early, f32[2,2,128,512]{3,2,1,0:T(8,128)S(1)} %get-tuple-element.30.after.own, bf16[2,2,128,512]{3,2,1,0:T(8,128)(2,1)S(1)} %collective-permute-done.9.other, ...), custom_call_target="tpu_custom_call", output_to_operand_aliasing={{0}: (4, {})} | custom-call | flops 4294967296 | bytes 33554432 | tf_op jit(solution)/shard_map/down/pallas_call | solution.py:234
  57.4 0.1 convert.22
  57.6 1.6 %collective-permute-start.15 = (bf16[8,16,512]{2,1,0:T(8,128)(2,1)S(1)}, bf16[8,16,512]{2,1,0:T(8,128)(2,1)S(1)}, u32[]{:S(2)}, u32[]{:S(2)}) collective-permute-start(bf16[8,16,512]{2,1,0:T(8,128)(2,1)S(1)} %get-tuple-element.38), channel_id=1, source_target_pairs={{0,4},{4,8},{8,12},{12,14},{14,10},{10,6},{6,2},{2,0},{1,5},{5,9},... | collective-permute-start | bytes 393224 | tf_op jit(solution)/shard_map/ppermute | solution.py:307
  59.2 0.5 collective-permute-start.12
  59.7 1.6 %collective-permute-start.13 = (bf16[4,16,512]{2,1,0:T(8,128)(2,1)S(1)}, bf16[4,16,512]{2,1,0:T(8,128)(2,1)S(1)}, u32[]{:S(2)}, u32[]{:S(2)}) collective-permute-start(bf16[4,16,512]{2,1,0:T(8,128)(2,1)S(1)} %get-tuple-element.41), channel_id=1, source_target_pairs={{0,6},{4,2},{8,0},{12,4},{14,8},{10,12},{6,14},{2,10},{1,7},{5,3},... | collective-permute-start | bytes 196616 | tf_op jit(solution)/shard_map/ppermute | solution.py:307
  61.3 1.4 %collective-permute-start.16 = (bf16[4,16,512]{2,1,0:T(8,128)(2,1)S(1)}, bf16[4,16,512]{2,1,0:T(8,128)(2,1)S(1)}, u32[]{:S(2)}, u32[]{:S(2)}) collective-permute-start(bf16[4,16,512]{2,1,0:T(8,128)(2,1)S(1)} %get-tuple-element.42), channel_id=1, source_target_pairs={{0,8},{4,12},{8,14},{12,10},{14,6},{10,2},{6,0},{2,4},{1,9},{5,13}... | collective-permute-start | bytes 196616 | tf_op jit(solution)/shard_map/ppermute | solution.py:307
  62.7 0.5 collective-permute-start.10
  63.2 0.0 collective-permute-done.15
  63.2 2.4 %collective-permute-start.11 = (bf16[8,16,512]{2,1,0:T(8,128)(2,1)S(1)}, bf16[8,16,512]{2,1,0:T(8,128)(2,1)S(1)}, u32[]{:S(2)}, u32[]{:S(2)}) collective-permute-start(bf16[8,16,512]{2,1,0:T(8,128)(2,1)S(1)} %get-tuple-element.40), channel_id=1, source_target_pairs={{0,4},{4,8},{8,12},{12,14},{14,10},{10,6},{6,2},{2,0},{1,5},{5,9},... | collective-permute-start | bytes 393224 | tf_op jit(solution)/shard_map/ppermute | solution.py:307
  65.6 0.7 collective-permute-done.12
  66.3 0.1 convert_add_fusion.1
  66.4 1.4 %collective-permute-done.16 = bf16[4,16,512]{2,1,0:T(8,128)(2,1)S(1)} collective-permute-done((bf16[4,16,512]{2,1,0:T(8,128)(2,1)S(1)}, bf16[4,16,512]{2,1,0:T(8,128)(2,1)S(1)}, u32[]{:S(2)}, u32[]{:S(2)}) %collective-permute-start.16) | collective-permute-done | bytes 65568 | tf_op jit(solution)/shard_map/ppermute | solution.py:307
  67.9 1.5 %collective-permute-start.17 = (bf16[8,16,512]{2,1,0:T(8,128)(2,1)S(1)}, bf16[8,16,512]{2,1,0:T(8,128)(2,1)S(1)}, u32[]{:S(2)}, u32[]{:S(2)}) collective-permute-start(bf16[8,16,512]{2,1,0:T(8,128)(2,1)S(1)} %pad_maximum_fusion.1), channel_id=1, source_target_pairs={{0,8},{4,12},{8,14},{12,10},{14,6},{10,2},{6,0},{2,4},{1,9},{5,13}... | collective-permute-start | bytes 393224 | tf_op jit(solution)/shard_map/ppermute | solution.py:307
  69.4 0.0 collective-permute-done.13
  69.4 1.5 %collective-permute-start.14 = (bf16[8,16,512]{2,1,0:T(8,128)(2,1)S(1)}, bf16[8,16,512]{2,1,0:T(8,128)(2,1)S(1)}, u32[]{:S(2)}, u32[]{:S(2)}) collective-permute-start(bf16[8,16,512]{2,1,0:T(8,128)(2,1)S(1)} %pad_maximum_fusion), channel_id=1, source_target_pairs={{0,6},{4,2},{8,0},{12,4},{14,8},{10,12},{6,14},{2,10},{1,7},{5,3},... | collective-permute-start | bytes 393224 | tf_op jit(solution)/shard_map/ppermute | solution.py:307
  71.0 0.0 collective-permute-done.10
  71.0 0.0 collective-permute-done.11
  71.0 3.9 %collective-permute-done.17 = bf16[8,16,512]{2,1,0:T(8,128)(2,1)S(1)} collective-permute-done((bf16[8,16,512]{2,1,0:T(8,128)(2,1)S(1)}, bf16[8,16,512]{2,1,0:T(8,128)(2,1)S(1)}, u32[]{:S(2)}, u32[]{:S(2)}) %collective-permute-start.17) | collective-permute-done | bytes 131104 | tf_op jit(solution)/shard_map/ppermute | solution.py:307
  74.9 0.9 %collective-permute-done.14 = bf16[8,16,512]{2,1,0:T(8,128)(2,1)S(1)} collective-permute-done((bf16[8,16,512]{2,1,0:T(8,128)(2,1)S(1)}, bf16[8,16,512]{2,1,0:T(8,128)(2,1)S(1)}, u32[]{:S(2)}, u32[]{:S(2)}) %collective-permute-start.14) | collective-permute-done | bytes 131104 | tf_op jit(solution)/shard_map/ppermute | solution.py:307
  75.8 0.1 fusion
  75.9 0.7 copy.13
  (17 shorter events, 0.2 us)
Async XLA Ops:
  0.0 24.8 %copy-start = (bf16[16,4096]{1,0:T(8,128)(2,1)S(1)}, bf16[16,4096]{1,0:T(8,128)(2,1)}, u32[]{:S(2)}) copy-start(bf16[16,4096]{1,0:T(8,128)(2,1)} %refs_0_.3) | copy-start | bytes 393220
  0.0 16.7 %copy-start.2 = (f32[32,32]{1,0:T(8,128)S(1)}, f32[32,32]{1,0:T(8,128)}, u32[]{:S(2)}) copy-start(f32[32,32]{1,0:T(8,128)} %param.9) | copy-start | bytes 12292
  0.0 19.7 %copy-start.3 = (f32[32,32]{1,0:T(8,128)S(1)}, f32[32,32]{1,0:T(8,128)}, u32[]{:S(2)}) copy-start(f32[32,32]{1,0:T(8,128)} %param.11) | copy-start | bytes 12292
  0.0 14.6 %collective-permute-start.2 = (bf16[16,4096]{1,0:T(8,128)(2,1)}, bf16[16,4096]{1,0:T(8,128)(2,1)S(1)}, u32[]{:S(2)}, u32[]{:S(2)}) collective-permute-start(bf16[16,4096]{1,0:T(8,128)(2,1)} %refs_0_.3), channel_id=1, source_target_pairs={{0,6},{4,2},{8,0},{12,4},{14,8},{10,12},{6,14},{2,10},{1,7},{5,3},... | collective-permute-start | bytes 393224 | tf_op jit(solution)/shard_map/ppermute | solution.py:307
  4.0 10.5 %collective-permute-start.1 = (bf16[16,4096]{1,0:T(8,128)(2,1)}, bf16[16,4096]{1,0:T(8,128)(2,1)S(1)}, u32[]{:S(2)}, u32[]{:S(2)}) collective-permute-start(bf16[16,4096]{1,0:T(8,128)(2,1)} %refs_0_.3), channel_id=1, source_target_pairs={{0,8},{4,12},{8,14},{12,10},{14,6},{10,2},{6,0},{2,4},{1,9},{5,13}... | collective-permute-start | bytes 393224 | tf_op jit(solution)/shard_map/ppermute | solution.py:307
  4.2 15.5 %collective-permute-start = (bf16[16,4096]{1,0:T(8,128)(2,1)}, bf16[16,4096]{1,0:T(8,128)(2,1)S(1)}, u32[]{:S(2)}, u32[]{:S(2)}) collective-permute-start(bf16[16,4096]{1,0:T(8,128)(2,1)} %refs_0_.3), channel_id=1, source_target_pairs={{0,2},{4,0},{8,4},{12,8},{14,12},{10,14},{6,10},{2,6},{1,3},{5,1},... | collective-permute-start | bytes 393224 | tf_op jit(solution)/shard_map/ppermute | solution.py:307
  6.0 13.7 %collective-permute-start.7 = (bf16[16,4096]{1,0:T(8,128)(2,1)}, bf16[16,4096]{1,0:T(8,128)(2,1)S(1)}, u32[]{:S(2)}, u32[]{:S(2)}) collective-permute-start(bf16[16,4096]{1,0:T(8,128)(2,1)} %refs_0_.3), channel_id=1, source_target_pairs={{0,4},{4,8},{8,12},{12,14},{14,10},{10,6},{6,2},{2,0},{1,5},{5,9},... | collective-permute-start | bytes 393224 | tf_op jit(solution)/shard_map/ppermute | solution.py:307
  14.6 10.2 %collective-permute-start.3 = (bf16[16,4096]{1,0:T(8,128)(2,1)S(1)}, bf16[16,4096]{1,0:T(8,128)(2,1)S(1)}, u32[]{:S(2)}, u32[]{:S(2)}) collective-permute-start(bf16[16,4096]{1,0:T(8,128)(2,1)S(1)} %collective-permute-done.2.refs_2_), channel_id=1, source_target_pairs={{0,2},{4,0},{8,4},{12,8},{14,12},{10,14},{6,10},{2,6},{1,3},{5,1},... | collective-permute-start | bytes 393224 | tf_op jit(solution)/shard_map/ppermute | solution.py:307
  16.4 8.4 %collective-permute-start.6 = (bf16[16,4096]{1,0:T(8,128)(2,1)S(1)}, bf16[16,4096]{1,0:T(8,128)(2,1)S(1)}, u32[]{:S(2)}, u32[]{:S(2)}) collective-permute-start(bf16[16,4096]{1,0:T(8,128)(2,1)S(1)} %collective-permute-done.1.refs_7_), channel_id=1, source_target_pairs={{0,4},{4,8},{8,12},{12,14},{14,10},{10,6},{6,2},{2,0},{1,5},{5,9},... | collective-permute-start | bytes 393224 | tf_op jit(solution)/shard_map/ppermute | solution.py:307
  16.7 7.0 %collective-permute-start.4 = (bf16[16,2048]{1,0:T(8,128)(2,1)S(1)}, bf16[16,2048]{1,0:T(8,128)(2,1)S(1)}, u32[]{:S(2)}, u32[]{:S(2)}) collective-permute-start(bf16[16,2048]{1,0:T(8,128)(2,1)S(1)} %slice.57), channel_id=1, source_target_pairs={{0,8},{4,12},{8,14},{12,10},{14,6},{10,2},{6,0},{2,4},{1,9},{5,13}... | collective-permute-start | bytes 196616 | tf_op jit(solution)/shard_map/ppermute | solution.py:307
  19.6 5.2 %collective-permute-start.5 = (bf16[16,2048]{1,0:T(8,128)(2,1)S(1)}, bf16[16,2048]{1,0:T(8,128)(2,1)S(1)}, u32[]{:S(2)}, u32[]{:S(2)}) collective-permute-start(bf16[16,2048]{1,0:T(8,128)(2,1)S(1)} %slice.58), channel_id=1, source_target_pairs={{0,6},{4,2},{8,0},{12,4},{14,8},{10,12},{6,14},{2,10},{1,7},{5,3},... | collective-permute-start | bytes 196616 | tf_op jit(solution)/shard_map/ppermute | solution.py:307
  39.4 6.0 %collective-permute-start.8 = (bf16[2,6,128,512]{3,2,1,0:T(8,128)(2,1)S(1)}, bf16[2,6,128,512]{3,2,1,0:T(8,128)(2,1)S(1)}, u32[]{:S(2)}, u32[]{:S(2)}) collective-permute-start(bf16[2,6,128,512]{3,2,1,0:T(8,128)(2,1)S(1)} %get-tuple-element.26), channel_id=1, source_target_pairs={{0,1},{1,0},{2,3},{3,2},{4,5},{5,4},{6,7},{7,6},{8,9},{9,8},{10,11... | collective-permute-start | bytes 4718600 | tf_op jit(solution)/shard_map/ppermute | solution.py:329
  44.8 4.1 %collective-permute-start.9 = (bf16[2,2,128,512]{3,2,1,0:T(8,128)(2,1)S(1)}, bf16[2,2,128,512]{3,2,1,0:T(8,128)(2,1)S(1)}, u32[]{:S(2)}, u32[]{:S(2)}) collective-permute-start(bf16[2,2,128,512]{3,2,1,0:T(8,128)(2,1)S(1)} %get-tuple-element.32), channel_id=1, source_target_pairs={{0,1},{1,0},{2,3},{3,2},{4,5},{5,4},{6,7},{7,6},{8,9},{9,8},{10,11... | collective-permute-start | bytes 1572872 | tf_op jit(solution)/shard_map/ppermute | solution.py:329
  45.4 3.5 %copy-start.1 = (f32[32,32]{1,0:T(8,128)S(1)}, f32[32,32]{1,0:T(8,128)}, u32[]{:S(2)}) copy-start(f32[32,32]{1,0:T(8,128)} %scales.1) | copy-start | bytes 12292
  57.6 5.6 %collective-permute-start.15 = (bf16[8,16,512]{2,1,0:T(8,128)(2,1)S(1)}, bf16[8,16,512]{2,1,0:T(8,128)(2,1)S(1)}, u32[]{:S(2)}, u32[]{:S(2)}) collective-permute-start(bf16[8,16,512]{2,1,0:T(8,128)(2,1)S(1)} %get-tuple-element.38), channel_id=1, source_target_pairs={{0,4},{4,8},{8,12},{12,14},{14,10},{10,6},{6,2},{2,0},{1,5},{5,9},... | collective-permute-start | bytes 393224 | tf_op jit(solution)/shard_map/ppermute | solution.py:307
  59.2 7.1 %collective-permute-start.12 = (bf16[8,16,512]{2,1,0:T(8,128)(2,1)S(1)}, bf16[8,16,512]{2,1,0:T(8,128)(2,1)S(1)}, u32[]{:S(2)}, u32[]{:S(2)}) collective-permute-start(bf16[8,16,512]{2,1,0:T(8,128)(2,1)S(1)} %get-tuple-element.39), channel_id=1, source_target_pairs={{0,2},{4,0},{8,4},{12,8},{14,12},{10,14},{6,10},{2,6},{1,3},{5,1},... | collective-permute-start | bytes 393224 | tf_op jit(solution)/shard_map/ppermute | solution.py:307
  59.7 9.7 %collective-permute-start.13 = (bf16[4,16,512]{2,1,0:T(8,128)(2,1)S(1)}, bf16[4,16,512]{2,1,0:T(8,128)(2,1)S(1)}, u32[]{:S(2)}, u32[]{:S(2)}) collective-permute-start(bf16[4,16,512]{2,1,0:T(8,128)(2,1)S(1)} %get-tuple-element.41), channel_id=1, source_target_pairs={{0,6},{4,2},{8,0},{12,4},{14,8},{10,12},{6,14},{2,10},{1,7},{5,3},... | collective-permute-start | bytes 196616 | tf_op jit(solution)/shard_map/ppermute | solution.py:307
  61.3 6.6 %collective-permute-start.16 = (bf16[4,16,512]{2,1,0:T(8,128)(2,1)S(1)}, bf16[4,16,512]{2,1,0:T(8,128)(2,1)S(1)}, u32[]{:S(2)}, u32[]{:S(2)}) collective-permute-start(bf16[4,16,512]{2,1,0:T(8,128)(2,1)S(1)} %get-tuple-element.42), channel_id=1, source_target_pairs={{0,8},{4,12},{8,14},{12,10},{14,6},{10,2},{6,0},{2,4},{1,9},{5,13}... | collective-permute-start | bytes 196616 | tf_op jit(solution)/shard_map/ppermute | solution.py:307
  62.7 8.3 %collective-permute-start.10 = (bf16[8,16,512]{2,1,0:T(8,128)(2,1)S(1)}, bf16[8,16,512]{2,1,0:T(8,128)(2,1)S(1)}, u32[]{:S(2)}, u32[]{:S(2)}) collective-permute-start(bf16[8,16,512]{2,1,0:T(8,128)(2,1)S(1)} %get-tuple-element.37), channel_id=1, source_target_pairs={{0,2},{4,0},{8,4},{12,8},{14,12},{10,14},{6,10},{2,6},{1,3},{5,1},... | collective-permute-start | bytes 393224 | tf_op jit(solution)/shard_map/ppermute | solution.py:307
  63.2 7.8 %collective-permute-start.11 = (bf16[8,16,512]{2,1,0:T(8,128)(2,1)S(1)}, bf16[8,16,512]{2,1,0:T(8,128)(2,1)S(1)}, u32[]{:S(2)}, u32[]{:S(2)}) collective-permute-start(bf16[8,16,512]{2,1,0:T(8,128)(2,1)S(1)} %get-tuple-element.40), channel_id=1, source_target_pairs={{0,4},{4,8},{8,12},{12,14},{14,10},{10,6},{6,2},{2,0},{1,5},{5,9},... | collective-permute-start | bytes 393224 | tf_op jit(solution)/shard_map/ppermute | solution.py:307
  67.9 7.0 %collective-permute-start.17 = (bf16[8,16,512]{2,1,0:T(8,128)(2,1)S(1)}, bf16[8,16,512]{2,1,0:T(8,128)(2,1)S(1)}, u32[]{:S(2)}, u32[]{:S(2)}) collective-permute-start(bf16[8,16,512]{2,1,0:T(8,128)(2,1)S(1)} %pad_maximum_fusion.1), channel_id=1, source_target_pairs={{0,8},{4,12},{8,14},{12,10},{14,6},{10,2},{6,0},{2,4},{1,9},{5,13}... | collective-permute-start | bytes 393224 | tf_op jit(solution)/shard_map/ppermute | solution.py:307
  69.4 6.4 %collective-permute-start.14 = (bf16[8,16,512]{2,1,0:T(8,128)(2,1)S(1)}, bf16[8,16,512]{2,1,0:T(8,128)(2,1)S(1)}, u32[]{:S(2)}, u32[]{:S(2)}) collective-permute-start(bf16[8,16,512]{2,1,0:T(8,128)(2,1)S(1)} %pad_maximum_fusion), channel_id=1, source_target_pairs={{0,6},{4,2},{8,0},{12,4},{14,8},{10,12},{6,14},{2,10},{1,7},{5,3},... | collective-permute-start | bytes 393224 | tf_op jit(solution)/shard_map/ppermute | solution.py:307

commit v5 on v4

--- a/solution.py
+++ b/solution.py
@@ -55,9 +55,9 @@
     return pltpu.CompilerParams(vmem_limit_bytes=max(13 * MIB, 6 * MIB + 4 * rows * depth))
 
 
-def stage_kernel(first, count, *refs):
+def stage_kernel(count, slot, *refs):
     quant, store, token, sems = refs[0], refs[-3], refs[-2], refs[-1]
-    copies = [tile_copy(quant, first + i, store, first + i, sems.at[i]) for i in range(count)]
+    copies = [tile_copy(quant, i, store, slot + i, sems.at[i]) for i in range(count)]
     for copy in copies:
         copy.start()
     token[...] = jnp.zeros_like(token)
@@ -65,20 +65,23 @@
         copy.wait()
 
 
-def stage(quant, tile, count, rows, slots):
+def stage(quant, tile, count, rows, slot, shape=None, store=None, after=()):
     depth = quant.shape[0]
+    more = list(after) if store is None else [in_vmem(store), *after]
+    shape = shape or store.shape
     return pl.pallas_call(
-        functools.partial(stage_kernel, 0, count),
-        in_specs=[ANY],
+        functools.partial(stage_kernel, count, slot),
+        in_specs=[ANY] + ([] if store is None else [VMEM]) + [ANY] * len(after),
         out_specs=[VMEM, VMEM],
-        out_shape=[pltpu.VMEM((slots, depth, tile), quant.dtype), pltpu.VMEM((16, BLOCK), jnp.bfloat16)],
+        out_shape=[pltpu.VMEM(shape, quant.dtype), pltpu.VMEM((16, BLOCK), jnp.bfloat16)],
+        input_output_aliases={} if store is None else {1: 0},
         scratch_shapes=[pltpu.SemaphoreType.DMA((count,))],
         compiler_params=limit(rows, depth),
         cost_estimate=pl.CostEstimate(
             flops=0, bytes_accessed=2 * count * depth * tile, transcendentals=0
         ),
         name="stage",
-    )(quant)
+    )(quant, *more)
 
 
 def gate_up_kernel(first, tiles, gate_at, spare, rest, places, downs, *refs):
@@ -102,9 +105,6 @@
         at = tiles - rest + i
         copies.append((at, tile_copy(nq, first + tiles + i, store, at, next_sems.at[i])))
         copies.append((tiles + i, tile_copy(uq, first + tiles + i, store, spare + i, next_sems.at[rest + i])))
-    if rest:
-        for i in range(min(2, tiles)):
-            up_copy(jnp.int32(i)).start()
     if len(places) > 1:
         for ref, (row, col) in zip(xs, places):
             x[row:row + ref.shape[0], col:col + ref.shape[1]] = ref[...]
@@ -116,7 +116,7 @@
         slot = jnp.where(step < tiles, gate_at + i, slot_of(i))
 
         if rest:
-            @pl.when(step >= tiles)
+            @pl.when(step >= tiles + 2)
             def _():
                 up_copy(i).wait()
 
@@ -260,7 +260,7 @@
         left, right = shift(two_back[:, :half], 2), shift(two_ahead[:, half:], -2)
         blocks = [own, one_ahead, two_ahead, three_ahead, left, right, three_back, two_back, one_back]
         at = [0, 1, 2, 3, 4, 4, 5, 6, 7]
-        return blocks, [(r * rows, half if i == 5 else 0) for i, r in enumerate(at)], beside
+        return blocks, [(r * rows, half if i == 5 else 0) for i, r in enumerate(at)], beside, (two_back,)
     blocks = [own] + [None] * (n - 1)
     fw = bw = own
     for step in range(1, n // 2 + 1):
@@ -269,7 +269,7 @@
         if step <= n - 1 - n // 2:
             bw = shift(bw, -1)
             blocks[step] = bw
-    return [jnp.concatenate(blocks, axis=0)], [(0, 0)], beside
+    return [jnp.concatenate(blocks, axis=0)], [(0, 0)], beside, ()
 
 
 def scatter_sums(total, n, rows, shift):
@@ -316,8 +316,9 @@
     early = tiles * 3 // 4
     rest, slots = tiles - early, early + 2
     scales = jnp.concatenate([gate_scales, up_scales], axis=0)
-    store, token = stage(gate_quant, tile, early, n * rows, slots)
-    xs, places, token = gather_rows(activations, n, shift, token)
+    store, token = stage(gate_quant, tile, early, n * rows, 0, (slots, gate_quant.shape[0], tile))
+    xs, places, token, second = gather_rows(activations, n, shift, token)
+    store, token = stage(up_quant, tile, min(2, early), n * rows, early, store=store, after=(token, *second))
     downs = min(2, early - rest)
     parts = []
     for start, end, at, more, ahead in ((0, early, 0, rest, 0), (early, tiles, early - rest, 0, downs)):

time: 76.7 us -> 75.1 us (0.979)
  waiting for transfers between devices: 12.1 us -> 8.59 us
  Pallas kernels: 40.3 us -> 42.2 us
    ppermute x16, waiting for transfers between devices: 12.1 us -> 8.59 us  [shift(): lax.ppermute(value, 'hid', [(order[i], order[(i + by) % n]) for i in rang...]
    pallas_call x1 -> x2, Pallas kernels: 8.37 us -> 11.9 us  [stage(): pl.pallas_call(functools.partial(stage_kernel, count, slot), in_specs=[AN...]
    pallas_call x2, Pallas kernels: 19.9 us -> 18.4 us  [gate_up(): pl.pallas_call(functools.partial(gate_up_kernel, first, tiles, gate_at, s...]
  transfers between devices with their start and end apart: 18 -> 18, of which waited for: 6 -> 6; matrix products, arithmetic and copies ran while one was open for 0% -> 0% of each run, Pallas kernels for 23% -> 28%
where the time goes in v5:
time: 75.1 us; the launch traced here: 75 us
  Pallas kernels  42.2 us (56%)
  starting transfers between devices  22.8 us (30%)
  waiting for transfers between devices  8.59 us (11%)
  local copies, waits for them, and re-layouts  0.77 us (1%)
    ppermute x16, starting transfers between devices, shift(): lax.ppermute(value, 'hid', [(order[i], order[(i + by) % n]) for i in rang...  22.2 us
    pallas_call x2, Pallas kernels, gate_up(): pl.pallas_call(functools.partial(gate_up_kernel, first, tiles, gate_at, s...  18.4 us
    pallas_call x2, Pallas kernels, stage(): pl.pallas_call(functools.partial(stage_kernel, count, slot), in_specs=[AN...  11.9 us
    ppermute x16, waiting for transfers between devices, shift(): lax.ppermute(value, 'hid', [(order[i], order[(i + by) % n]) for i in rang...  8.59 us
    pallas_call x1, Pallas kernels, down(): pl.pallas_call(functools.partial(down_kernel, kept), in_specs=[VMEM, VMEM...  8.48 us
    pallas_call x1, Pallas kernels, prepare(): pl.pallas_call(functools.partial(prepare_kernel, downs, kept), in_specs=[...  3.51 us
  transfers between devices with their start and end apart: 18, of which 6 were waited for; matrix products, arithmetic and copies ran while one was open for 0% of the time, Pallas kernels for 28%

profile of v5, /device:TPU:0, one launch (start us, length us, event | category | flops | bytes accessed | tf_op | source)
XLA Modules:
  0.0 75.0 jit_solution(11323927456594130355)
XLA Ops:
  0.0 4.0 %collective-permute-start.2 = (bf16[16,4096]{1,0:T(8,128)(2,1)}, bf16[16,4096]{1,0:T(8,128)(2,1)S(1)}, u32[]{:S(2)}, u32[]{:S(2)}) collective-permute-start(bf16[16,4096]{1,0:T(8,128)(2,1)} %refs_0_.5), channel_id=1, source_target_pairs={{0,6},{4,2},{8,0},{12,4},{14,8},{10,12},{6,14},{2,10},{1,7},{5,3},... | collective-permute-start | bytes 393224 | tf_op jit(solution)/shard_map/ppermute | solution.py:307
  4.0 0.1 collective-permute-start.1
  4.1 1.8 %collective-permute-start = (bf16[16,4096]{1,0:T(8,128)(2,1)}, bf16[16,4096]{1,0:T(8,128)(2,1)S(1)}, u32[]{:S(2)}, u32[]{:S(2)}) collective-permute-start(bf16[16,4096]{1,0:T(8,128)(2,1)} %refs_0_.5), channel_id=1, source_target_pairs={{0,2},{4,0},{8,4},{12,8},{14,12},{10,14},{6,10},{2,6},{1,3},{5,1},... | collective-permute-start | bytes 393224 | tf_op jit(solution)/shard_map/ppermute | solution.py:307
  5.9 0.2 collective-permute-start.7
  6.1 8.4 %stage.2 = (bf16[8,4096,512]{2,1,0:T(8,128)(2,1)S(1)}, bf16[16,128]{1,0:T(8,128)(2,1)S(1)}) custom-call(bf16[4096,4096]{1,0:T(8,128)(2,1)} %refs_12_.1), custom_call_target="tpu_custom_call" | custom-call | bytes 25165824 | tf_op jit(solution)/shard_map/stage/pallas_call | solution.py:72
  14.5 0.0 collective-permute-done.2.refs_2_
  14.5 0.0 collective-permute-done.1.refs_3_.refs_7_
  14.5 1.8 %collective-permute-start.3 = (bf16[16,4096]{1,0:T(8,128)(2,1)S(1)}, bf16[16,4096]{1,0:T(8,128)(2,1)S(1)}, u32[]{:S(2)}, u32[]{:S(2)}) collective-permute-start(bf16[16,4096]{1,0:T(8,128)(2,1)S(1)} %collective-permute-done.2.refs_2_), channel_id=1, source_target_pairs={{0,2},{4,0},{8,4},{12,8},{14,12},{10,14},{6,10},{2,6},{1,3},{5,1},... | collective-permute-start | bytes 393224 | tf_op jit(solution)/shard_map/ppermute | solution.py:307
  16.4 0.2 collective-permute-start.6
  16.6 0.0 copy-done.2
  16.6 2.9 %collective-permute-start.4 = (bf16[16,2048]{1,0:T(8,128)(2,1)S(1)}, bf16[16,2048]{1,0:T(8,128)(2,1)S(1)}, u32[]{:S(2)}, u32[]{:S(2)}) collective-permute-start(bf16[16,2048]{1,0:T(8,128)(2,1)S(1)} %slice.57), channel_id=1, source_target_pairs={{0,8},{4,12},{8,14},{12,10},{14,6},{10,2},{6,0},{2,4},{1,9},{5,13}... | collective-permute-start | bytes 196616 | tf_op jit(solution)/shard_map/ppermute | solution.py:307
  19.6 0.0 collective-permute-done.refs_1_
  19.6 0.1 collective-permute-start.5
  19.6 3.5 %stage.3 = (bf16[8,4096,512]{2,1,0:T(8,128)(2,1)S(1)}, bf16[16,128]{1,0:T(8,128)(2,1)S(1)}) custom-call(bf16[4096,4096]{1,0:T(8,128)(2,1)} %refs_3_.1, bf16[8,4096,512]{2,1,0:T(8,128)(2,1)S(1)} %get-tuple-element.25.refs_1_, bf16[16,128]{1,0:T(8,128)(2,1)S(1)} %get-tuple-element.26.refs_2_, ...), custom_call_target="tpu_custom_call", output_to_operand_aliasing={{0}: (1, {})} | custom-call | bytes 8388608 | tf_op jit(solution)/shard_map/stage/pallas_call | solution.py:72
  23.2 0.0 collective-permute-done.7.refs_8_
  23.2 0.5 collective-permute-done.4.refs_4_
  23.6 1.1 %collective-permute-done.5.refs_5_ = bf16[16,2048]{1,0:T(8,128)(2,1)S(1)} collective-permute-done((bf16[16,2048]{1,0:T(8,128)(2,1)S(1)}, bf16[16,2048]{1,0:T(8,128)(2,1)S(1)}, u32[]{:S(2)}, u32[]{:S(2)}) %collective-permute-start.5) | collective-permute-done | bytes 65568 | tf_op jit(solution)/shard_map/ppermute | solution.py:307
  24.7 0.0 collective-permute-done.3.refs_3_
  24.7 0.0 collective-permute-done.6.refs_6_
  24.7 13.0 %gate_up.2 = (bf16[8,4096,512]{2,1,0:T(8,128)(2,1)S(1)}, f32[2,6,128,512]{3,2,1,0:T(8,128)S(1)}, bf16[2,6,128,512]{3,2,1,0:T(8,128)(2,1)S(1)}, bf16[128,4096]{1,0:T(8,128)(2,1)S(1)}) custom-call(bf16[16,4096]{1,0:T(8,128)(2,1)S(1)} %copy-done, bf16[16,4096]{1,0:T(8,128)(2,1)S(1)} %collective-permute-done.refs_1_, ...), custom_call_target="tpu_custom_call", output_to_operand_aliasing={{0}: (10, {})} | custom-call | flops 6442450944 | bytes 50331648 | tf_op jit(solution)/shard_map/gate_up/pallas_call | solution.py:149
  37.7 0.1 collective-permute-start.8
  37.8 5.4 %gate_up.3 = (bf16[8,4096,512]{2,1,0:T(8,128)(2,1)S(1)}, f32[2,2,128,512]{3,2,1,0:T(8,128)S(1)}, bf16[2,2,128,512]{3,2,1,0:T(8,128)(2,1)S(1)}) custom-call(bf16[128,4096]{1,0:T(8,128)(2,1)S(1)} %get-tuple-element.31.refs_0_, f32[64,32]{1,0:T(8,128)S(1)} %constant_dynamic-update-slice_fusion.refs_9_.refs_1_, ...), custom_call_target="tpu_custom_call", output_to_operand_aliasing={{0}: (2, {})} | custom-call | flops 2147483648 | bytes 16777216 | tf_op jit(solution)/shard_map/gate_up/pallas_call | solution.py:149
  43.2 0.6 collective-permute-start.9
  43.8 0.0 collective-permute-done.8.other
  43.8 3.5 %prepare.1 = (bf16[8,4096,512]{2,1,0:T(8,128)(2,1)S(1)}, bf16[128,3072]{1,0:T(8,128)(2,1)S(1)}) custom-call(bf16[4096,4096]{1,0:T(8,128)(2,1)} %dq.3, f32[2,6,128,512]{3,2,1,0:T(8,128)S(1)} %get-tuple-element.29.own, bf16[2,6,128,512]{3,2,1,0:T(8,128)(2,1)S(1)} %collective-permute-done.8.other, ...), custom_call_target="tpu_custom_call", output_to_operand_aliasing={{0}: (3, {})} | custom-call | bytes 8388608 | tf_op jit(solution)/shard_map/prepare/pallas_call | solution.py:188
  47.3 0.0 collective-permute-done.9.other
  47.3 0.0 copy-done.1
  47.3 8.5 %down.1 = (bf16[8,4096,512]{2,1,0:T(8,128)(2,1)S(1)}, f32[8,128,512]{2,1,0:T(8,128)S(1)}) custom-call(bf16[128,3072]{1,0:T(8,128)(2,1)S(1)} %get-tuple-element.35.early, f32[2,2,128,512]{3,2,1,0:T(8,128)S(1)} %get-tuple-element.34.after.own, bf16[2,2,128,512]{3,2,1,0:T(8,128)(2,1)S(1)} %collective-permute-done.9.other, ...), custom_call_target="tpu_custom_call", output_to_operand_aliasing={{0}: (4, {})} | custom-call | flops 4294967296 | bytes 33554432 | tf_op jit(solution)/shard_map/down/pallas_call | solution.py:234
  55.8 0.1 convert.22
  56.0 1.6 %collective-permute-start.15 = (bf16[8,16,512]{2,1,0:T(8,128)(2,1)S(1)}, bf16[8,16,512]{2,1,0:T(8,128)(2,1)S(1)}, u32[]{:S(2)}, u32[]{:S(2)}) collective-permute-start(bf16[8,16,512]{2,1,0:T(8,128)(2,1)S(1)} %get-tuple-element.42), channel_id=1, source_target_pairs={{0,4},{4,8},{8,12},{12,14},{14,10},{10,6},{6,2},{2,0},{1,5},{5,9},... | collective-permute-start | bytes 393224 | tf_op jit(solution)/shard_map/ppermute | solution.py:307
  57.6 0.5 collective-permute-start.12
  58.1 1.6 %collective-permute-start.13 = (bf16[4,16,512]{2,1,0:T(8,128)(2,1)S(1)}, bf16[4,16,512]{2,1,0:T(8,128)(2,1)S(1)}, u32[]{:S(2)}, u32[]{:S(2)}) collective-permute-start(bf16[4,16,512]{2,1,0:T(8,128)(2,1)S(1)} %get-tuple-element.45), channel_id=1, source_target_pairs={{0,6},{4,2},{8,0},{12,4},{14,8},{10,12},{6,14},{2,10},{1,7},{5,3},... | collective-permute-start | bytes 196616 | tf_op jit(solution)/shard_map/ppermute | solution.py:307
  59.7 1.4 %collective-permute-start.16 = (bf16[4,16,512]{2,1,0:T(8,128)(2,1)S(1)}, bf16[4,16,512]{2,1,0:T(8,128)(2,1)S(1)}, u32[]{:S(2)}, u32[]{:S(2)}) collective-permute-start(bf16[4,16,512]{2,1,0:T(8,128)(2,1)S(1)} %get-tuple-element.46), channel_id=1, source_target_pairs={{0,8},{4,12},{8,14},{12,10},{14,6},{10,2},{6,0},{2,4},{1,9},{5,13}... | collective-permute-start | bytes 196616 | tf_op jit(solution)/shard_map/ppermute | solution.py:307
  61.0 0.5 collective-permute-start.10
  61.6 0.0 collective-permute-done.15
  61.6 2.4 %collective-permute-start.11 = (bf16[8,16,512]{2,1,0:T(8,128)(2,1)S(1)}, bf16[8,16,512]{2,1,0:T(8,128)(2,1)S(1)}, u32[]{:S(2)}, u32[]{:S(2)}) collective-permute-start(bf16[8,16,512]{2,1,0:T(8,128)(2,1)S(1)} %get-tuple-element.44), channel_id=1, source_target_pairs={{0,4},{4,8},{8,12},{12,14},{14,10},{10,6},{6,2},{2,0},{1,5},{5,9},... | collective-permute-start | bytes 393224 | tf_op jit(solution)/shard_map/ppermute | solution.py:307
  64.0 0.7 collective-permute-done.12
  64.7 0.1 convert_add_fusion.1
  64.8 1.2 %collective-permute-done.16 = bf16[4,16,512]{2,1,0:T(8,128)(2,1)S(1)} collective-permute-done((bf16[4,16,512]{2,1,0:T(8,128)(2,1)S(1)}, bf16[4,16,512]{2,1,0:T(8,128)(2,1)S(1)}, u32[]{:S(2)}, u32[]{:S(2)}) %collective-permute-start.16) | collective-permute-done | bytes 65568 | tf_op jit(solution)/shard_map/ppermute | solution.py:307
  66.0 1.7 %collective-permute-start.17 = (bf16[8,16,512]{2,1,0:T(8,128)(2,1)S(1)}, bf16[8,16,512]{2,1,0:T(8,128)(2,1)S(1)}, u32[]{:S(2)}, u32[]{:S(2)}) collective-permute-start(bf16[8,16,512]{2,1,0:T(8,128)(2,1)S(1)} %pad_maximum_fusion.1), channel_id=1, source_target_pairs={{0,8},{4,12},{8,14},{12,10},{14,6},{10,2},{6,0},{2,4},{1,9},{5,13}... | collective-permute-start | bytes 393224 | tf_op jit(solution)/shard_map/ppermute | solution.py:307
  67.8 0.0 collective-permute-done.13
  67.8 1.3 %collective-permute-start.14 = (bf16[8,16,512]{2,1,0:T(8,128)(2,1)S(1)}, bf16[8,16,512]{2,1,0:T(8,128)(2,1)S(1)}, u32[]{:S(2)}, u32[]{:S(2)}) collective-permute-start(bf16[8,16,512]{2,1,0:T(8,128)(2,1)S(1)} %pad_maximum_fusion), channel_id=1, source_target_pairs={{0,6},{4,2},{8,0},{12,4},{14,8},{10,12},{6,14},{2,10},{1,7},{5,3},... | collective-permute-start | bytes 393224 | tf_op jit(solution)/shard_map/ppermute | solution.py:307
  69.1 0.0 collective-permute-done.10
  69.1 0.0 collective-permute-done.11
  69.1 4.0 %collective-permute-done.17 = bf16[8,16,512]{2,1,0:T(8,128)(2,1)S(1)} collective-permute-done((bf16[8,16,512]{2,1,0:T(8,128)(2,1)S(1)}, bf16[8,16,512]{2,1,0:T(8,128)(2,1)S(1)}, u32[]{:S(2)}, u32[]{:S(2)}) %collective-permute-start.17) | collective-permute-done | bytes 131104 | tf_op jit(solution)/shard_map/ppermute | solution.py:307
  73.2 1.0 %collective-permute-done.14 = bf16[8,16,512]{2,1,0:T(8,128)(2,1)S(1)} collective-permute-done((bf16[8,16,512]{2,1,0:T(8,128)(2,1)S(1)}, bf16[8,16,512]{2,1,0:T(8,128)(2,1)S(1)}, u32[]{:S(2)}, u32[]{:S(2)}) %collective-permute-start.14) | collective-permute-done | bytes 131104 | tf_op jit(solution)/shard_map/ppermute | solution.py:307
  74.2 0.1 fusion
  74.3 0.7 copy.14
  (18 shorter events, 0.2 us)
Async XLA Ops:
  0.0 16.6 %copy-start.2 = (f32[32,32]{1,0:T(8,128)S(1)}, f32[32,32]{1,0:T(8,128)}, u32[]{:S(2)}) copy-start(f32[32,32]{1,0:T(8,128)} %param.9) | copy-start | bytes 12292
  0.0 19.6 %copy-start.3 = (f32[32,32]{1,0:T(8,128)S(1)}, f32[32,32]{1,0:T(8,128)}, u32[]{:S(2)}) copy-start(f32[32,32]{1,0:T(8,128)} %param.11) | copy-start | bytes 12292
  0.0 14.5 %collective-permute-start.2 = (bf16[16,4096]{1,0:T(8,128)(2,1)}, bf16[16,4096]{1,0:T(8,128)(2,1)S(1)}, u32[]{:S(2)}, u32[]{:S(2)}) collective-permute-start(bf16[16,4096]{1,0:T(8,128)(2,1)} %refs_0_.5), channel_id=1, source_target_pairs={{0,6},{4,2},{8,0},{12,4},{14,8},{10,12},{6,14},{2,10},{1,7},{5,3},... | collective-permute-start | bytes 393224 | tf_op jit(solution)/shard_map/ppermute | solution.py:307
  4.0 10.5 %collective-permute-start.1 = (bf16[16,4096]{1,0:T(8,128)(2,1)}, bf16[16,4096]{1,0:T(8,128)(2,1)S(1)}, u32[]{:S(2)}, u32[]{:S(2)}) collective-permute-start(bf16[16,4096]{1,0:T(8,128)(2,1)} %refs_0_.5), channel_id=1, source_target_pairs={{0,8},{4,12},{8,14},{12,10},{14,6},{10,2},{6,0},{2,4},{1,9},{5,13}... | collective-permute-start | bytes 393224 | tf_op jit(solution)/shard_map/ppermute | solution.py:307
  4.1 15.5 %collective-permute-start = (bf16[16,4096]{1,0:T(8,128)(2,1)}, bf16[16,4096]{1,0:T(8,128)(2,1)S(1)}, u32[]{:S(2)}, u32[]{:S(2)}) collective-permute-start(bf16[16,4096]{1,0:T(8,128)(2,1)} %refs_0_.5), channel_id=1, source_target_pairs={{0,2},{4,0},{8,4},{12,8},{14,12},{10,14},{6,10},{2,6},{1,3},{5,1},... | collective-permute-start | bytes 393224 | tf_op jit(solution)/shard_map/ppermute | solution.py:307
  5.9 17.3 %collective-permute-start.7 = (bf16[16,4096]{1,0:T(8,128)(2,1)}, bf16[16,4096]{1,0:T(8,128)(2,1)S(1)}, u32[]{:S(2)}, u32[]{:S(2)}) collective-permute-start(bf16[16,4096]{1,0:T(8,128)(2,1)} %refs_0_.5), channel_id=1, source_target_pairs={{0,4},{4,8},{8,12},{12,14},{14,10},{10,6},{6,2},{2,0},{1,5},{5,9},... | collective-permute-start | bytes 393224 | tf_op jit(solution)/shard_map/ppermute | solution.py:307
  14.5 10.2 %collective-permute-start.3 = (bf16[16,4096]{1,0:T(8,128)(2,1)S(1)}, bf16[16,4096]{1,0:T(8,128)(2,1)S(1)}, u32[]{:S(2)}, u32[]{:S(2)}) collective-permute-start(bf16[16,4096]{1,0:T(8,128)(2,1)S(1)} %collective-permute-done.2.refs_2_), channel_id=1, source_target_pairs={{0,2},{4,0},{8,4},{12,8},{14,12},{10,14},{6,10},{2,6},{1,3},{5,1},... | collective-permute-start | bytes 393224 | tf_op jit(solution)/shard_map/ppermute | solution.py:307
  16.4 8.4 %collective-permute-start.6 = (bf16[16,4096]{1,0:T(8,128)(2,1)S(1)}, bf16[16,4096]{1,0:T(8,128)(2,1)S(1)}, u32[]{:S(2)}, u32[]{:S(2)}) collective-permute-start(bf16[16,4096]{1,0:T(8,128)(2,1)S(1)} %collective-permute-done.1.refs_3_.refs_7_), channel_id=1, source_target_pairs={{0,4},{4,8},{8,12},{12,14},{14,10},{10,6},{6,2},{2,0},{1,5},{5,9},... | collective-permute-start | bytes 393224 | tf_op jit(solution)/shard_map/ppermute | solution.py:307
  16.6 7.0 %collective-permute-start.4 = (bf16[16,2048]{1,0:T(8,128)(2,1)S(1)}, bf16[16,2048]{1,0:T(8,128)(2,1)S(1)}, u32[]{:S(2)}, u32[]{:S(2)}) collective-permute-start(bf16[16,2048]{1,0:T(8,128)(2,1)S(1)} %slice.57), channel_id=1, source_target_pairs={{0,8},{4,12},{8,14},{12,10},{14,6},{10,2},{6,0},{2,4},{1,9},{5,13}... | collective-permute-start | bytes 196616 | tf_op jit(solution)/shard_map/ppermute | solution.py:307
  19.6 5.2 %collective-permute-start.5 = (bf16[16,2048]{1,0:T(8,128)(2,1)S(1)}, bf16[16,2048]{1,0:T(8,128)(2,1)S(1)}, u32[]{:S(2)}, u32[]{:S(2)}) collective-permute-start(bf16[16,2048]{1,0:T(8,128)(2,1)S(1)} %slice.58), channel_id=1, source_target_pairs={{0,6},{4,2},{8,0},{12,4},{14,8},{10,12},{6,14},{2,10},{1,7},{5,3},... | collective-permute-start | bytes 196616 | tf_op jit(solution)/shard_map/ppermute | solution.py:307
  19.6 5.1 %copy-start = (bf16[16,4096]{1,0:T(8,128)(2,1)S(1)}, bf16[16,4096]{1,0:T(8,128)(2,1)}, u32[]{:S(2)}) copy-start(bf16[16,4096]{1,0:T(8,128)(2,1)} %refs_0_.5) | copy-start | bytes 393220
  37.7 6.0 %collective-permute-start.8 = (bf16[2,6,128,512]{3,2,1,0:T(8,128)(2,1)S(1)}, bf16[2,6,128,512]{3,2,1,0:T(8,128)(2,1)S(1)}, u32[]{:S(2)}, u32[]{:S(2)}) collective-permute-start(bf16[2,6,128,512]{3,2,1,0:T(8,128)(2,1)S(1)} %get-tuple-element.30), channel_id=1, source_target_pairs={{0,1},{1,0},{2,3},{3,2},{4,5},{5,4},{6,7},{7,6},{8,9},{9,8},{10,11... | collective-permute-start | bytes 4718600 | tf_op jit(solution)/shard_map/ppermute | solution.py:330
  43.2 4.1 %collective-permute-start.9 = (bf16[2,2,128,512]{3,2,1,0:T(8,128)(2,1)S(1)}, bf16[2,2,128,512]{3,2,1,0:T(8,128)(2,1)S(1)}, u32[]{:S(2)}, u32[]{:S(2)}) collective-permute-start(bf16[2,2,128,512]{3,2,1,0:T(8,128)(2,1)S(1)} %get-tuple-element.36), channel_id=1, source_target_pairs={{0,1},{1,0},{2,3},{3,2},{4,5},{5,4},{6,7},{7,6},{8,9},{9,8},{10,11... | collective-permute-start | bytes 1572872 | tf_op jit(solution)/shard_map/ppermute | solution.py:330
  43.8 3.5 %copy-start.1 = (f32[32,32]{1,0:T(8,128)S(1)}, f32[32,32]{1,0:T(8,128)}, u32[]{:S(2)}) copy-start(f32[32,32]{1,0:T(8,128)} %scales.1) | copy-start | bytes 12292
  56.0 5.6 %collective-permute-start.15 = (bf16[8,16,512]{2,1,0:T(8,128)(2,1)S(1)}, bf16[8,16,512]{2,1,0:T(8,128)(2,1)S(1)}, u32[]{:S(2)}, u32[]{:S(2)}) collective-permute-start(bf16[8,16,512]{2,1,0:T(8,128)(2,1)S(1)} %get-tuple-element.42), channel_id=1, source_target_pairs={{0,4},{4,8},{8,12},{12,14},{14,10},{10,6},{6,2},{2,0},{1,5},{5,9},... | collective-permute-start | bytes 393224 | tf_op jit(solution)/shard_map/ppermute | solution.py:307
  57.6 7.1 %collective-permute-start.12 = (bf16[8,16,512]{2,1,0:T(8,128)(2,1)S(1)}, bf16[8,16,512]{2,1,0:T(8,128)(2,1)S(1)}, u32[]{:S(2)}, u32[]{:S(2)}) collective-permute-start(bf16[8,16,512]{2,1,0:T(8,128)(2,1)S(1)} %get-tuple-element.43), channel_id=1, source_target_pairs={{0,2},{4,0},{8,4},{12,8},{14,12},{10,14},{6,10},{2,6},{1,3},{5,1},... | collective-permute-start | bytes 393224 | tf_op jit(solution)/shard_map/ppermute | solution.py:307
  58.1 9.7 %collective-permute-start.13 = (bf16[4,16,512]{2,1,0:T(8,128)(2,1)S(1)}, bf16[4,16,512]{2,1,0:T(8,128)(2,1)S(1)}, u32[]{:S(2)}, u32[]{:S(2)}) collective-permute-start(bf16[4,16,512]{2,1,0:T(8,128)(2,1)S(1)} %get-tuple-element.45), channel_id=1, source_target_pairs={{0,6},{4,2},{8,0},{12,4},{14,8},{10,12},{6,14},{2,10},{1,7},{5,3},... | collective-permute-start | bytes 196616 | tf_op jit(solution)/shard_map/ppermute | solution.py:307
  59.7 6.3 %collective-permute-start.16 = (bf16[4,16,512]{2,1,0:T(8,128)(2,1)S(1)}, bf16[4,16,512]{2,1,0:T(8,128)(2,1)S(1)}, u32[]{:S(2)}, u32[]{:S(2)}) collective-permute-start(bf16[4,16,512]{2,1,0:T(8,128)(2,1)S(1)} %get-tuple-element.46), channel_id=1, source_target_pairs={{0,8},{4,12},{8,14},{12,10},{14,6},{10,2},{6,0},{2,4},{1,9},{5,13}... | collective-permute-start | bytes 196616 | tf_op jit(solution)/shard_map/ppermute | solution.py:307
  61.0 8.1 %collective-permute-start.10 = (bf16[8,16,512]{2,1,0:T(8,128)(2,1)S(1)}, bf16[8,16,512]{2,1,0:T(8,128)(2,1)S(1)}, u32[]{:S(2)}, u32[]{:S(2)}) collective-permute-start(bf16[8,16,512]{2,1,0:T(8,128)(2,1)S(1)} %get-tuple-element.41), channel_id=1, source_target_pairs={{0,2},{4,0},{8,4},{12,8},{14,12},{10,14},{6,10},{2,6},{1,3},{5,1},... | collective-permute-start | bytes 393224 | tf_op jit(solution)/shard_map/ppermute | solution.py:307
  61.6 7.6 %collective-permute-start.11 = (bf16[8,16,512]{2,1,0:T(8,128)(2,1)S(1)}, bf16[8,16,512]{2,1,0:T(8,128)(2,1)S(1)}, u32[]{:S(2)}, u32[]{:S(2)}) collective-permute-start(bf16[8,16,512]{2,1,0:T(8,128)(2,1)S(1)} %get-tuple-element.44), channel_id=1, source_target_pairs={{0,4},{4,8},{8,12},{12,14},{14,10},{10,6},{6,2},{2,0},{1,5},{5,9},... | collective-permute-start | bytes 393224 | tf_op jit(solution)/shard_map/ppermute | solution.py:307
  66.0 7.1 %collective-permute-start.17 = (bf16[8,16,512]{2,1,0:T(8,128)(2,1)S(1)}, bf16[8,16,512]{2,1,0:T(8,128)(2,1)S(1)}, u32[]{:S(2)}, u32[]{:S(2)}) collective-permute-start(bf16[8,16,512]{2,1,0:T(8,128)(2,1)S(1)} %pad_maximum_fusion.1), channel_id=1, source_target_pairs={{0,8},{4,12},{8,14},{12,10},{14,6},{10,2},{6,0},{2,4},{1,9},{5,13}... | collective-permute-start | bytes 393224 | tf_op jit(solution)/shard_map/ppermute | solution.py:307
  67.8 6.4 %collective-permute-start.14 = (bf16[8,16,512]{2,1,0:T(8,128)(2,1)S(1)}, bf16[8,16,512]{2,1,0:T(8,128)(2,1)S(1)}, u32[]{:S(2)}, u32[]{:S(2)}) collective-permute-start(bf16[8,16,512]{2,1,0:T(8,128)(2,1)S(1)} %pad_maximum_fusion), channel_id=1, source_target_pairs={{0,6},{4,2},{8,0},{12,4},{14,8},{10,12},{6,14},{2,10},{1,7},{5,3},... | collective-permute-start | bytes 393224 | tf_op jit(solution)/shard_map/ppermute | solution.py:307
